TPU v7x, 32 devices: a whole 2x2x4 slice. The times are simulated.
32 devices in a mesh: groups: 2 (over y), hid: 16 (over z, x, core).
Axes of the slice: x: 2, y: 2, z: 4, core: 2. Of those that a mesh axis runs over, the one named last changes fastest.
Arguments:
- tokens: bfloat16 [4096, 8192], P(('groups', 'hid')), parts along dimension 0, may hold values from -6 to 6
- cotangent: bfloat16 [4096, 8192], P(('groups', 'hid')), parts along dimension 0, may hold values from -5 to 5
- gate_weight: bfloat16 [8192, 2048], P(None, 'hid'), may hold values from -0.0625 to 0.0625
- up_weight: bfloat16 [8192, 2048], P(None, 'hid'), may hold values from -0.0625 to 0.0625
- down_weight: bfloat16 [2048, 8192], P('hid'), may hold values from -0.375 to 0.375
- adapter_input_maps: float32 [16, 16, 2048], P('groups', None, 'hid'), parts along dimension 0, may hold values from -0.375 to 0.375
- adapter_output_maps: float32 [16, 16, 8192], P('groups', None, 'hid'), parts along dimension 0, may hold values from -1.5 to 1.5
- first_moment_input: float32 [16, 16, 2048], P('groups', None, 'hid'), parts along dimension 0, may hold values from -6 to 6
- second_moment_input: float32 [16, 16, 2048], P('groups', None, 'hid'), parts along dimension 0, may hold values from 0.1 to 2
- first_moment_output: float32 [16, 16, 8192], P('groups', None, 'hid'), parts along dimension 0, may hold values from -6 to 6
- second_moment_output: float32 [16, 16, 8192], P('groups', None, 'hid'), parts along dimension 0, may hold values from 0.1 to 2
- active: int32 [32, 2], P('groups'), parts along dimension 0, may hold values from 0 to 15, all different within a row; in each aligned block of 16 rows (0 to 15, 16 to 31, ...) at most 4 rows name the same one
- counts: int32 [32], P('groups'), parts along dimension 0, may hold values from 1 to 2
- dropout_tiles: int32 [4, 128, 128], replicated, may hold values 0 or 1
- seeds: int32 [16], P('groups'), parts along dimension 0, may hold values from 0 to 3
Outputs:
- output: bfloat16 [4096, 8192], P(('groups', 'hid')), parts along dimension 0
- updated_input_maps: float32 [16, 16, 2048], P('groups', None, 'hid'), parts along dimension 0
- new_moment_a: float32 [16, 16, 2048], P('groups', None, 'hid'), parts along dimension 0
- new_second_a: float32 [16, 16, 2048], P('groups', None, 'hid'), parts along dimension 0
- updated_output_maps: float32 [16, 16, 8192], P('groups', None, 'hid'), parts along dimension 0
- new_moment_b: float32 [16, 16, 8192], P('groups', None, 'hid'), parts along dimension 0
- new_second_b: float32 [16, 16, 8192], P('groups', None, 'hid'), parts along dimension 0
There are 2 independent parts, one for each index of `groups`. A program takes and returns all parts, laid end to end along the dimension named above; an argument that names none is the same for every part. Nothing has to cross between parts.
Inputs may be any that keep to these rules, and one draw needn't show every extreme that they name: `active`: each row names 2 different hidden blocks; taking all entries of all rows, no hidden block is named more than 4 times, and some block exactly 4 times. Entries at positions counts[t] or later are padding.
All inputs are finite; a program needn't handle non-finite values.
Results may differ from a plain program's by a relative error of at most 0.0095.
Values may be sent and summed in bfloat16 or wider, within the bound.
No kernel may reach another device: no remote copies, remote signals or barrier semaphores. Data moves between devices by JAX's collectives and lax.ppermute only.
A program may use at most 192 MiB of HBM per device.

v0:
```python
import math

import jax
import jax.numpy as jnp
from jax import lax
from jax.sharding import PartitionSpec as P

adapter_scale = 2.0 / 0.9
highest_precision = lax.Precision.HIGHEST


def adamw_step_update(param, moment, second, grad):
    moment_next = 0.9 * moment + 0.1 * grad
    second_next = 0.999 * second + 0.001 * grad * grad
    corrected = moment_next / (1.0 - 0.9**10)
    spread = jnp.sqrt(second_next / (1.0 - 0.999**10)) + 1e-08
    return (param - 0.01 * (corrected / spread + 0.1 * param), moment_next, second_next)


def body(
    tokens,
    cotangent,
    gate_weight,
    up_weight,
    down_weight,
    adapter_input_maps,
    adapter_output_maps,
    first_moment_input,
    second_moment_input,
    first_moment_output,
    second_moment_output,
    active,
    counts,
    dropout_tiles,
    seeds,
):
    parts = lax.axis_size("hid")
    me = lax.axis_index("hid")
    model = tokens.shape[1]
    block = dropout_tiles.shape[1]
    tiles_n = dropout_tiles.shape[0]
    local_blocks = tokens.shape[0] // block
    all_blocks = local_blocks * parts
    own_hidden = gate_weight.shape[1] // block
    hidden_blocks = own_hidden * parts
    picks = active.shape[1]
    run_indices = adapter_output_maps.shape[0]
    adapter_rank_size = adapter_output_maps.shape[1]
    piece = block // parts
    pair_count = all_blocks * picks
    pair_blk = active.reshape(-1)
    pair_tok = jnp.arange(pair_count, dtype=jnp.int32) // picks
    pair_valid = jnp.arange(pair_count, dtype=jnp.int32) % picks < counts[pair_tok]
    own_ids = me * local_blocks + jnp.arange(local_blocks, dtype=jnp.int32)
    own_runs = own_ids * run_indices // all_blocks
    x_blocks = tokens.reshape(local_blocks, block, model)
    output_gradient_blocks = cotangent.reshape(local_blocks, block, model)
    adapter_in_half = adapter_input_maps.astype(jnp.bfloat16)
    adapter_out_half = adapter_output_maps.astype(jnp.bfloat16)
    b_full = lax.all_gather(adapter_out_half, "hid", axis=2, tiled=True)
    block_owner_term = b_full[own_runs]
    low_rank_gradient = (
        adapter_scale
        * jnp.einsum(
            "jzy,jfy->jzf",
            output_gradient_blocks,
            block_owner_term,
            preferred_element_type=jnp.float32,
        )
    ).astype(jnp.bfloat16)
    gate_w = gate_weight.reshape(model, own_hidden, block)
    up_w = up_weight.reshape(model, own_hidden, block)
    down_t = jnp.transpose(down_weight.reshape(own_hidden, block, model), (2, 0, 1))
    stacked = jnp.concatenate([gate_w, up_w, down_t], axis=2)
    a_rows = adapter_in_half.reshape(run_indices * adapter_rank_size, own_hidden, block)
    spread_w, spread_a = (
        lax.all_to_all(stacked, "hid", split_axis=0, concat_axis=1, tiled=True),
        lax.all_to_all(a_rows, "hid", split_axis=0, concat_axis=1, tiled=True),
    )
    pick = jnp.where(pair_valid, pair_blk, 0)
    send_w = jnp.where(
        pair_valid[None, :, None], jnp.take(spread_w, pick, axis=1), jnp.zeros((), jnp.bfloat16)
    )
    send_a = jnp.where(
        pair_valid[None, :, None], jnp.take(spread_a, pick, axis=1), jnp.zeros((), jnp.bfloat16)
    )
    got_w, got_a = (
        lax.all_to_all(send_w, "hid", split_axis=1, concat_axis=0, tiled=True),
        lax.all_to_all(send_a, "hid", split_axis=1, concat_axis=0, tiled=True),
    )
    four = got_w.reshape(model, local_blocks, picks, 3 * block)
    gate = jnp.einsum(
        "btd,dbku->bktu", x_blocks, four[..., :block], preferred_element_type=jnp.float32
    )
    upper = jnp.einsum(
        "btd,dbku->bktu", x_blocks, four[..., block : 2 * block], preferred_element_type=jnp.float32
    )
    hidden = (jax.nn.silu(gate) * upper).astype(jnp.bfloat16)
    partial_value = jnp.einsum(
        "bktu,dbku->bktd", hidden, four[..., 2 * block :], preferred_element_type=jnp.float32
    ).astype(jnp.bfloat16)
    base_output = jnp.sum(partial_value.astype(jnp.float32), axis=1).astype(jnp.bfloat16)
    my_active = lax.dynamic_slice_in_dim(active, me * local_blocks, local_blocks, 0)
    tile_pick = (seeds[own_runs][:, None] + own_ids[:, None] + 3 * my_active) % tiles_n
    dropped = hidden * dropout_tiles[tile_pick].astype(jnp.bfloat16)
    a_five = got_a.reshape(run_indices, adapter_rank_size, local_blocks, picks, block)
    run_hot = (own_runs[:, None] == jnp.arange(run_indices, dtype=jnp.int32)[None, :]).astype(
        jnp.bfloat16
    )
    a_pair = jnp.einsum(
        "br,rqbku->bkqu", run_hot, a_five, preferred_element_type=jnp.float32
    ).astype(jnp.bfloat16)
    low = jnp.einsum("bktu,bkqu->bktq", dropped, a_pair, preferred_element_type=jnp.float32).astype(
        jnp.bfloat16
    )
    low_rank_block = jnp.sum(low.astype(jnp.float32), axis=1).astype(jnp.bfloat16)
    contrib = jnp.einsum(
        "bti,bktu->bkiu", low_rank_gradient, dropped, preferred_element_type=jnp.float32
    ).reshape(local_blocks * picks, adapter_rank_size, block)
    columns = lax.all_to_all(contrib, "hid", split_axis=2, concat_axis=0, tiled=True)
    target = pick * run_indices + pair_tok * run_indices // all_blocks
    hot = (
        (target[:, None] == jnp.arange(hidden_blocks * run_indices, dtype=jnp.int32)[None, :])
        & pair_valid[:, None]
    ).astype(jnp.float32)
    collected = jnp.einsum("pg,pqu->gqu", hot, columns, precision=highest_precision).reshape(
        hidden_blocks, run_indices, adapter_rank_size, piece
    )
    owned = lax.all_to_all(
        collected.astype(jnp.bfloat16), "hid", split_axis=0, concat_axis=3, tiled=True
    ).astype(collected.dtype)
    input_map_gradient = jnp.transpose(owned, (1, 2, 0, 3)).reshape(
        run_indices, adapter_rank_size, own_hidden * block
    )
    adapter_extra = jnp.einsum(
        "nmy,nyh->nmh", low_rank_block, block_owner_term, preferred_element_type=jnp.float32
    )
    output = (
        (base_output.astype(jnp.float32) + adapter_scale * adapter_extra)
        .astype(jnp.bfloat16)
        .reshape(local_blocks * block, model)
    )
    block_adapter_term = adapter_scale * jnp.einsum(
        "ekh,ekw->ehw", low_rank_block, output_gradient_blocks, preferred_element_type=jnp.float32
    )
    block_onehot = (own_runs[:, None] == jnp.arange(run_indices, dtype=jnp.int32)[None, :]).astype(
        jnp.float32
    )
    complete_term = jnp.einsum(
        "yt,yxo->txo", block_onehot, block_adapter_term, precision=highest_precision
    )
    output_map_gradient = lax.psum_scatter(complete_term, "hid", scatter_dimension=2, tiled=True)
    squares = jnp.sum(input_map_gradient * input_map_gradient, axis=(1, 2)) + jnp.sum(
        output_map_gradient * output_map_gradient, axis=(1, 2)
    )
    totals = lax.psum(squares, "hid")
    limit = math.sqrt(adapter_rank_size * (hidden_blocks * block + model))
    clip_factor = jnp.minimum(1.0, limit / jnp.sqrt(totals))
    updated_input_maps, next_first_input, next_second_input = adamw_step_update(
        adapter_input_maps,
        first_moment_input,
        second_moment_input,
        input_map_gradient * clip_factor[:, None, None],
    )
    updated_output_maps, next_first_output, next_second_output = adamw_step_update(
        adapter_output_maps,
        first_moment_output,
        second_moment_output,
        output_map_gradient * clip_factor[:, None, None],
    )
    return (
        output,
        updated_input_maps,
        next_first_input,
        next_second_input,
        updated_output_maps,
        next_first_output,
        next_second_output,
    )


def solution(mesh):
    return jax.shard_map(
        body,
        mesh=mesh,
        in_specs=(
            P(("groups", "hid"), None),
            P(("groups", "hid"), None),
            P(None, "hid"),
            P(None, "hid"),
            P("hid", None),
            P("groups", None, "hid"),
            P("groups", None, "hid"),
            P("groups", None, "hid"),
            P("groups", None, "hid"),
            P("groups", None, "hid"),
            P("groups", None, "hid"),
            P("groups", None),
            P("groups"),
            P(),
            P("groups"),
        ),
        out_specs=(
            P(("groups", "hid"), None),
            P("groups", None, "hid"),
            P("groups", None, "hid"),
            P("groups", None, "hid"),
            P("groups", None, "hid"),
            P("groups", None, "hid"),
            P("groups", None, "hid"),
        ),
        check_vma=False,
    )
```

profile of v0, /device:TPU:9, one launch (start us, length us, event | category | flops | bytes accessed | tf_op | source)
XLA Modules:
  0.0 683.1 jit_solution(18373441871085367324)
XLA Ops:
  7.2 1.0 convert_element_type.84
  8.2 0.5 broadcast.407
  8.7 0.7 reduce.11
  9.4 0.6 reshape.420
  10.0 6.6 all-to-all-start.2
  16.6 4.1 copy.137
  20.6 6.5 pad_maximum_fusion
  27.1 8.8 %reduce.12 = bf16[8192,384]{1,0:T(8,128)(2,1)} reduce(bf16[8192,1,384]{2,0,1:T(8,128)(2,1)} %pad_maximum_fusion, bf16[]{:T(256)} %broadcast.407), dimensions={1}, to_apply=%copy.138.reduce_sub_computation | reduce | bytes 12582914 | tf_op jit(solution)/shard_map/concatenate | solution.py:74
  36.0 11.6 %reshape.422 = bf16[16,2,98304]{2,1,0:T(2,128)(2,1)} reshape(bf16[8192,384]{1,0:T(8,128)(2,1)} %reduce.12) | data formatting | bytes 12582912
  47.6 6.2 all-to-all-start
  54.0 0.7 gather_fusion
  54.8 0.6 gather_fusion.3
  55.4 0.8 select_bitcast_fusion.1
  56.2 132.8 %all-to-all-done = bf16[16,2,98304]{2,1,0:T(2,128)(2,1)} async-done(((bf16[16,2,98304]{2,1,0:T(2,128)(2,1)}), bf16[16,2,98304]{2,1,0:T(2,128)(2,1)}, u32[]{:S(2)}, u32[]{:S(2)}) %all-to-all-start) | async-done | bytes 6291488 | tf_op jit(solution)/shard_map/all_to_all | solution.py:77
  189.0 7.1 %all-to-all-start.3 = ((bf16[8,32,128]{2,0,1:T(8,128)(2,1)}), bf16[8,32,128]{2,0,1:T(8,128)(2,1)S(1)}, u32[]{:S(2)}, u32[]{:S(2)}) async-start(bf16[8,32,128]{2,0,1:T(8,128)(2,1)} %select_bitcast_fusion.1), calls=%async_computation.3 | async-start | bytes 131072 | tf_op jit(solution)/shard_map/all_to_all | solution.py:89
  196.0 14.3 %reshape.423 = bf16[8192,1,384]{2,1,0:T(2,128)(2,1)} reshape(bf16[16,2,98304]{2,1,0:T(2,128)(2,1)} %all-to-all-done) | data formatting | bytes 12582912
  210.4 8.4 %copy.163 = bf16[8192,1,384]{2,0,1:T(8,128)(2,1)} copy(bf16[8192,1,384]{2,1,0:T(2,128)(2,1)} %reshape.423) | data formatting | bytes 12582912
  218.7 9.7 %gather_fusion.1 = bf16[32,512,384]{2,1,0:T(8,128)(2,1)} fusion(bf16[512,16,384]{2,0,1:T(8,128)(2,1)} %bitcast.175, s32[1024]{0:T(1024)S(1)} %pad_clamp_fusion.1), kind=kCustom, calls=%fused_computation.1 | custom fusion | bytes 25165952 | tf_op jit(solution)/shard_map/jit(_take)/gather | solution.py:82
  228.4 11.1 %select_bitcast_fusion = bf16[512,32,384]{2,0,1:T(8,128)(2,1)} fusion(bf16[32,512,384]{2,1,0:T(8,128)(2,1)} %gather_fusion.1, pred[32]{0:T(512)(128)(4,1)S(1)} %get-tuple-element.64, pred[32]{0:T(512)(128)(4,1)S(1)} %compare_and_fusion), kind=kLoop, calls=%fused_computation.4 | loop fusion | flops 12582912 | bytes 25165888 | tf_op jit(solution)/shard_map/jit(_where)/select_n | solution.py:81
  239.5 6.2 all-to-all-start.1
  245.7 0.7 convert_element_type.89
  246.4 0.2 reduce-scatter.2.cloned.1.call-start
  246.7 0.6 dynamic-slice.5
  248.1 0.6 gather_fusion.2
  249.0 279.3 %all-to-all-done.1 = bf16[512,32,384]{2,0,1:T(8,128)(2,1)} async-done(((bf16[512,32,384]{2,0,1:T(8,128)(2,1)}), bf16[512,32,384]{2,0,1:T(8,128)(2,1)}, u32[]{:S(2)}, u32[]{:S(2)}) %all-to-all-start.1) | async-done | bytes 12582944 | tf_op jit(solution)/shard_map/all_to_all | solution.py:88
  528.3 16.7 %copy.140 = bf16[16,512,2,384]{1,0,3,2:T(8,128)(2,1)} copy(bf16[16,512,2,384]{3,1,2,0:T(8,128)(2,1)} %bitcast.11) | data formatting | bytes 25165824 | tf_op jit(solution)/shard_map/all_to_all | solution.py:88
  545.0 19.6 %reshape.324 = bf16[8192,1,2,384]{0,3,2,1:T(8,128)(2,1)} reshape(bf16[16,512,2,384]{1,0,3,2:T(8,128)(2,1)} %copy.140) | data formatting | bytes 25165824 | tf_op jit(solution)/shard_map/reshape | solution.py:91
  564.6 4.2 fusion.7
  568.8 3.4 fusion.16
  572.4 0.4 convolution_multiply_fusion.1
  572.8 2.4 broadcast_multiply_fusion
  575.3 1.7 convolution_bitcast_fusion
  577.2 0.8 reshape.424
  578.0 7.1 %all-to-all-start.4 = ((f32[16,1,256]{2,1,0:T(1,128)}), f32[16,1,256]{2,1,0:T(1,128)S(1)}, u32[]{:S(2)}, u32[]{:S(2)}) async-start(f32[16,1,256]{2,1,0:T(1,128)} %reshape.424), calls=%async_computation.4 | async-start | bytes 32768 | tf_op jit(solution)/shard_map/all_to_all | solution.py:120
  585.1 5.5 fusion.6
  590.6 0.5 broadcast.409
  591.1 0.7 reduce.13
  592.1 0.4 convolution_convert_fusion.1
  592.7 0.9 reshape.426
  593.6 6.0 all-to-all-start.5
  599.6 3.7 fusion.1
  603.3 1.3 all-to-all-done.5
  604.6 0.2 reshape.427
  605.0 42.5 %reduce-scatter.2.cloned.1.call-done = f32[8,16,512]{2,1,0:T(8,128)} async-done(((f32[8,16,8192]{2,1,0:T(8,128)}), f32[8,16,512]{2,1,0:T(8,128)}) %reduce-scatter.2.cloned.1.call-update) | async-done | bytes 262160 | tf_op jit(solution)/shard_map/reduce_scatter | solution.py:152
  647.5 1.1 multiply_reduce_fusion
  648.8 23.8 %psum.7 = f32[8]{0:T(128)S(1)} all-reduce(f32[8]{0:T(128)S(1)} %add.184), channel_id=1, replica_groups=mesh['groups'=2,'hid'=16] {'hid'}, use_global_device_ids=true, to_apply=%region_5.6 | all-reduce | flops 8 | bytes 64 | tf_op jit(solution)/shard_map/psum | solution.py:156
  672.5 1.6 multiply_subtract_fusion.1
  674.2 2.1 multiply_subtract_fusion
  (57 shorter events, 2.0 us)
Async XLA Ops:
  7.2 565.3 %copy-start = (bf16[128,8192]{1,0:T(8,128)(2,1)S(1)}, bf16[128,8192]{1,0:T(8,128)(2,1)}, u32[]{:S(2)}) copy-start(bf16[128,8192]{1,0:T(8,128)(2,1)} %param.16) | copy-start | bytes 6291460
  10.0 37.6 %all-to-all-start.2 = ((bf16[16,2,512]{2,1,0:T(2,128)(2,1)}), bf16[16,2,512]{2,1,0:T(2,128)(2,1)S(1)}, u32[]{:S(2)}, u32[]{:S(2)}) async-start(bf16[16,2,512]{2,1,0:T(2,128)(2,1)} %reshape.420), calls=%async_computation.2 | async-start | bytes 65536 | tf_op jit(solution)/shard_map/all_to_all | solution.py:78
  47.5 6.2 copy-start.7
  47.6 6.5 copy-start.1
  47.6 141.4 %all-to-all-start = ((bf16[16,2,98304]{2,1,0:T(2,128)(2,1)}), bf16[16,2,98304]{2,1,0:T(2,128)(2,1)}, u32[]{:S(2)}, u32[]{:S(2)}) async-start(bf16[16,2,98304]{2,1,0:T(2,128)(2,1)} %reshape.422), calls=%async_computation | async-start | bytes 12582912 | tf_op jit(solution)/shard_map/all_to_all | solution.py:77
  189.0 50.5 %all-to-all-start.3 = ((bf16[8,32,128]{2,0,1:T(8,128)(2,1)}), bf16[8,32,128]{2,0,1:T(8,128)(2,1)S(1)}, u32[]{:S(2)}, u32[]{:S(2)}) async-start(bf16[8,32,128]{2,0,1:T(8,128)(2,1)} %select_bitcast_fusion.1), calls=%async_computation.3 | async-start | bytes 131072 | tf_op jit(solution)/shard_map/all_to_all | solution.py:89
  239.5 6.2 copy-start.2
  239.5 7.2 %copy-start.9 = (s32[8]{0:T(128)S(1)}, s32[8]{0:T(128)}, u32[]{:S(2)}) copy-start(s32[8]{0:T(128)} %param.29) | copy-start | bytes 100
  239.5 8.6 %copy-start.5 = (s32[4,128,128]{2,1,0:T(8,128)S(1)}, s32[4,128,128]{2,1,0:T(8,128)}, u32[]{:S(2)}) copy-start(s32[4,128,128]{2,1,0:T(8,128)} %param.28) | copy-start | bytes 786436
  239.5 288.8 %all-to-all-start.1 = ((bf16[512,32,384]{2,0,1:T(8,128)(2,1)}), bf16[512,32,384]{2,0,1:T(8,128)(2,1)}, u32[]{:S(2)}, u32[]{:S(2)}) async-start(bf16[512,32,384]{2,0,1:T(8,128)(2,1)} %select_bitcast_fusion), calls=%async_computation.1 | async-start | bytes 25165824 | tf_op jit(solution)/shard_map/all_to_all | solution.py:88
  245.7 329.6 %all-gather.2.cloned.1.call-start = ((), (), s32[]{:S(2)}) async-start(), calls=%async_computation.7 | async-start | bytes 2228224 | tf_op jit(solution)/shard_map/all_gather | solution.py:60
  246.4 401.1 %reduce-scatter.2.cloned.1.call-start = ((), (), s32[]{:S(2)}) async-start(), calls=%async_computation.8 | async-start | bytes 4456448 | tf_op jit(solution)/shard_map/reduce_scatter | solution.py:152
  564.6 4.3 copy-start.8
  578.0 12.6 %all-to-all-start.4 = ((f32[16,1,256]{2,1,0:T(1,128)}), f32[16,1,256]{2,1,0:T(1,128)S(1)}, u32[]{:S(2)}, u32[]{:S(2)}) async-start(f32[16,1,256]{2,1,0:T(1,128)} %reshape.424), calls=%async_computation.4 | async-start | bytes 32768 | tf_op jit(solution)/shard_map/all_to_all | solution.py:120
  592.0 80.5 %copy-start.3 = (f32[8,16,128]{2,1,0:T(8,128)S(1)}, f32[8,16,128]{2,1,0:T(8,128)}, u32[]{:S(2)}) copy-start(f32[8,16,128]{2,1,0:T(8,128)} %param.20) | copy-start | bytes 196612
  592.0 80.5 %copy-start.6 = (f32[8,16,128]{2,1,0:T(8,128)S(1)}, f32[8,16,128]{2,1,0:T(8,128)}, u32[]{:S(2)}) copy-start(f32[8,16,128]{2,1,0:T(8,128)} %param.22) | copy-start | bytes 196612
  592.1 82.0 %copy-start.4 = (f32[8,16,512]{2,1,0:T(8,128)S(1)}, f32[8,16,512]{2,1,0:T(8,128)}, u32[]{:S(2)}) copy-start(f32[8,16,512]{2,1,0:T(8,128)} %param.24) | copy-start | bytes 786436
  593.6 11.0 %all-to-all-start.5 = ((bf16[16,2,512]{2,1,0:T(2,128)(2,1)}), bf16[16,2,512]{2,1,0:T(2,128)(2,1)S(1)}, u32[]{:S(2)}, u32[]{:S(2)}) async-start(bf16[16,2,512]{2,1,0:T(2,128)(2,1)} %reshape.426), calls=%async_computation.5 | async-start | bytes 65536 | tf_op jit(solution)/shard_map/all_to_all | solution.py:129
Sparse Core Ops, SparseCore 0:
  249.2 149.2 all-gather.1
  575.4 72.0 reduce-scatter.1
where the time goes:
time: 696 us; the launch traced here: 683 us
  waiting for transfers between devices  456 us (66%)
  local copies, waits for them, and re-layouts  91.5 us (13%)
  starting transfers between devices  39.3 us (6%)
  other arithmetic  37.9 us (5%)
  blocking collectives  23.8 us (3%)
  matrix products  19.7 us (3%)
  between operations  15 us (2%)
    all_to_all x1, waiting for transfers between devices, body(): lax.all_to_all(send_w, 'hid', split_axis=1, concat_axis=0, tiled=True)  279 us
    all_to_all x1, waiting for transfers between devices, body(): lax.all_to_all(stacked, 'hid', split_axis=0, concat_axis=1, tiled=True)  133 us
    reduce_scatter x1, waiting for transfers between devices, body(): lax.psum_scatter(complete_term, 'hid', scatter_dimension=2, tiled=True)  42.5 us
    unnamed x31, local copies, waits for them, and re-layouts  37.2 us
    psum x1, blocking collectives, body(): totals = lax.psum(squares, 'hid')  23.8 us
    reshape x1, local copies, waits for them, and re-layouts, body(): four = got_w.reshape(model, local_blocks, picks, 3 * block)  19.6 us
    all_to_all x1, local copies, waits for them, and re-layouts, body(): lax.all_to_all(send_w, 'hid', split_axis=1, concat_axis=0, tiled=True)  16.7 us
    concatenate x2, other arithmetic, body(): stacked = jnp.concatenate([gate_w, up_w, down_t], axis=2)  15.4 us
  transfers between devices with their start and end apart: 8, of which 4 were waited for; matrix products, arithmetic and copies ran while one was open for 21% of the time, Pallas kernels for 0%

commit v1 on v0

v1 whole, which is shorter than its diff:
```python
import functools
import math

import jax
import jax.numpy as jnp
from jax import lax
from jax.experimental import pallas as pl
from jax.experimental.pallas import tpu as pltpu
from jax.sharding import Mesh, PartitionSpec as P

adapter_scale = 2.0 / 0.9
bf16 = jnp.bfloat16
f32 = jnp.float32
vmem_limit = 48 * 1024 * 1024


def dot(a, b, dims=((1,), (0,))):
    return lax.dot_general(a, b, (dims, ((), ())), preferred_element_type=f32)


def adamw_step_update(param, moment, second, grad):
    moment_next = 0.9 * moment + 0.1 * grad
    second_next = 0.999 * second + 0.001 * grad * grad
    corrected = moment_next / (1.0 - 0.9**10)
    spread = jnp.sqrt(second_next / (1.0 - 0.999**10)) + 1e-08
    return (param - 0.01 * (corrected / spread + 0.1 * param), moment_next, second_next)


def partial_kernel(tok, active, x_ref, wm_ref, wo_ref, o_ref, *, block, chunk, picks):
    t = tok[pl.program_id(0)]
    x = x_ref[0, :block, :]
    for k in range(picks):
        j = active[t, k]
        o_ref[0, k, :, :block] = dot(x, wm_ref[j, :chunk, :]).astype(o_ref.dtype)
        o_ref[0, k, :, block:] = dot(x, wo_ref[j, :chunk, :]).astype(o_ref.dtype)


def partial_products(tok, active, xb, wm, wo, block, chunk):
    picks = active.shape[1]
    steps = tok.shape[0]
    whole = lambda a: pl.BlockSpec(a.shape, lambda i, *_: (0, 0, 0))
    return pl.pallas_call(
        functools.partial(partial_kernel, block=block, chunk=chunk, picks=picks),
        out_shape=jax.ShapeDtypeStruct((steps, picks, block, 2 * block), bf16),
        grid_spec=pltpu.PrefetchScalarGridSpec(
            num_scalar_prefetch=2,
            grid=(steps,),
            in_specs=[
                pl.BlockSpec((1,) + xb.shape[1:], lambda i, tok, act: (tok[i], 0, 0)),
                whole(wm),
                whole(wo),
            ],
            out_specs=pl.BlockSpec((1, picks, block, 2 * block), lambda i, *_: (i, 0, 0, 0)),
        ),
        compiler_params=pltpu.CompilerParams(vmem_limit_bytes=vmem_limit),
        cost_estimate=pl.CostEstimate(
            flops=steps * picks * 4 * block * block * chunk,
            bytes_accessed=2 * (wm.size + wo.size + xb.size // 2 + steps * picks * 2 * block * block),
            transcendentals=0,
        ),
        name="gate_up_partial",
    )(tok, active, xb, wm, wo)


def hidden_kernel(flags, r_ref, tile_ref, a_ref, dzt_ref, o_ref, *, block, picks, rank):
    total = jnp.sum(r_ref[...].astype(f32), axis=0)
    swap = flags[0] == 1
    low_t = jnp.zeros((rank, block), f32)
    for k in range(picks):
        first, second = total[k, :, :block], total[k, :, block:]
        gate = jnp.where(swap, second, first)
        up = jnp.where(swap, first, second)
        hidden = (gate / (1.0 + jnp.exp(-gate)) * up).astype(bf16)
        hidden = jnp.where(flags[1 + k] == 1, hidden, jnp.zeros_like(hidden))
        dropped = hidden * tile_ref[flags[1 + picks + k]].astype(f32).astype(bf16)
        low_t += dot(a_ref[k], dropped, ((1,), (1,))).astype(bf16).astype(f32)
        o_ref[k * block : (k + 1) * block, :] = hidden
        base = picks * block + rank * (1 + k)
        o_ref[base : base + rank, :] = dot(dzt_ref[...], dropped).astype(bf16)
    o_ref[picks * block : picks * block + rank, :] = low_t.astype(bf16)


def output_kernel(pos, active, h_ref, d_ref, b_ref, o_ref, *, block, picks, rank, per, runs, n):
    for s in range(per):
        t = pl.program_id(0) * per + s
        p = pos[t]
        acc = None
        for k in range(picks):
            j = active[t, k]
            part = dot(h_ref[p, k * block : (k + 1) * block, :], d_ref[j]).astype(bf16).astype(f32)
            acc = part if acc is None else acc + part
        base = acc.astype(bf16).astype(f32)
        z_t = h_ref[p, picks * block : picks * block + rank, :]
        extra = dot(z_t, b_ref[t * runs // n], ((0,), (0,)))
        o_ref[s] = (base + adapter_scale * extra).astype(bf16)


def body(
    tokens,
    cotangent,
    gate_weight,
    up_weight,
    down_weight,
    adapter_input_maps,
    adapter_output_maps,
    first_moment_input,
    second_moment_input,
    first_moment_output,
    second_moment_output,
    active,
    counts,
    dropout_tiles,
    seeds,
):
    hid = ("chip", "core")
    chips, cores = lax.axis_size("chip"), lax.axis_size("core")
    n = chips * cores
    group, core = lax.axis_index("groups"), lax.axis_index("core")
    me = lax.axis_index("chip") * cores + core
    model = tokens.shape[1]
    tiles_n, block = dropout_tiles.shape[0], dropout_tiles.shape[1]
    picks = active.shape[1]
    runs, rank = adapter_output_maps.shape[0], adapter_output_maps.shape[1]
    chunk = model // n
    half = chunk // 2
    blocks = jnp.arange(n, dtype=jnp.int32)
    run_of = blocks * runs // n
    my_run = me * runs // n
    mine = lax.dynamic_index_in_dim(active, me, 0, keepdims=False)
    my_count = lax.dynamic_index_in_dim(counts, me, 0, keepdims=False)
    a_bf = adapter_input_maps.astype(bf16)
    b_bf = adapter_output_maps.astype(bf16)
    per_run = n // runs

    w_rows = jnp.where(group == 0, gate_weight, up_weight).reshape(n, chunk, block)
    w_send = jnp.concatenate([w_rows, jnp.repeat(a_bf, per_run, axis=0)], axis=1)
    wm = lax.all_to_all(w_send, hid, split_axis=0, concat_axis=0, tiled=True)
    other = [(0, 1), (1, 0)]
    wo = lax.ppermute(wm, "groups", other)

    x_rows = jnp.transpose(tokens.reshape(block, n, chunk), (1, 0, 2))
    x_send = jnp.concatenate([x_rows, jnp.repeat(b_bf, per_run, axis=0)], axis=1)
    xb = lax.all_to_all(x_send, hid, split_axis=0, concat_axis=0, tiled=True)

    d_cols = jnp.transpose(down_weight.reshape(block, n, 2, half), (1, 2, 0, 3))
    d_send = lax.dynamic_index_in_dim(d_cols, group, 1, keepdims=False)
    dm = lax.all_to_all(d_send, hid, split_axis=0, concat_axis=0, tiled=True)
    do = lax.ppermute(dm, "groups", other)
    d_all = jnp.where(
        group == 0, jnp.concatenate([dm, do], axis=2), jnp.concatenate([do, dm], axis=2)
    )

    my_b = jnp.transpose(xb[:, block:, :], (1, 0, 2)).reshape(rank, model)
    dz_t = (adapter_scale * dot(my_b, cotangent, ((1,), (1,)))).astype(bf16)
    my_a = wm[mine, chunk:, :]

    evens = jnp.arange(chips, dtype=jnp.int32) * cores
    sent = partial_products(evens + (1 - core), active, xb, wm, wo, block, chunk)
    got = lax.ppermute(sent, "core", other)
    kept = partial_products(evens + core, active, xb, wm, wo, block, chunk)
    paired = (kept.astype(f32) + got.astype(f32)).astype(bf16)
    summed = lax.all_to_all(paired, "chip", split_axis=0, concat_axis=0, tiled=True)

    tile_pick = (seeds[my_run] + me + 3 * mine) % tiles_n
    flags = jnp.concatenate(
        [
            group[None].astype(jnp.int32),
            (jnp.arange(picks) < my_count).astype(jnp.int32),
            tile_pick.astype(jnp.int32),
        ]
    )
    rows = picks * block + rank * (1 + picks)
    vmem = pl.BlockSpec(memory_space=pltpu.VMEM)
    held = pl.pallas_call(
        functools.partial(hidden_kernel, block=block, picks=picks, rank=rank),
        out_shape=jax.ShapeDtypeStruct((rows, block), bf16),
        in_specs=[pl.BlockSpec(memory_space=pltpu.SMEM), vmem, vmem, vmem, vmem],
        out_specs=vmem,
        compiler_params=pltpu.CompilerParams(vmem_limit_bytes=vmem_limit),
        name="hidden_values",
    )(flags, summed, dropout_tiles, my_a, dz_t)

    z_t = held[picks * block : picks * block + rank]
    term_b = adapter_scale * dot(z_t, cotangent)
    term_b = jnp.transpose(term_b.reshape(rank, n, chunk), (1, 0, 2))
    parts_b = lax.all_to_all(term_b, hid, split_axis=0, concat_axis=0, tiled=True)
    grad_b = jnp.sum(parts_b.reshape(runs, per_run, rank, chunk), axis=1)

    gathered = held[None]
    where = blocks[:1]
    mask = chips // 2
    while mask:
        swapped = lax.ppermute(gathered, "chip", [(i, i ^ mask) for i in range(chips)])
        gathered = jnp.concatenate([gathered, swapped], axis=0)
        where = jnp.concatenate([where, where ^ (mask * cores)])
        mask //= 2
    swapped = lax.ppermute(gathered, "core", other)
    gathered = jnp.concatenate([gathered, swapped], axis=0)
    where = jnp.concatenate([where, where ^ 1]) ^ me
    pos = jnp.zeros((n,), jnp.int32).at[where].set(blocks)

    per = 4
    out_chunks = pl.pallas_call(
        functools.partial(
            output_kernel, block=block, picks=picks, rank=rank, per=per, runs=runs, n=n
        ),
        out_shape=jax.ShapeDtypeStruct((n, block, chunk), bf16),
        grid_spec=pltpu.PrefetchScalarGridSpec(
            num_scalar_prefetch=2,
            grid=(n // per,),
            in_specs=[
                pl.BlockSpec(gathered.shape, lambda i, *_: (0, 0, 0)),
                pl.BlockSpec(d_all.shape, lambda i, *_: (0, 0, 0)),
                pl.BlockSpec(b_bf.shape, lambda i, *_: (0, 0, 0)),
            ],
            out_specs=pl.BlockSpec((per, block, chunk), lambda i, *_: (i, 0, 0)),
        ),
        compiler_params=pltpu.CompilerParams(vmem_limit_bytes=vmem_limit),
        name="output_columns",
    )(pos, active, gathered, d_all, b_bf)
    out_cols = lax.all_to_all(out_chunks, hid, split_axis=0, concat_axis=0, tiled=True)
    output = jnp.transpose(out_cols, (1, 0, 2)).reshape(block, model)

    terms_a = gathered[:, picks * block + rank :, :].reshape(n * picks, rank * block)
    run_at = (where * runs // n)[:, None]
    named = (active[where] == me) & (jnp.arange(picks)[None, :] < counts[where][:, None])
    hot = (run_at[None] == jnp.arange(runs)[:, None, None]) & named[None]
    grad_a = dot(hot.reshape(runs, n * picks).astype(bf16), terms_a).reshape(runs, rank, block)

    squares = jnp.sum(grad_a * grad_a, axis=(1, 2)) + jnp.sum(grad_b * grad_b, axis=(1, 2))
    totals = jnp.sum(lax.all_gather(squares, hid, axis=0), axis=0)
    limit = math.sqrt(rank * (n * block + model))
    factor = jnp.minimum(1.0, limit / jnp.sqrt(totals))[:, None, None]
    new_a = adamw_step_update(
        adapter_input_maps, first_moment_input, second_moment_input, grad_a * factor
    )
    new_b = adamw_step_update(
        adapter_output_maps, first_moment_output, second_moment_output, grad_b * factor
    )
    return (output, *new_a, *new_b)


def solution(mesh):
    groups, n = mesh.devices.shape
    fine = Mesh(mesh.devices.reshape(groups, n // 2, 2), ("groups", "chip", "core"))
    hid = ("chip", "core")
    rows = P(("groups",) + hid, None)
    maps = P("groups", None, hid)
    return jax.shard_map(
        body,
        mesh=fine,
        in_specs=(rows, rows, P(None, hid), P(None, hid), P(hid, None))
        + (maps,) * 6
        + (P("groups", None), P("groups"), P(), P("groups")),
        out_specs=(rows,) + (maps,) * 6,
        check_vma=False,
    )
```

time: 696 us -> 319 us (0.46); the launches traced: 683 us -> 315 us
  waiting for transfers between devices: 456 us -> 125 us
  local copies, waits for them, and re-layouts: 91.5 us -> 44.6 us
  blocking collectives: 23.8 us -> 57.7 us
  other arithmetic: 37.9 us -> 17.8 us
  Pallas kernels: 0 us -> 18.5 us
  matrix products: 19.7 us -> 1.35 us
  between operations: 15 us -> 2.36 us
  starting transfers between devices: 39.3 us -> 47.5 us
    all_to_all x6, waiting for transfers between devices: 413 us -> 115 us  [the longest x1 50 us: body(): xb = lax.all_to_all(x_send, hid, split_axis=0, concat_axis=0, tiled=True)]
    unnamed x0 -> x1, blocking collectives: none -> 57.7 us
    reduce_scatter x1 -> x0, waiting for transfers between devices: 42.5 us -> none  [body(): lax.psum_scatter(complete_term, 'hid', scatter_dimension=2, tiled=True)]
    psum x1 -> x0, blocking collectives: 23.8 us -> none  [body(): totals = lax.psum(squares, 'hid')]
    reshape x6 -> x4, local copies, waits for them, and re-layouts: 24.5 us -> 4.91 us  [the longest x1 3.96 us: body(): x_rows = jnp.transpose(tokens.reshape(block, n, chunk), (1, 0, 2))]
    pallas_call x0 -> x4, Pallas kernels: none -> 18.5 us  [the longest x2 14.7 us: partial_products(): pl.pallas_call(functools.partial(partial_kernel, block=block, chunk=chunk...]
    dot_general x9 -> x3, matrix products: 19.7 us -> 1.35 us  [dot(): return lax.dot_general(a, b, (dims, ((), ())), preferred_element_type=f32)]
    all_to_all x6 -> x1, local copies, waits for them, and re-layouts: 17.4 us -> 3.51 us  [body(): wm = lax.all_to_all(w_send, hid, split_axis=0, concat_axis=0, tiled=True)]
  transfers between devices with their start and end apart: 8 -> 13, of which waited for: 4 -> 7; matrix products, arithmetic and copies ran while one was open for 21% -> 15% of each run, Pallas kernels for 0% -> 4%
where the time goes in v1:
time: 319 us; the launch traced here: 315 us
  waiting for transfers between devices  125 us (39%)
  blocking collectives  57.7 us (18%)
  starting transfers between devices  47.5 us (15%)
  local copies, waits for them, and re-layouts  44.6 us (14%)
  Pallas kernels  18.5 us (6%)
  other arithmetic  17.8 us (6%)
    unnamed x1, blocking collectives  57.7 us
    all_to_all x1, waiting for transfers between devices, body(): xb = lax.all_to_all(x_send, hid, split_axis=0, concat_axis=0, tiled=True)  50 us
    all_to_all x1, waiting for transfers between devices, body(): wm = lax.all_to_all(w_send, hid, split_axis=0, concat_axis=0, tiled=True)  36.1 us
    unnamed x44, local copies, waits for them, and re-layouts  24.1 us
    all_to_all x1, waiting for transfers between devices, body(): lax.all_to_all(paired, 'chip', split_axis=0, concat_axis=0, tiled=True)  14.9 us
    pallas_call x2, Pallas kernels, partial_products(): pl.pallas_call(functools.partial(partial_kernel, block=block, chunk=chunk...  14.7 us
    all_to_all x1, waiting for transfers between devices, body(): dm = lax.all_to_all(d_send, hid, split_axis=0, concat_axis=0, tiled=True)  13.7 us
    all_to_all x1, starting transfers between devices, body(): dm = lax.all_to_all(d_send, hid, split_axis=0, concat_axis=0, tiled=True)  7.18 us
  transfers between devices with their start and end apart: 13, of which 7 were waited for; matrix products, arithmetic and copies ran while one was open for 15% of the time, Pallas kernels for 4%

profile of v1, /device:TPU:9, one launch (start us, length us, event | category | flops | bytes accessed | tf_op | source)
XLA Modules:
  0.0 314.6 jit_solution(2085067563509696230)
XLA Ops:
  0.7 1.0 convert_element_type.24
  1.6 1.8 broadcast_select_fusion
  3.5 1.5 pad_maximum_fusion.1
  5.0 6.7 %all-to-all-start.1 = ((bf16[16,528,128]{2,1,0:T(8,128)(2,1)}), bf16[16,528,128]{2,1,0:T(8,128)(2,1)}, u32[]{:S(2)}, u32[]{:S(2)}) async-start(bf16[16,528,128]{2,1,0:T(8,128)(2,1)} %pad_maximum_fusion.1), calls=%async_computation.1 | async-start | bytes 4325376 | tf_op jit(solution)/shard_map/all_to_all | solution.py:137
  11.7 4.1 %copy.57 = bf16[128,8192]{0,1:T(8,128)(2,1)} copy(bf16[128,8192]{1,0:T(8,128)(2,1)} %param.15) | data formatting | bytes 4194304 | tf_op args[0]
  15.8 4.0 %copy.58 = bf16[128,16,512]{2,0,1:T(8,128)(2,1)} copy(bf16[128,16,512]{0,2,1:T(8,128)(2,1)} %bitcast.71) | data formatting | bytes 4194304 | tf_op jit(solution)/shard_map/reshape | solution.py:141
  19.8 3.2 %pad_maximum_fusion = bf16[16,144,512]{2,1,0:T(8,128)(2,1)} fusion(bf16[16,16,512]{2,1,0:T(8,128)(2,1)S(1)} %bitcast.76, bf16[16,128,512]{2,1,0:T(8,128)(2,1)} %bitcast.69), kind=kLoop, calls=%fused_computation.5 | loop fusion | flops 4718592 | bytes 4718592 | tf_op jit(solution)/shard_map/concatenate | solution.py:142
  23.0 36.1 %all-to-all-done.1.wm_ref = bf16[16,528,128]{2,1,0:T(8,128)(2,1)} async-done(((bf16[16,528,128]{2,1,0:T(8,128)(2,1)}), bf16[16,528,128]{2,1,0:T(8,128)(2,1)}, u32[]{:S(2)}, u32[]{:S(2)}) %all-to-all-start.1) | async-done | bytes 2162720 | tf_op jit(solution)/shard_map/all_to_all | solution.py:137
  59.1 6.4 %all-to-all-start = ((bf16[16,144,512]{2,1,0:T(8,128)(2,1)}), bf16[16,144,512]{2,1,0:T(8,128)(2,1)}, u32[]{:S(2)}, u32[]{:S(2)}) async-start(bf16[16,144,512]{2,1,0:T(8,128)(2,1)} %pad_maximum_fusion), calls=%async_computation | async-start | bytes 4718592 | tf_op jit(solution)/shard_map/all_to_all | solution.py:143
  65.5 1.2 collective-permute-start
  66.9 50.0 %all-to-all-done.x_ref = bf16[16,144,512]{2,1,0:T(8,128)(2,1)} async-done(((bf16[16,144,512]{2,1,0:T(8,128)(2,1)}), bf16[16,144,512]{2,1,0:T(8,128)(2,1)}, u32[]{:S(2)}, u32[]{:S(2)}) %all-to-all-start) | async-done | bytes 2359328 | tf_op jit(solution)/shard_map/all_to_all | solution.py:143
  116.9 7.3 %gate_up_partial.3 = bf16[8,2,128,256]{3,2,1,0:T(8,128)(2,1)S(1)} custom-call(s32[8]{0:T(128)S(1)} %fusion.17.tok, s32[16,2]{1,0:T(8,128)S(1)} %copy.66.active, bf16[16,144,512]{2,1,0:T(8,128)(2,1)} %all-to-all-done.x_ref, bf16[16,528,128]{2,1,0:T(8,128)(2,1)} %all-to-all-done.1.wm_ref, bf16[16,528,128]{2,1,0:T(8,128)(2,1)} %collective-permute-done.wo_ref), custom_call_target="tpu_custom_call" | custom-call | flops 536870912 | bytes 6553600 | tf_op jit(solution)/shard_map/gate_up_partial/pallas_call | solution.py:42
  124.8 7.3 %gate_up_partial.2 = bf16[8,2,128,256]{3,2,1,0:T(8,128)(2,1)S(1)} custom-call(s32[8]{0:T(128)S(1)} %fusion.18.tok, s32[16,2]{1,0:T(8,128)S(1)} %copy.66.active, bf16[16,144,512]{2,1,0:T(8,128)(2,1)} %all-to-all-done.x_ref, bf16[16,528,128]{2,1,0:T(8,128)(2,1)} %all-to-all-done.1.wm_ref, bf16[16,528,128]{2,1,0:T(8,128)(2,1)} %collective-permute-done.wo_ref), custom_call_target="tpu_custom_call" | custom-call | flops 536870912 | bytes 6553600 | tf_op jit(solution)/shard_map/gate_up_partial/pallas_call | solution.py:42
  132.2 1.3 add_convert_fusion
  133.5 6.0 %all-to-all-start.2 = ((bf16[8,2,128,256]{3,2,1,0:T(8,128)(2,1)}), bf16[8,2,128,256]{3,2,1,0:T(8,128)(2,1)S(1)}, u32[]{:S(2)}, u32[]{:S(2)}) async-start(bf16[8,2,128,256]{3,2,1,0:T(8,128)(2,1)} %add_convert_fusion), calls=%async_computation.2 | async-start | bytes 2097152 | tf_op jit(solution)/shard_map/all_to_all | solution.py:162
  139.5 4.1 %copy.64 = bf16[128,8192]{0,1:T(8,128)(2,1)} copy(bf16[128,8192]{1,0:T(8,128)(2,1)} %param.19) | data formatting | bytes 4194304 | tf_op args[4]
  143.6 2.3 constant_dynamic-slice_fusion
  145.9 2.3 copy.91
  148.1 14.9 %all-to-all-done.2.r_ref = bf16[8,2,128,256]{3,2,1,0:T(8,128)(2,1)S(1)} async-done(((bf16[8,2,128,256]{3,2,1,0:T(8,128)(2,1)}), bf16[8,2,128,256]{3,2,1,0:T(8,128)(2,1)S(1)}, u32[]{:S(2)}, u32[]{:S(2)}) %all-to-all-start.2) | async-done | bytes 1048608 | tf_op jit(solution)/shard_map/all_to_all | solution.py:162
  163.1 7.2 %all-to-all-start.3 = ((bf16[16,128,256]{2,1,0:T(8,128)(2,1)}), bf16[16,128,256]{2,1,0:T(8,128)(2,1)}, u32[]{:S(2)}, u32[]{:S(2)}) async-start(bf16[16,128,256]{2,1,0:T(8,128)(2,1)} %bitcast.73), calls=%async_computation.3 | async-start | bytes 2097152 | tf_op jit(solution)/shard_map/all_to_all | solution.py:147
  173.3 3.5 %copy.61 = bf16[16,528,128]{2,0,1:T(8,128)(2,1)} copy(bf16[16,528,128]{2,1,0:T(8,128)(2,1)} %all-to-all-done.1.wm_ref) | data formatting | bytes 4325376 | tf_op jit(solution)/shard_map/all_to_all | solution.py:137
  176.8 1.5 gather_fusion
  178.3 1.0 slice_bitcast_fusion
  180.0 0.9 hidden_values.1
  180.9 2.2 collective-permute-start.2
  183.2 13.7 %all-to-all-done.3 = bf16[16,128,256]{2,1,0:T(8,128)(2,1)} async-done(((bf16[16,128,256]{2,1,0:T(8,128)(2,1)}), bf16[16,128,256]{2,1,0:T(8,128)(2,1)}, u32[]{:S(2)}, u32[]{:S(2)}) %all-to-all-start.3) | async-done | bytes 1048608 | tf_op jit(solution)/shard_map/all_to_all | solution.py:147
  196.9 1.2 collective-permute-start.6
  198.1 1.4 collective-permute-start.3
  199.9 3.6 %collective-permute-done.3 = bf16[2,304,128]{2,1,0:T(8,128)(2,1)S(1)} collective-permute-done((bf16[2,304,128]{2,1,0:T(8,128)(2,1)S(1)}, bf16[2,304,128]{2,1,0:T(8,128)(2,1)S(1)}, u32[]{:S(2)}, u32[]{:S(2)}) %collective-permute-start.3) | collective-permute-done | bytes 155680 | tf_op jit(solution)/shard_map/ppermute | solution.py:193
  204.2 2.2 collective-permute-start.4
  207.4 0.9 copy.128
  208.3 5.1 %all-to-all-start.5 = ((f32[16,16,512]{2,1,0:T(8,128)}), f32[16,16,512]{2,1,0:T(8,128)S(1)}, u32[]{:S(2)}, u32[]{:S(2)}) async-start(f32[16,16,512]{2,1,0:T(8,128)} %bitcast.75), calls=%async_computation.5 | async-start | bytes 1048576 | tf_op jit(solution)/shard_map/all_to_all | solution.py:186
  213.7 1.0 pad_maximum_fusion.2
  214.7 1.4 collective-permute-start.5
  216.1 6.1 %collective-permute-done.6 = bf16[16,128,256]{2,1,0:T(8,128)(2,1)} collective-permute-done((bf16[16,128,256]{2,1,0:T(8,128)(2,1)}, bf16[16,128,256]{2,1,0:T(8,128)(2,1)}, u32[]{:S(2)}, u32[]{:S(2)}) %collective-permute-start.6) | collective-permute-done | bytes 1048608 | tf_op jit(solution)/shard_map/ppermute | solution.py:148
  222.2 2.9 maximum_select_fusion.d_ref
  225.2 1.0 constant_dynamic-update-slice_fusion.1
  226.3 3.0 output_columns.1
  229.3 1.3 copy-done.1
  230.6 1.0 copy-done.2
  231.7 5.9 %all-to-all-start.4 = ((bf16[16,128,512]{2,1,0:T(8,128)(2,1)}), bf16[16,128,512]{2,1,0:T(8,128)(2,1)}, u32[]{:S(2)}, u32[]{:S(2)}) async-start(bf16[16,128,512]{2,1,0:T(8,128)(2,1)} %copy-done.1), calls=%async_computation.4 | async-start | bytes 4194304 | tf_op jit(solution)/shard_map/all_to_all | solution.py:221
  240.8 0.9 slice.41
  242.2 57.7 %all-reduce.1 = f32[128]{0:T(128)S(1)} all-reduce(f32[128]{0:T(128)S(1)} %add_dynamic-update-slice_fusion), channel_id=2, replica_groups=mesh['groups'=2,'chip'=8,'core'=2] {'chip','core'}, use_global_device_ids=true, to_apply=%add.1 | all-reduce | flops 128 | bytes 1024
  302.1 1.9 multiply_subtract_fusion
  304.0 0.9 copy.85
  304.9 0.9 copy.86
  306.6 3.9 %copy.67 = bf16[128,16,512]{0,2,1:T(8,128)(2,1)} copy(bf16[128,16,512]{2,0,1:T(8,128)(2,1)} %bitcast.20) | data formatting | bytes 4194304 | tf_op jit(solution)/shard_map/transpose | solution.py:222
  310.5 4.1 %copy.81 = bf16[128,8192]{1,0:T(8,128)(2,1)} copy(bf16[128,8192]{0,1:T(8,128)(2,1)} %bitcast.70) | data formatting | bytes 4194304
  (89 shorter events, 12.4 us)
Async XLA Ops:
  0.6 178.7 %copy-start = (bf16[128,8192]{1,0:T(8,128)(2,1)S(1)}, bf16[128,8192]{1,0:T(8,128)(2,1)}, u32[]{:S(2)}) copy-start(bf16[128,8192]{1,0:T(8,128)(2,1)} %param.16) | copy-start | bytes 6291460
  5.0 6.7 %copy-start.5 = (f32[8,16,512]{2,1,0:T(8,128)S(1)}, f32[8,16,512]{2,1,0:T(8,128)}, u32[]{:S(2)}) copy-start(f32[8,16,512]{2,1,0:T(8,128)} %param.21) | copy-start | bytes 786436
  5.0 54.1 %all-to-all-start.1 = ((bf16[16,528,128]{2,1,0:T(8,128)(2,1)}), bf16[16,528,128]{2,1,0:T(8,128)(2,1)}, u32[]{:S(2)}, u32[]{:S(2)}) async-start(bf16[16,528,128]{2,1,0:T(8,128)(2,1)} %pad_maximum_fusion.1), calls=%async_computation.1 | async-start | bytes 4325376 | tf_op jit(solution)/shard_map/all_to_all | solution.py:137
  23.0 43.8 %copy-start.10 = (s32[16,2]{0,1:T(2,128)S(1)}, s32[16,2]{0,1:T(2,128)}, u32[]{:S(2)}) copy-start(s32[16,2]{0,1:T(2,128)} %param.26) | copy-start | bytes 388
  59.1 57.8 %all-to-all-start = ((bf16[16,144,512]{2,1,0:T(8,128)(2,1)}), bf16[16,144,512]{2,1,0:T(8,128)(2,1)}, u32[]{:S(2)}, u32[]{:S(2)}) async-start(bf16[16,144,512]{2,1,0:T(8,128)(2,1)} %pad_maximum_fusion), calls=%async_computation | async-start | bytes 4718592 | tf_op jit(solution)/shard_map/all_to_all | solution.py:143
  65.5 51.4 %collective-permute-start = (bf16[16,528,128]{2,1,0:T(8,128)(2,1)}, bf16[16,528,128]{2,1,0:T(8,128)(2,1)}, u32[]{:S(2)}, u32[]{:S(2)}) collective-permute-start(bf16[16,528,128]{2,1,0:T(8,128)(2,1)} %all-to-all-done.1.wm_ref), channel_id=1, source_target_pairs={{0,16},{16,0},{1,17},{17,1},{2,18},{18,2},{3,19},{19,3},{4,20},{20... | collective-permute-start | bytes 6488072 | tf_op jit(solution)/shard_map/ppermute | solution.py:139
  124.3 7.9 %collective-permute-start.1 = (bf16[8,2,128,256]{3,2,1,0:T(8,128)(2,1)S(1)}, bf16[8,2,128,256]{3,2,1,0:T(8,128)(2,1)S(1)}, u32[]{:S(2)}, u32[]{:S(2)}) collective-permute-start(bf16[8,2,128,256]{3,2,1,0:T(8,128)(2,1)S(1)} %gate_up_partial.3), channel_id=1, source_target_pairs={{0,1},{1,0},{2,3},{3,2},{4,5},{5,4},{6,7},{7,6},{8,9},{9,8},{10,11... | collective-permute-start | bytes 3145736 | tf_op jit(solution)/shard_map/ppermute | solution.py:159
  133.5 29.5 %all-to-all-start.2 = ((bf16[8,2,128,256]{3,2,1,0:T(8,128)(2,1)}), bf16[8,2,128,256]{3,2,1,0:T(8,128)(2,1)S(1)}, u32[]{:S(2)}, u32[]{:S(2)}) async-start(bf16[8,2,128,256]{3,2,1,0:T(8,128)(2,1)} %add_convert_fusion), calls=%async_computation.2 | async-start | bytes 2097152 | tf_op jit(solution)/shard_map/all_to_all | solution.py:162
  145.9 24.4 %copy-start.11 = (s32[8]{0:T(128)S(1)}, s32[8]{0:T(128)}, u32[]{:S(2)}) copy-start(s32[8]{0:T(128)} %param.29) | copy-start | bytes 100
  145.9 25.7 %copy-start.4 = (s32[16]{0:T(128)S(1)}, s32[16]{0:T(128)}, u32[]{:S(2)}) copy-start(s32[16]{0:T(128)} %param.27) | copy-start | bytes 196
  163.1 33.8 %all-to-all-start.3 = ((bf16[16,128,256]{2,1,0:T(8,128)(2,1)}), bf16[16,128,256]{2,1,0:T(8,128)(2,1)}, u32[]{:S(2)}, u32[]{:S(2)}) async-start(bf16[16,128,256]{2,1,0:T(8,128)(2,1)} %bitcast.73), calls=%async_computation.3 | async-start | bytes 2097152 | tf_op jit(solution)/shard_map/all_to_all | solution.py:147
  178.3 1.7 copy-start.3
  180.9 17.2 %collective-permute-start.2 = (bf16[1,304,128]{2,1,0:T(8,128)(2,1)S(1)}, bf16[1,304,128]{2,1,0:T(8,128)(2,1)S(1)}, u32[]{:S(2)}, u32[]{:S(2)}) collective-permute-start(bf16[1,304,128]{2,1,0:T(8,128)(2,1)S(1)} %bitcast.64), channel_id=1, source_target_pairs={{0,8},{2,10},{4,12},{6,14},{8,0},{10,2},{12,4},{14,6},{1,9},{3,11}... | collective-permute-start | bytes 233480 | tf_op jit(solution)/shard_map/ppermute | solution.py:193
  196.9 25.3 %collective-permute-start.6 = (bf16[16,128,256]{2,1,0:T(8,128)(2,1)}, bf16[16,128,256]{2,1,0:T(8,128)(2,1)}, u32[]{:S(2)}, u32[]{:S(2)}) collective-permute-start(bf16[16,128,256]{2,1,0:T(8,128)(2,1)} %all-to-all-done.3), channel_id=1, source_target_pairs={{0,16},{16,0},{1,17},{17,1},{2,18},{18,2},{3,19},{19,3},{4,20},{20... | collective-permute-start | bytes 3145736 | tf_op jit(solution)/shard_map/ppermute | solution.py:148
  198.1 5.3 %collective-permute-start.3 = (bf16[2,304,128]{2,1,0:T(8,128)(2,1)S(1)}, bf16[2,304,128]{2,1,0:T(8,128)(2,1)S(1)}, u32[]{:S(2)}, u32[]{:S(2)}) collective-permute-start(bf16[2,304,128]{2,1,0:T(8,128)(2,1)S(1)} %pad_maximum_fusion.4), channel_id=1, source_target_pairs={{0,4},{2,6},{4,0},{6,2},{8,12},{10,14},{12,8},{14,10},{1,5},{3,7},... | collective-permute-start | bytes 466952 | tf_op jit(solution)/shard_map/ppermute | solution.py:193
  204.2 9.5 %collective-permute-start.4 = (bf16[4,304,128]{2,1,0:T(8,128)(2,1)}, bf16[4,304,128]{2,1,0:T(8,128)(2,1)}, u32[]{:S(2)}, u32[]{:S(2)}) collective-permute-start(bf16[4,304,128]{2,1,0:T(8,128)(2,1)} %pad_maximum_fusion.3), channel_id=1, source_target_pairs={{0,2},{2,0},{4,6},{6,4},{8,10},{10,8},{12,14},{14,12},{1,3},{3,1},... | collective-permute-start | bytes 933896 | tf_op jit(solution)/shard_map/ppermute | solution.py:193
  208.3 23.4 %all-to-all-start.5 = ((f32[16,16,512]{2,1,0:T(8,128)}), f32[16,16,512]{2,1,0:T(8,128)S(1)}, u32[]{:S(2)}, u32[]{:S(2)}) async-start(f32[16,16,512]{2,1,0:T(8,128)} %bitcast.75), calls=%async_computation.5 | async-start | bytes 1048576 | tf_op jit(solution)/shard_map/all_to_all | solution.py:186
  214.7 11.5 %collective-permute-start.5 = (bf16[8,304,128]{2,1,0:T(8,128)(2,1)S(1)}, bf16[8,304,128]{2,1,0:T(8,128)(2,1)S(1)}, u32[]{:S(2)}, u32[]{:S(2)}) collective-permute-start(bf16[8,304,128]{2,1,0:T(8,128)(2,1)S(1)} %pad_maximum_fusion.2), channel_id=1, source_target_pairs={{0,1},{1,0},{2,3},{3,2},{4,5},{5,4},{6,7},{7,6},{8,9},{9,8},{10,11... | collective-permute-start | bytes 1867784 | tf_op jit(solution)/shard_map/ppermute | solution.py:197
  229.3 1.3 copy-start.1
  230.6 1.0 copy-start.2
  231.7 7.6 %copy-start.12 = (u32[32]{0:T(128)S(1)}, u32[32]{0:T(128)}, u32[]{:S(2)}) copy-start(u32[32]{0:T(128)} %constant.139) | copy-start | bytes 388
  231.7 75.0 %all-to-all-start.4 = ((bf16[16,128,512]{2,1,0:T(8,128)(2,1)}), bf16[16,128,512]{2,1,0:T(8,128)(2,1)}, u32[]{:S(2)}, u32[]{:S(2)}) async-start(bf16[16,128,512]{2,1,0:T(8,128)(2,1)} %copy-done.1), calls=%async_computation.4 | async-start | bytes 4194304 | tf_op jit(solution)/shard_map/all_to_all | solution.py:221
  237.6 62.5 %copy-start.7 = (f32[8,16,128]{2,1,0:T(8,128)S(1)}, f32[8,16,128]{2,1,0:T(8,128)}, u32[]{:S(2)}) copy-start(f32[8,16,128]{2,1,0:T(8,128)} %param.20) | copy-start | bytes 196612
  237.6 62.5 %copy-start.8 = (f32[8,16,128]{2,1,0:T(8,128)S(1)}, f32[8,16,128]{2,1,0:T(8,128)}, u32[]{:S(2)}) copy-start(f32[8,16,128]{2,1,0:T(8,128)} %param.22) | copy-start | bytes 196612
  237.6 62.5 %copy-start.9 = (f32[8,16,128]{2,1,0:T(8,128)S(1)}, f32[8,16,128]{2,1,0:T(8,128)}, u32[]{:S(2)}) copy-start(f32[8,16,128]{2,1,0:T(8,128)} %param.23) | copy-start | bytes 196612
  237.6 64.5 %copy-start.6 = (f32[8,16,512]{2,1,0:T(8,128)S(1)}, f32[8,16,512]{2,1,0:T(8,128)}, u32[]{:S(2)}) copy-start(f32[8,16,512]{2,1,0:T(8,128)} %param.21) | copy-start | bytes 786436

commit v2 on v1

v2 whole, which is shorter than its diff:
```python
import functools
import math

import jax
import jax.numpy as jnp
from jax import lax
from jax.experimental import pallas as pl
from jax.experimental.pallas import tpu as pltpu
from jax.sharding import Mesh, PartitionSpec as P

adapter_scale = 2.0 / 0.9
bf16 = jnp.bfloat16
f32 = jnp.float32
vmem_limit = 48 * 1024 * 1024
vmem_full = 62 * 1024 * 1024
strips = 8
paired_step = 4


def dot(a, b, dims=((1,), (0,))):
    return lax.dot_general(a, b, (dims, ((), ())), preferred_element_type=f32)


def call(kernel, name, out, grid, in_specs, out_specs, scalars, arrays, flops=0):
    outs = out if isinstance(out, (tuple, list)) else [out]
    moved = sum(a.size * a.dtype.itemsize for a in (*arrays, *outs))
    return pl.pallas_call(
        kernel,
        out_shape=out,
        grid_spec=pltpu.PrefetchScalarGridSpec(
            num_scalar_prefetch=len(scalars),
            grid=grid,
            in_specs=in_specs,
            out_specs=out_specs,
        ),
        compiler_params=pltpu.CompilerParams(vmem_limit_bytes=vmem_limit),
        cost_estimate=pl.CostEstimate(flops=flops, bytes_accessed=moved, transcendentals=0),
        name=name,
    )(*scalars, *arrays)


def whole(a):
    zeros = (0,) * len(a.shape)
    return pl.BlockSpec(a.shape, lambda i, *_: zeros)


def weight_rows_kernel(gate_ref, up_ref, a_ref, o_ref, held, loads, stores, *, chunk, n, runs):
    group = lax.axis_index("groups")

    def copies(w_ref):
        return [
            pltpu.make_async_copy(
                w_ref.at[pl.ds(s * chunk, chunk)], held.at[s, pl.ds(0, chunk)], loads.at[s]
            )
            for s in range(n)
        ]

    @pl.when(group == 0)
    def _():
        for copy in copies(gate_ref):
            copy.start()

    @pl.when(group != 0)
    def _():
        for copy in copies(up_ref):
            copy.start()

    for s in range(n):
        held[s, chunk:, :] = a_ref[s * runs // n].astype(bf16)
    out = [pltpu.make_async_copy(held.at[s], o_ref.at[s], stores.at[s]) for s in range(n)]
    for s, copy in enumerate(copies(gate_ref)):
        copy.wait()
        out[s].start()
    for copy in out:
        copy.wait()


def token_columns_kernel(ids, x_ref, b_ref, o_ref, *, block, chunk, n, runs):
    per = n // strips
    for s in range(per):
        o_ref[s, :block, :] = x_ref[:, s * chunk : (s + 1) * chunk]
        run = (pl.program_id(0) * per + s) * runs // n
        o_ref[s, block:, :] = b_ref[run].astype(bf16)


def down_columns_kernel(ids, d_ref, o_ref, *, chunk, n):
    half = chunk // 2
    for s in range(n // strips):
        base = s * chunk

        @pl.when(ids[0] == 0)
        def _():
            o_ref[s] = d_ref[:, base : base + half]

        @pl.when(ids[0] != 0)
        def _():
            o_ref[s] = d_ref[:, base + half : base + chunk]


def partial_kernel(ids, active, x_ref, wm_ref, wo_ref, o_ref, *, block, chunk, picks, away):
    side = jnp.bitwise_xor(ids[1], away)
    for s in range(paired_step):
        x = x_ref[s, 0, :block, :]
        for k in range(picks):
            j = active[2 * (paired_step * pl.program_id(0) + s) + side, k]
            w = jnp.concatenate([wm_ref[j, :chunk, :], wo_ref[j, :chunk, :]], axis=1)
            o_ref[s, k] = dot(x, w).astype(o_ref.dtype)


def partial_products(ids, active, xb, wm, wo, block, chunk, away):
    n, picks = active.shape
    shape = (n // 2, picks, block, 2 * block)
    token = lambda i, ids, act: (i, jnp.bitwise_xor(ids[1], away), 0, 0)
    xp = xb.reshape(n // 2, 2, *xb.shape[1:])
    return call(
        functools.partial(partial_kernel, block=block, chunk=chunk, picks=picks, away=away),
        "gate_up_partial",
        jax.ShapeDtypeStruct(shape, bf16),
        (n // 2 // paired_step,),
        [pl.BlockSpec((paired_step, 1) + xb.shape[1:], token), whole(wm), whole(wo)],
        pl.BlockSpec((paired_step,) + shape[1:], lambda i, *_: (i, 0, 0, 0)),
        (ids, active),
        (xp, wm, wo),
        flops=n * picks * 2 * block * block * chunk,
    )


def side_rows_kernel(ids, active, counts, seeds, *refs, block, chunk, picks, rank, n):
    b_ref, dy_ref = refs[:2]
    tile_refs, a_refs, o_ref = refs[2 : 2 + picks], refs[2 + picks : -1], refs[-1]
    total = None
    for e in range(n):
        part = dot(b_ref[e], dy_ref[:, e * chunk : (e + 1) * chunk], ((1,), (1,)))
        total = part if total is None else total + part
    for k in range(picks):
        o_ref[k * block : (k + 1) * block, :] = tile_refs[k][0].astype(f32).astype(bf16)
        base = picks * block + rank * (1 + k)
        o_ref[base : base + rank, :] = a_refs[k][0]
    base = picks * block
    o_ref[base : base + rank, :] = (adapter_scale * total).astype(bf16)


def hidden_kernel(ids, counts, r_ref, side_ref, o_ref, *, block, picks, rank):
    total = jnp.sum(r_ref[...].astype(f32), axis=0)
    swap = ids[0] != 0
    count = counts[ids[2]]
    low_t = jnp.zeros((rank, block), f32)
    own = slice(picks * block, picks * block + rank)
    for k in range(picks):
        first, second = total[k, :, :block], total[k, :, block:]
        gate = jnp.where(swap, second, first)
        up = jnp.where(swap, first, second)
        hidden = (gate / (1.0 + jnp.exp(-gate)) * up).astype(bf16)
        hidden = jnp.where(k < count, hidden, jnp.zeros_like(hidden))
        rows = slice(k * block, (k + 1) * block)
        pair = slice(picks * block + rank * (1 + k), picks * block + rank * (2 + k))
        dropped = hidden * side_ref[rows, :]
        low_t += dot(side_ref[pair, :], dropped, ((1,), (1,))).astype(bf16).astype(f32)
        o_ref[rows, :] = hidden
        o_ref[pair, :] = dot(side_ref[own, :], dropped).astype(bf16)
    o_ref[own, :] = low_t.astype(bf16)


def output_terms_kernel(ids, z_ref, dy_ref, o_ref, *, chunk, n):
    for s in range(n // strips):
        part = dot(z_ref[...], dy_ref[:, s * chunk : (s + 1) * chunk])
        o_ref[s] = (adapter_scale * part).astype(bf16)


def output_kernel(
    ids, active, slot, h_ref, dm_ref, do_ref, b_ref, o_ref, *, block, picks, rank, per, runs, n
):
    half = dm_ref.shape[2]
    swap = ids[0] != 0
    for s in range(per):
        t = pl.program_id(0) * per + s
        p = slot[jnp.bitwise_xor(t, ids[2])]
        sums = [None, None]
        for k in range(picks):
            j = active[t, k]
            h = h_ref[p, k * block : (k + 1) * block, :]
            for side, d_ref in enumerate((dm_ref, do_ref)):
                part = dot(h, d_ref[j]).astype(bf16).astype(f32)
                sums[side] = part if k == 0 else sums[side] + part
        left = jnp.where(swap, sums[1], sums[0]).astype(bf16).astype(f32)
        right = jnp.where(swap, sums[0], sums[1]).astype(bf16).astype(f32)
        z_t = h_ref[p, picks * block : picks * block + rank, :]
        extra = adapter_scale * dot(z_t, b_ref[t * runs // n].astype(bf16), ((0,), (0,)))
        o_ref[s, :, :half] = (left + extra[:, :half]).astype(bf16)
        o_ref[s, :, half:] = (right + extra[:, half:]).astype(bf16)


def join_columns_kernel(ids, c_ref, o_ref, *, chunk, n):
    for s in range(n // strips):
        o_ref[:, s * chunk : (s + 1) * chunk] = c_ref[s]


def join_copies_kernel(c_ref, o_ref, held, loads, stores, *, chunk, n):
    into = [pltpu.make_async_copy(c_ref.at[s], held.at[s], loads.at[s]) for s in range(n)]
    out = [
        pltpu.make_async_copy(held.at[s], o_ref.at[:, pl.ds(s * chunk, chunk)], stores.at[s])
        for s in range(n)
    ]
    for copy in into:
        copy.start()
    for first, second in zip(into, out):
        first.wait()
        second.start()
    for copy in out:
        copy.wait()


def gradients_kernel(ids, active, counts, order, *refs, picks, runs, n):
    term_refs, part_ref, ga_ref, gb_ref, sq_ref = refs[:picks], *refs[picks:]
    me = ids[2]
    per_run = n // runs
    ga_ref[...] = jnp.zeros_like(ga_ref)

    def add(s, carry):
        t = jnp.bitwise_xor(order[s], me)
        for k in range(picks):

            @pl.when((active[t, k] == me) & (k < counts[t]))
            def _():
                run = t * runs // n
                ga_ref[run] = ga_ref[run] + term_refs[k][s].astype(f32)

        return carry

    lax.fori_loop(0, n, add, 0)
    for r in range(runs):
        total = part_ref[r * per_run].astype(f32)
        for q in range(1, per_run):
            total = total + part_ref[r * per_run + q].astype(f32)
        gb_ref[r] = total
        square = jnp.sum(ga_ref[r] * ga_ref[r]) + jnp.sum(total * total)
        sq_ref[r : r + 1, :] = jnp.full((1, sq_ref.shape[1]), square, f32)


def adamw_kernel(ids, sq_ref, *refs, limit, runs):
    ins, outs = refs[:8], refs[8:]
    for r in range(runs):
        factor = jnp.minimum(1.0, limit / jnp.sqrt(sq_ref[r : r + 1, :1]))
        for side in range(2):
            p_ref, m_ref, v_ref, g_ref = ins[4 * side : 4 * side + 4]
            grad = g_ref[r] * factor
            param = p_ref[r]
            moment = 0.9 * m_ref[r] + 0.1 * grad
            second = 0.999 * v_ref[r] + 0.001 * grad * grad
            corrected = moment / (1.0 - 0.9**10)
            spread = jnp.sqrt(second / (1.0 - 0.999**10)) + 1e-08
            outs[3 * side][r] = param - 0.01 * (corrected / spread + 0.1 * param)
            outs[3 * side + 1][r] = moment
            outs[3 * side + 2][r] = second


def body(
    tokens,
    cotangent,
    gate_weight,
    up_weight,
    down_weight,
    adapter_input_maps,
    adapter_output_maps,
    first_moment_input,
    second_moment_input,
    first_moment_output,
    second_moment_output,
    active,
    counts,
    dropout_tiles,
    seeds,
):
    hid = ("chip", "core")
    chips, cores = lax.axis_size("chip"), lax.axis_size("core")
    n = chips * cores
    core = lax.axis_index("core")
    me = lax.axis_index("chip") * cores + core
    ids = jnp.stack([lax.axis_index("groups"), core, me]).astype(jnp.int32)
    model = tokens.shape[1]
    tiles_n, block = dropout_tiles.shape[0], dropout_tiles.shape[1]
    picks = active.shape[1]
    runs, rank = adapter_output_maps.shape[0], adapter_output_maps.shape[1]
    chunk = model // n
    half = chunk // 2
    per = n // strips
    strip = model // strips
    other = [(0, 1), (1, 0)]
    across = lambda m: [(i, i ^ m) for i in range(chips)]
    sizes = dict(chunk=chunk, n=n)

    anywhere = pl.BlockSpec(memory_space=pl.ANY)
    w_send = pl.pallas_call(
        functools.partial(weight_rows_kernel, runs=runs, **sizes),
        out_shape=jax.ShapeDtypeStruct((n, chunk + rank, block), bf16),
        in_specs=[anywhere, anywhere, pl.BlockSpec(memory_space=pltpu.VMEM)],
        out_specs=anywhere,
        scratch_shapes=[
            pltpu.VMEM((n, chunk + rank, block), bf16),
            pltpu.SemaphoreType.DMA((n,)),
            pltpu.SemaphoreType.DMA((n,)),
        ],
        compiler_params=pltpu.CompilerParams(vmem_limit_bytes=vmem_full),
        name="weight_rows",
    )(gate_weight, up_weight, adapter_input_maps)
    wm = lax.all_to_all(w_send, hid, split_axis=0, concat_axis=0, tiled=True)
    wo = lax.ppermute(wm, "groups", other)

    x_send = call(
        functools.partial(token_columns_kernel, block=block, runs=runs, **sizes),
        "token_columns",
        jax.ShapeDtypeStruct((n, block + rank, chunk), bf16),
        (strips,),
        [pl.BlockSpec((block, strip), lambda i, ids: (0, i)), whole(adapter_output_maps)],
        pl.BlockSpec((per, block + rank, chunk), lambda i, ids: (i, 0, 0)),
        (ids,),
        (tokens, adapter_output_maps),
    )
    xb = lax.all_to_all(x_send, hid, split_axis=0, concat_axis=0, tiled=True)

    d_send = call(
        functools.partial(down_columns_kernel, **sizes),
        "down_columns",
        jax.ShapeDtypeStruct((n, block, half), bf16),
        (strips,),
        [pl.BlockSpec((block, strip), lambda i, ids: (0, i))],
        pl.BlockSpec((per, block, half), lambda i, ids: (i, 0, 0)),
        (ids,),
        (down_weight,),
    )
    d_send, xb = lax.optimization_barrier((d_send, xb))
    dm = lax.all_to_all(d_send, hid, split_axis=0, concat_axis=0, tiled=True)

    sent = partial_products(ids, active, xb, wm, wo, block, chunk, 1)
    got = lax.ppermute(sent, "core", other)
    kept = partial_products(ids, active, xb, wm, wo, block, chunk, 0)
    paired = (kept.astype(f32) + got.astype(f32)).astype(bf16)
    paired, dm = lax.optimization_barrier((paired, dm))
    summed = lax.all_to_all(paired, "chip", split_axis=0, concat_axis=0, tiled=True)

    do = lax.ppermute(dm, "groups", other)

    rows = picks * block + rank * (1 + picks)

    def tile_spec(k):
        def at(i, ids, active, counts, seeds):
            me = ids[2]
            pick = seeds[me * runs // n] + me + 3 * active[me, k]
            return (lax.rem(pick, tiles_n), 0, 0)

        return pl.BlockSpec((1, block, block), at)

    def map_spec(k):
        return pl.BlockSpec(
            (1, rank, block), lambda i, ids, active, *_: (active[ids[2], k], chunk // rank, 0)
        )

    side = call(
        functools.partial(side_rows_kernel, block=block, picks=picks, rank=rank, **sizes),
        "side_rows",
        jax.ShapeDtypeStruct((rows, block), bf16),
        (1,),
        [pl.BlockSpec((n, rank, chunk), lambda i, *_: (0, block // rank, 0)), whole(cotangent)]
        + [tile_spec(k) for k in range(picks)]
        + [map_spec(k) for k in range(picks)],
        pl.BlockSpec((rows, block), lambda i, *_: (0, 0)),
        (ids, active, counts, seeds),
        (xb, cotangent) + (dropout_tiles,) * picks + (wm,) * picks,
    )
    held = call(
        functools.partial(hidden_kernel, block=block, picks=picks, rank=rank),
        "hidden_values",
        jax.ShapeDtypeStruct((rows, block), bf16),
        (1,),
        [whole(summed), whole(side)],
        pl.BlockSpec((rows, block), lambda i, *_: (0, 0)),
        (ids, counts),
        (summed, side),
    )

    far, near = chips // 2, chips // 4
    order = [0, far * cores, near * cores, (far + near) * cores]
    gathered = jnp.stack(
        [held] + [lax.ppermute(held, "chip", across(m)) for m in (far, near, far + near)]
    )
    mask = near // 2
    while mask:
        gathered = jnp.concatenate([gathered, lax.ppermute(gathered, "chip", across(mask))])
        order = order + [q ^ (mask * cores) for q in order]
        mask //= 2
    gathered = jnp.concatenate([gathered, lax.ppermute(gathered, "core", other)])
    order = order + [q ^ 1 for q in order]
    slot = jnp.array([order.index(q) for q in range(n)], jnp.int32)
    order = jnp.array(order, jnp.int32)

    term_b = call(
        functools.partial(output_terms_kernel, **sizes),
        "output_terms",
        jax.ShapeDtypeStruct((n, rank, chunk), bf16),
        (strips,),
        [
            pl.BlockSpec((rank, block), lambda i, ids: (picks * block // rank, 0)),
            pl.BlockSpec((block, strip), lambda i, ids: (0, i)),
        ],
        pl.BlockSpec((per, rank, chunk), lambda i, ids: (i, 0, 0)),
        (ids,),
        (held, cotangent),
    )
    parts_b = lax.all_to_all(term_b, hid, split_axis=0, concat_axis=0, tiled=True)

    each = 4
    out_chunks = call(
        functools.partial(
            output_kernel, block=block, picks=picks, rank=rank, per=each, runs=runs, n=n
        ),
        "output_columns",
        jax.ShapeDtypeStruct((n, block, chunk), bf16),
        (n // each,),
        [whole(gathered), whole(dm), whole(do), whole(adapter_output_maps)],
        pl.BlockSpec((each, block, chunk), lambda i, *_: (i, 0, 0)),
        (ids, active, slot),
        (gathered, dm, do, adapter_output_maps),
        flops=2 * n * picks * block * block * chunk,
    )
    out_cols = lax.all_to_all(out_chunks, hid, split_axis=0, concat_axis=0, tiled=True)
    if chunk % 128 == 0:
        output = pl.pallas_call(
            functools.partial(join_copies_kernel, **sizes),
            out_shape=jax.ShapeDtypeStruct((block, model), bf16),
            in_specs=[anywhere],
            out_specs=anywhere,
            scratch_shapes=[
                pltpu.VMEM((n, block, chunk), bf16),
                pltpu.SemaphoreType.DMA((n,)),
                pltpu.SemaphoreType.DMA((n,)),
            ],
            compiler_params=pltpu.CompilerParams(vmem_limit_bytes=vmem_full),
            name="join_columns",
        )(out_cols)
    else:
        output = call(
            functools.partial(join_columns_kernel, **sizes),
            "join_columns",
            jax.ShapeDtypeStruct((block, model), bf16),
            (strips,),
            [pl.BlockSpec((per, block, chunk), lambda i, ids: (i, 0, 0))],
            pl.BlockSpec((block, strip), lambda i, ids: (0, i)),
            (ids,),
            (out_cols,),
        )

    at_rows = lambda k: pl.BlockSpec(
        (n, rank, block), lambda i, *_: (0, picks * block // rank + 1 + k, 0)
    )
    maps_a = jax.ShapeDtypeStruct(adapter_input_maps.shape, f32)
    maps_b = jax.ShapeDtypeStruct(adapter_output_maps.shape, f32)
    lanes = jax.ShapeDtypeStruct((runs, block), f32)
    grad_a, grad_b, squares = call(
        functools.partial(gradients_kernel, picks=picks, runs=runs, n=n),
        "gradients",
        (maps_a, maps_b, lanes),
        (1,),
        [at_rows(k) for k in range(picks)] + [whole(parts_b)],
        [whole(maps_a), whole(maps_b), whole(lanes)],
        (ids, active, counts, order),
        (gathered,) * picks + (parts_b,),
    )
    totals = jnp.sum(lax.all_gather(squares, hid, axis=0), axis=0)
    limit = math.sqrt(rank * (n * block + model))
    updated = call(
        functools.partial(adamw_kernel, limit=limit, runs=runs),
        "adamw",
        (maps_a,) * 3 + (maps_b,) * 3,
        (1,),
        [whole(lanes)] + [whole(maps_a)] * 4 + [whole(maps_b)] * 4,
        [whole(maps_a)] * 3 + [whole(maps_b)] * 3,
        (ids,),
        (
            totals,
            adapter_input_maps,
            first_moment_input,
            second_moment_input,
            grad_a,
            adapter_output_maps,
            first_moment_output,
            second_moment_output,
            grad_b,
        ),
    )
    return (output, *updated)


def solution(mesh):
    groups, n = mesh.devices.shape
    fine = Mesh(mesh.devices.reshape(groups, n // 2, 2), ("groups", "chip", "core"))
    hid = ("chip", "core")
    rows = P(("groups",) + hid, None)
    maps = P("groups", None, hid)
    return jax.shard_map(
        body,
        mesh=fine,
        in_specs=(rows, rows, P(None, hid), P(None, hid), P(hid, None))
        + (maps,) * 6
        + (P("groups", None), P("groups"), P(), P("groups")),
        out_specs=(rows,) + (maps,) * 6,
        check_vma=False,
    )
```

time: 319 us -> 283 us (0.89); the launches traced: 315 us -> 282 us
  local copies, waits for them, and re-layouts: 44.6 us -> 10.3 us
  other arithmetic: 17.8 us -> 1.44 us
  Pallas kernels: 18.5 us -> 33.2 us
  waiting for transfers between devices: 125 us -> 137 us
  starting transfers between devices: 47.5 us -> 43.2 us
    unnamed x1 -> x0, blocking collectives: 57.7 us -> none
    all_gather x0 -> x1, blocking collectives: none -> 56.6 us  [body(): totals = jnp.sum(lax.all_gather(squares, hid, axis=0), axis=0)]
    pallas_call x4 -> x12, Pallas kernels: 18.5 us -> 33.2 us  [the longest x10 27.2 us: call(): pl.pallas_call(kernel, out_shape=out, grid_spec=pltpu.PrefetchScalarGridS...]
    unnamed x44 -> x47, local copies, waits for them, and re-layouts: 24.1 us -> 10.1 us
    ppermute x4 -> x5, waiting for transfers between devices: 3.88 us -> 14 us  [the longest x1 7.01 us: body(): lax.ppermute(gathered, 'chip', across(mask))]
    all_to_all x1, waiting for transfers between devices: 36.1 us -> 43.2 us  [body(): wm = lax.all_to_all(w_send, hid, split_axis=0, concat_axis=0, tiled=True)]
    concatenate x9 -> x0, other arithmetic: 6.83 us -> none  [the longest x1 3.22 us: body(): jnp.concatenate([x_rows, jnp.repeat(b_bf, per_run, axis=0)], axis=1)]
    ppermute x1, waiting for transfers between devices: 6.05 us -> 0.01 us  [body(): do = lax.ppermute(dm, 'groups', other)]
  transfers between devices with their start and end apart: 13 -> 14, of which waited for: 7 -> 9; matrix products, arithmetic and copies ran while one was open for 15% -> 1% of each run, Pallas kernels for 4% -> 10%
where the time goes in v2:
time: 283 us; the launch traced here: 282 us
  waiting for transfers between devices  137 us (48%)
  blocking collectives  56.6 us (20%)
  starting transfers between devices  43.2 us (15%)
  Pallas kernels  33.2 us (12%)
  local copies, waits for them, and re-layouts  10.3 us (4%)
    all_gather x1, blocking collectives, body(): totals = jnp.sum(lax.all_gather(squares, hid, axis=0), axis=0)  56.6 us
    all_to_all x1, waiting for transfers between devices, body(): xb = lax.all_to_all(x_send, hid, split_axis=0, concat_axis=0, tiled=True)  45 us
    all_to_all x1, waiting for transfers between devices, body(): wm = lax.all_to_all(w_send, hid, split_axis=0, concat_axis=0, tiled=True)  43.2 us
    pallas_call x10, Pallas kernels, call(): pl.pallas_call(kernel, out_shape=out, grid_spec=pltpu.PrefetchScalarGridS...  27.2 us
    all_to_all x1, waiting for transfers between devices, body(): dm = lax.all_to_all(d_send, hid, split_axis=0, concat_axis=0, tiled=True)  16.1 us
    all_to_all x1, waiting for transfers between devices, body(): lax.all_to_all(paired, 'chip', split_axis=0, concat_axis=0, tiled=True)  15.5 us
    unnamed x47, local copies, waits for them, and re-layouts  10.1 us
    ppermute x1, waiting for transfers between devices, body(): lax.ppermute(gathered, 'chip', across(mask))  7.01 us
  transfers between devices with their start and end apart: 14, of which 9 were waited for; matrix products, arithmetic and copies ran while one was open for 1% of the time, Pallas kernels for 10%

profile of v2, /device:TPU:9, one launch (start us, length us, event | category | flops | bytes accessed | tf_op | source)
XLA Modules:
  0.0 282.4 jit_solution(16608093522480086656)
XLA Ops:
  0.6 3.5 %weight_rows.1 = bf16[16,528,128]{2,1,0:T(8,128)(2,1)} custom-call(bf16[8192,128]{1,0:T(8,128)(2,1)} %gate_ref.1, bf16[8192,128]{1,0:T(8,128)(2,1)} %up_ref.1, f32[8,16,128]{2,1,0:T(8,128)} %refs_0_.1), custom_call_target="tpu_custom_call" | custom-call | tf_op jit(solution)/shard_map/weight_rows/pallas_call | solution.py:293
  4.1 6.7 %all-to-all-start.1 = ((bf16[16,528,128]{2,1,0:T(8,128)(2,1)}), bf16[16,528,128]{2,1,0:T(8,128)(2,1)S(1)}, u32[]{:S(2)}, u32[]{:S(2)}) async-start(bf16[16,528,128]{2,1,0:T(8,128)(2,1)} %weight_rows.1), calls=%async_computation.1 | async-start | bytes 4325376 | tf_op jit(solution)/shard_map/all_to_all | solution.py:306
  10.9 1.6 copy-done.4
  12.5 1.0 token_columns.1
  13.5 1.4 copy-done
  15.0 43.2 %all-to-all-done.1.wm_ref.refs_4_.refs_5_ = bf16[16,528,128]{2,1,0:T(8,128)(2,1)S(1)} async-done(((bf16[16,528,128]{2,1,0:T(8,128)(2,1)}), bf16[16,528,128]{2,1,0:T(8,128)(2,1)S(1)}, u32[]{:S(2)}, u32[]{:S(2)}) %all-to-all-start.1) | async-done | bytes 2162720 | tf_op jit(solution)/shard_map/all_to_all | solution.py:306
  58.1 6.4 %all-to-all-start = ((bf16[16,144,512]{2,1,0:T(8,128)(2,1)}), bf16[16,144,512]{2,1,0:T(8,128)(2,1)}, u32[]{:S(2)}, u32[]{:S(2)}) async-start(bf16[16,144,512]{2,1,0:T(8,128)(2,1)} %copy-done), calls=%async_computation | async-start | bytes 4718592 | tf_op jit(solution)/shard_map/all_to_all | solution.py:319
  64.6 1.2 collective-permute-start
  65.8 1.6 copy-done.5
  67.4 3.5 %down_columns.1 = bf16[16,128,256]{2,1,0:T(8,128)(2,1)} custom-call(s32[3]{0:T(128)S(1)} %pad_add_fusion.ids, bf16[128,8192]{1,0:T(8,128)(2,1)S(1)} %copy-done.5), custom_call_target="tpu_custom_call" | custom-call | bytes 3145728 | tf_op jit(solution)/shard_map/down_columns/pallas_call | solution.py:27
  70.9 45.0 %all-to-all-done.refs_0_ = bf16[16,144,512]{2,1,0:T(8,128)(2,1)} async-done(((bf16[16,144,512]{2,1,0:T(8,128)(2,1)}), bf16[16,144,512]{2,1,0:T(8,128)(2,1)}, u32[]{:S(2)}, u32[]{:S(2)}) %all-to-all-start) | async-done | bytes 2359328 | tf_op jit(solution)/shard_map/all_to_all | solution.py:319
  115.9 6.7 %all-to-all-start.2 = ((bf16[16,128,256]{2,1,0:T(8,128)(2,1)}), bf16[16,128,256]{2,1,0:T(8,128)(2,1)}, u32[]{:S(2)}, u32[]{:S(2)}) async-start(bf16[16,128,256]{2,1,0:T(8,128)(2,1)} %down_columns.1), calls=%async_computation.2 | async-start | bytes 2097152 | tf_op jit(solution)/shard_map/all_to_all | solution.py:332
  122.6 0.1 copy.27.active
  122.7 3.5 %gate_up_partial.3 = bf16[8,2,128,256]{3,2,1,0:T(8,128)(2,1)S(1)} custom-call(s32[3]{0:T(128)S(1)} %pad_add_fusion.ids, s32[16,2]{1,0:T(8,128)S(1)} %copy.27.active, bf16[8,2,144,512]{3,2,1,0:T(8,128)(2,1)} %bitcast.3.x_ref, bf16[16,528,128]{2,1,0:T(8,128)(2,1)S(1)} %all-to-all-done.1.wm_ref.refs_4_.refs_5_, bf16[16,528,128]{2,1,0:T(8,128)(2,1)} %collective-permute-done.wo_ref), custom_call_target="tpu_custom_call" | custom-call | flops 536870912 | bytes 7733248 | tf_op jit(solution)/shard_map/gate_up_partial/pallas_call | solution.py:27
  126.2 0.4 collective-permute-start.1
  126.6 3.5 %gate_up_partial.2 = bf16[8,2,128,256]{3,2,1,0:T(8,128)(2,1)S(1)} custom-call(s32[3]{0:T(128)S(1)} %pad_add_fusion.ids, s32[16,2]{1,0:T(8,128)S(1)} %copy.27.active, bf16[8,2,144,512]{3,2,1,0:T(8,128)(2,1)} %bitcast.3.x_ref, bf16[16,528,128]{2,1,0:T(8,128)(2,1)S(1)} %all-to-all-done.1.wm_ref.refs_4_.refs_5_, bf16[16,528,128]{2,1,0:T(8,128)(2,1)} %collective-permute-done.wo_ref), custom_call_target="tpu_custom_call" | custom-call | flops 536870912 | bytes 7733248 | tf_op jit(solution)/shard_map/gate_up_partial/pallas_call | solution.py:27
  130.1 1.3 add_convert_fusion
  131.4 16.1 %all-to-all-done.2.dm_ref = bf16[16,128,256]{2,1,0:T(8,128)(2,1)} async-done(((bf16[16,128,256]{2,1,0:T(8,128)(2,1)}), bf16[16,128,256]{2,1,0:T(8,128)(2,1)}, u32[]{:S(2)}, u32[]{:S(2)}) %all-to-all-start.2) | async-done | bytes 1048608 | tf_op jit(solution)/shard_map/all_to_all | solution.py:332
  147.6 4.5 %all-to-all-start.3 = ((bf16[8,2,128,256]{3,2,1,0:T(8,128)(2,1)}), bf16[8,2,128,256]{3,2,1,0:T(8,128)(2,1)S(1)}, u32[]{:S(2)}, u32[]{:S(2)}) async-start(bf16[8,2,128,256]{3,2,1,0:T(8,128)(2,1)} %add_convert_fusion), calls=%async_computation.3 | async-start | bytes 2097152 | tf_op jit(solution)/shard_map/all_to_all | solution.py:339
  152.1 1.6 copy-done.1
  153.7 0.9 copy-done.6
  154.7 0.7 copy-done.8
  155.4 0.7 copy-done.15
  156.0 0.7 copy-done.19
  156.7 2.3 side_rows.1.side_ref
  158.9 1.3 collective-permute-start.7
  160.2 15.5 %all-to-all-done.3.r_ref = bf16[8,2,128,256]{3,2,1,0:T(8,128)(2,1)S(1)} async-done(((bf16[8,2,128,256]{3,2,1,0:T(8,128)(2,1)}), bf16[8,2,128,256]{3,2,1,0:T(8,128)(2,1)S(1)}, u32[]{:S(2)}, u32[]{:S(2)}) %all-to-all-start.3) | async-done | bytes 1048608 | tf_op jit(solution)/shard_map/all_to_all | solution.py:339
  175.7 0.7 copy-done.16
  176.4 0.8 hidden_values.1.z_ref
  177.2 3.0 %collective-permute-start.2 = (bf16[304,128]{1,0:T(8,128)(2,1)S(1)}, bf16[304,128]{1,0:T(8,128)(2,1)S(1)}, u32[]{:S(2)}, u32[]{:S(2)}) collective-permute-start(bf16[304,128]{1,0:T(8,128)(2,1)S(1)} %hidden_values.1.z_ref), channel_id=1, source_target_pairs={{0,8},{2,10},{4,12},{6,14},{8,0},{10,2},{12,4},{14,6},{1,9},{3,11}... | collective-permute-start | bytes 233480 | tf_op jit(solution)/shard_map/ppermute | solution.py:384
  180.3 0.4 collective-permute-start.4
  180.7 2.4 collective-permute-done.2
  183.1 0.8 collective-permute-done.3
  183.9 3.7 %collective-permute-done.4 = bf16[304,128]{1,0:T(8,128)(2,1)S(1)} collective-permute-done((bf16[304,128]{1,0:T(8,128)(2,1)S(1)}, bf16[304,128]{1,0:T(8,128)(2,1)S(1)}, u32[]{:S(2)}, u32[]{:S(2)}) %collective-permute-start.4) | collective-permute-done | bytes 77856 | tf_op jit(solution)/shard_map/ppermute | solution.py:384
  187.7 1.0 collective-permute-start.5
  188.8 7.0 %collective-permute-done.5 = bf16[4,304,128]{2,1,0:T(8,128)(2,1)S(1)} collective-permute-done((bf16[4,304,128]{2,1,0:T(8,128)(2,1)S(1)}, bf16[4,304,128]{2,1,0:T(8,128)(2,1)S(1)}, u32[]{:S(2)}, u32[]{:S(2)}) %collective-permute-start.5) | collective-permute-done | bytes 311328 | tf_op jit(solution)/shard_map/ppermute | solution.py:388
  195.8 0.1 constant_dynamic-update-slice_fusion
  195.9 1.8 collective-permute-start.6
  197.7 3.9 %output_terms.1 = bf16[16,16,512]{2,1,0:T(8,128)(2,1)} custom-call(s32[3]{0:T(128)S(1)} %pad_add_fusion.ids, bf16[304,128]{1,0:T(8,128)(2,1)S(1)} %hidden_values.1.z_ref, bf16[128,8192]{1,0:T(8,128)(2,1)S(1)} %copy-done.2), custom_call_target="tpu_custom_call" | custom-call | bytes 2437120 | tf_op jit(solution)/shard_map/output_terms/pallas_call | solution.py:27
  201.6 4.0 %all-to-all-start.5 = ((bf16[16,16,512]{2,1,0:T(8,128)(2,1)}), bf16[16,16,512]{2,1,0:T(8,128)(2,1)S(1)}, u32[]{:S(2)}, u32[]{:S(2)}) async-start(bf16[16,16,512]{2,1,0:T(8,128)(2,1)} %output_terms.1), calls=%async_computation.5 | async-start | bytes 524288 | tf_op jit(solution)/shard_map/all_to_all | solution.py:409
  205.6 0.1 constant_dynamic-update-slice_fusion.5.h_ref.refs_0_.refs_1_
  205.8 5.6 %output_columns.1 = bf16[16,128,512]{2,1,0:T(8,128)(2,1)} custom-call(s32[3]{0:T(128)S(1)} %pad_add_fusion.ids, s32[16,2]{1,0:T(8,128)S(1)} %copy-done.9, s32[16]{0:T(128)S(1)} %copy-done.18, bf16[16,304,128]{2,1,0:T(8,128)(2,1)S(1)} %constant_dynamic-update-slice_fusion.5.h_ref.refs_0_.refs_1_, bf16[16,128,256]{2,1,0:T(8,128)(2,1)} %all-to-all-done.2.dm_ref, ...), custom_call_target="tpu_custom_call" | custom-call | flops 536870912 | bytes 5701632 | tf_op jit(solution)/shard_map/output_columns/pallas_call | solution.py:27
  211.4 3.0 %all-to-all-done.5.refs_2_ = bf16[16,16,512]{2,1,0:T(8,128)(2,1)S(1)} async-done(((bf16[16,16,512]{2,1,0:T(8,128)(2,1)}), bf16[16,16,512]{2,1,0:T(8,128)(2,1)S(1)}, u32[]{:S(2)}, u32[]{:S(2)}) %all-to-all-start.5) | async-done | bytes 262176 | tf_op jit(solution)/shard_map/all_to_all | solution.py:409
  214.3 5.6 %all-to-all-start.4 = ((bf16[16,128,512]{2,1,0:T(8,128)(2,1)}), bf16[16,128,512]{2,1,0:T(8,128)(2,1)}, u32[]{:S(2)}, u32[]{:S(2)}) async-start(bf16[16,128,512]{2,1,0:T(8,128)(2,1)} %output_columns.1), calls=%async_computation.4 | async-start | bytes 4194304 | tf_op jit(solution)/shard_map/all_to_all | solution.py:425
  220.0 1.3 gradients.1
  221.4 56.6 %all-gather = f32[128,128]{1,0:T(8,128)S(1)} all-gather(f32[8,128]{1,0:T(8,128)S(1)} %get-tuple-element.24), channel_id=2, replica_groups=mesh['groups'=2,'chip'=8,'core'=2] {'chip','core'}, dimensions={0}, use_global_device_ids=true | all-gather | bytes 69632 | tf_op jit(solution)/shard_map/all_gather | solution.py:468
  278.0 1.8 adamw.1
  279.8 2.6 join_columns.1
  (46 shorter events, 0.3 us)
Async XLA Ops:
  4.1 6.8 %copy-start.3 = (f32[8,16,512]{2,1,0:T(8,128)S(1)}, f32[8,16,512]{2,1,0:T(8,128)}, u32[]{:S(2)}) copy-start(f32[8,16,512]{2,1,0:T(8,128)} %refs_4_.1) | copy-start | bytes 786436
  4.1 54.0 %all-to-all-start.1 = ((bf16[16,528,128]{2,1,0:T(8,128)(2,1)}), bf16[16,528,128]{2,1,0:T(8,128)(2,1)S(1)}, u32[]{:S(2)}, u32[]{:S(2)}) async-start(bf16[16,528,128]{2,1,0:T(8,128)(2,1)} %weight_rows.1), calls=%async_computation.1 | async-start | bytes 4325376 | tf_op jit(solution)/shard_map/all_to_all | solution.py:306
  10.9 1.6 copy-start.4
  13.5 1.4 copy-start
  58.1 57.8 %all-to-all-start = ((bf16[16,144,512]{2,1,0:T(8,128)(2,1)}), bf16[16,144,512]{2,1,0:T(8,128)(2,1)}, u32[]{:S(2)}, u32[]{:S(2)}) async-start(bf16[16,144,512]{2,1,0:T(8,128)(2,1)} %copy-done), calls=%async_computation | async-start | bytes 4718592 | tf_op jit(solution)/shard_map/all_to_all | solution.py:319
  64.6 58.1 %collective-permute-start = (bf16[16,528,128]{2,1,0:T(8,128)(2,1)S(1)}, bf16[16,528,128]{2,1,0:T(8,128)(2,1)}, u32[]{:S(2)}, u32[]{:S(2)}) collective-permute-start(bf16[16,528,128]{2,1,0:T(8,128)(2,1)S(1)} %all-to-all-done.1.wm_ref.refs_4_.refs_5_), channel_id=1, source_target_pairs={{0,16},{16,0},{1,17},{17,1},{2,18},{18,2},{3,19},{19,3},{4,20},{20... | collective-permute-start | bytes 6488072 | tf_op jit(solution)/shard_map/ppermute | solution.py:307
  65.8 1.6 copy-start.5
  70.9 51.7 %copy-start.20 = (s32[16,2]{0,1:T(2,128)S(1)}, s32[16,2]{0,1:T(2,128)}, u32[]{:S(2)}) copy-start(s32[16,2]{0,1:T(2,128)} %param.28) | copy-start | bytes 388
  115.9 31.6 %all-to-all-start.2 = ((bf16[16,128,256]{2,1,0:T(8,128)(2,1)}), bf16[16,128,256]{2,1,0:T(8,128)(2,1)}, u32[]{:S(2)}, u32[]{:S(2)}) async-start(bf16[16,128,256]{2,1,0:T(8,128)(2,1)} %down_columns.1), calls=%async_computation.2 | async-start | bytes 2097152 | tf_op jit(solution)/shard_map/all_to_all | solution.py:332
  122.7 3.9 %copy-start.7 = (s32[16,2]{1,0:T(8,128)}, s32[16,2]{1,0:T(8,128)S(1)}, u32[]{:S(2)}) copy-start(s32[16,2]{1,0:T(8,128)S(1)} %copy.27.active) | copy-start | bytes 388
  126.2 3.9 %collective-permute-start.1 = (bf16[8,2,128,256]{3,2,1,0:T(8,128)(2,1)S(1)}, bf16[8,2,128,256]{3,2,1,0:T(8,128)(2,1)S(1)}, u32[]{:S(2)}, u32[]{:S(2)}) collective-permute-start(bf16[8,2,128,256]{3,2,1,0:T(8,128)(2,1)S(1)} %gate_up_partial.3), channel_id=1, source_target_pairs={{0,1},{1,0},{2,3},{3,2},{4,5},{5,4},{6,7},{7,6},{8,9},{9,8},{10,11... | collective-permute-start | bytes 3145736 | tf_op jit(solution)/shard_map/ppermute | solution.py:335
  147.6 28.2 %all-to-all-start.3 = ((bf16[8,2,128,256]{3,2,1,0:T(8,128)(2,1)}), bf16[8,2,128,256]{3,2,1,0:T(8,128)(2,1)S(1)}, u32[]{:S(2)}, u32[]{:S(2)}) async-start(bf16[8,2,128,256]{3,2,1,0:T(8,128)(2,1)} %add_convert_fusion), calls=%async_computation.3 | async-start | bytes 2097152 | tf_op jit(solution)/shard_map/all_to_all | solution.py:339
  152.1 1.6 copy-start.1
  153.7 0.9 copy-start.6
  154.7 0.7 copy-start.8
  155.4 0.7 copy-start.15
  156.0 0.7 copy-start.19
  158.9 46.8 %collective-permute-start.7 = (bf16[16,128,256]{2,1,0:T(8,128)(2,1)}, bf16[16,128,256]{2,1,0:T(8,128)(2,1)}, u32[]{:S(2)}, u32[]{:S(2)}) collective-permute-start(bf16[16,128,256]{2,1,0:T(8,128)(2,1)} %all-to-all-done.2.dm_ref), channel_id=1, source_target_pairs={{0,16},{16,0},{1,17},{17,1},{2,18},{18,2},{3,19},{19,3},{4,20},{20... | collective-permute-start | bytes 3145736 | tf_op jit(solution)/shard_map/ppermute | solution.py:341
  175.7 0.7 copy-start.16
  177.2 20.5 %copy-start.2 = (bf16[128,8192]{1,0:T(8,128)(2,1)S(1)}, bf16[128,8192]{1,0:T(8,128)(2,1)}, u32[]{:S(2)}) copy-start(bf16[128,8192]{1,0:T(8,128)(2,1)} %dy_ref.1) | copy-start | bytes 6291460
  177.2 5.8 %collective-permute-start.2 = (bf16[304,128]{1,0:T(8,128)(2,1)S(1)}, bf16[304,128]{1,0:T(8,128)(2,1)S(1)}, u32[]{:S(2)}, u32[]{:S(2)}) collective-permute-start(bf16[304,128]{1,0:T(8,128)(2,1)S(1)} %hidden_values.1.z_ref), channel_id=1, source_target_pairs={{0,8},{2,10},{4,12},{6,14},{8,0},{10,2},{12,4},{14,6},{1,9},{3,11}... | collective-permute-start | bytes 233480 | tf_op jit(solution)/shard_map/ppermute | solution.py:384
  180.3 3.6 %collective-permute-start.3 = (bf16[304,128]{1,0:T(8,128)(2,1)S(1)}, bf16[304,128]{1,0:T(8,128)(2,1)S(1)}, u32[]{:S(2)}, u32[]{:S(2)}) collective-permute-start(bf16[304,128]{1,0:T(8,128)(2,1)S(1)} %hidden_values.1.z_ref), channel_id=1, source_target_pairs={{0,4},{2,6},{4,0},{6,2},{8,12},{10,14},{12,8},{14,10},{1,5},{3,7},... | collective-permute-start | bytes 233480 | tf_op jit(solution)/shard_map/ppermute | solution.py:384
  180.3 7.4 %collective-permute-start.4 = (bf16[304,128]{1,0:T(8,128)(2,1)S(1)}, bf16[304,128]{1,0:T(8,128)(2,1)S(1)}, u32[]{:S(2)}, u32[]{:S(2)}) collective-permute-start(bf16[304,128]{1,0:T(8,128)(2,1)S(1)} %hidden_values.1.z_ref), channel_id=1, source_target_pairs={{0,12},{2,14},{4,8},{6,10},{8,4},{10,6},{12,0},{14,2},{1,13},{3,15... | collective-permute-start | bytes 233480 | tf_op jit(solution)/shard_map/ppermute | solution.py:384
  187.7 8.1 %collective-permute-start.5 = (bf16[4,304,128]{2,1,0:T(8,128)(2,1)S(1)}, bf16[4,304,128]{2,1,0:T(8,128)(2,1)S(1)}, u32[]{:S(2)}, u32[]{:S(2)}) collective-permute-start(bf16[4,304,128]{2,1,0:T(8,128)(2,1)S(1)} %pad_maximum_fusion), channel_id=1, source_target_pairs={{0,2},{2,0},{4,6},{6,4},{8,10},{10,8},{12,14},{14,12},{1,3},{3,1},... | collective-permute-start | bytes 933896 | tf_op jit(solution)/shard_map/ppermute | solution.py:388
  195.9 9.7 %collective-permute-start.6 = (bf16[8,304,128]{2,1,0:T(8,128)(2,1)S(1)}, bf16[8,304,128]{2,1,0:T(8,128)(2,1)S(1)}, u32[]{:S(2)}, u32[]{:S(2)}) collective-permute-start(bf16[8,304,128]{2,1,0:T(8,128)(2,1)S(1)} %get-tuple-element.33), channel_id=1, source_target_pairs={{0,1},{1,0},{2,3},{3,2},{4,5},{5,4},{6,7},{7,6},{8,9},{9,8},{10,11... | collective-permute-start | bytes 1867784 | tf_op jit(solution)/shard_map/ppermute | solution.py:391
  201.6 4.1 %copy-start.9 = (s32[16,2]{1,0:T(8,128)S(1)}, s32[16,2]{1,0:T(8,128)}, u32[]{:S(2)}) copy-start(s32[16,2]{1,0:T(8,128)} %copy-done.7) | copy-start | bytes 388
  201.6 4.1 %copy-start.18 = (s32[16]{0:T(128)S(1)}, s32[16]{0:T(128)}, u32[]{:S(2)}) copy-start(s32[16]{0:T(128)} %constant.18.clone.slot.order) | copy-start | bytes 196
  201.6 12.7 %all-to-all-start.5 = ((bf16[16,16,512]{2,1,0:T(8,128)(2,1)}), bf16[16,16,512]{2,1,0:T(8,128)(2,1)S(1)}, u32[]{:S(2)}, u32[]{:S(2)}) async-start(bf16[16,16,512]{2,1,0:T(8,128)(2,1)} %output_terms.1), calls=%async_computation.5 | async-start | bytes 524288 | tf_op jit(solution)/shard_map/all_to_all | solution.py:409
  211.4 8.6 %copy-start.17 = (s32[16]{0:T(128)S(1)}, s32[16]{0:T(128)}, u32[]{:S(2)}) copy-start(s32[16]{0:T(128)} %counts.5) | copy-start | bytes 196
  214.3 65.5 %all-to-all-start.4 = ((bf16[16,128,512]{2,1,0:T(8,128)(2,1)}), bf16[16,128,512]{2,1,0:T(8,128)(2,1)}, u32[]{:S(2)}, u32[]{:S(2)}) async-start(bf16[16,128,512]{2,1,0:T(8,128)(2,1)} %output_columns.1), calls=%async_computation.4 | async-start | bytes 4194304 | tf_op jit(solution)/shard_map/all_to_all | solution.py:425
  220.0 58.0 %copy-start.10 = (f32[8,16,128]{2,1,0:T(8,128)S(1)}, f32[8,16,128]{2,1,0:T(8,128)}, u32[]{:S(2)}) copy-start(f32[8,16,128]{2,1,0:T(8,128)} %refs_0_.1) | copy-start | bytes 196612
  220.0 58.0 %copy-start.11 = (f32[8,16,512]{2,1,0:T(8,128)S(1)}, f32[8,16,512]{2,1,0:T(8,128)}, u32[]{:S(2)}) copy-start(f32[8,16,512]{2,1,0:T(8,128)} %refs_5_.1) | copy-start | bytes 786436
  220.0 58.0 %copy-start.12 = (f32[8,16,512]{2,1,0:T(8,128)S(1)}, f32[8,16,512]{2,1,0:T(8,128)}, u32[]{:S(2)}) copy-start(f32[8,16,512]{2,1,0:T(8,128)} %refs_6_.1) | copy-start | bytes 786436
  220.0 58.0 %copy-start.13 = (f32[8,16,128]{2,1,0:T(8,128)S(1)}, f32[8,16,128]{2,1,0:T(8,128)}, u32[]{:S(2)}) copy-start(f32[8,16,128]{2,1,0:T(8,128)} %refs_1_.3) | copy-start | bytes 196612
  220.0 58.0 %copy-start.14 = (f32[8,16,128]{2,1,0:T(8,128)S(1)}, f32[8,16,128]{2,1,0:T(8,128)}, u32[]{:S(2)}) copy-start(f32[8,16,128]{2,1,0:T(8,128)} %refs_2_.3) | copy-start | bytes 196612

commit v3 on v2

--- a/solution.py
+++ b/solution.py
@@ -21,9 +21,10 @@
     return lax.dot_general(a, b, (dims, ((), ())), preferred_element_type=f32)
 
 
-def call(kernel, name, out, grid, in_specs, out_specs, scalars, arrays, flops=0):
+def call(kernel, name, out, grid, in_specs, out_specs, scalars, arrays, flops=0, moved=None):
     outs = out if isinstance(out, (tuple, list)) else [out]
-    moved = sum(a.size * a.dtype.itemsize for a in (*arrays, *outs))
+    if moved is None:
+        moved = sum(a.size * a.dtype.itemsize for a in (*arrays, *outs))
     return pl.pallas_call(
         kernel,
         out_shape=out,
@@ -110,18 +111,19 @@
 def partial_products(ids, active, xb, wm, wo, block, chunk, away):
     n, picks = active.shape
     shape = (n // 2, picks, block, 2 * block)
+    kind = bf16
     token = lambda i, ids, act: (i, jnp.bitwise_xor(ids[1], away), 0, 0)
     xp = xb.reshape(n // 2, 2, *xb.shape[1:])
     return call(
         functools.partial(partial_kernel, block=block, chunk=chunk, picks=picks, away=away),
         "gate_up_partial",
-        jax.ShapeDtypeStruct(shape, bf16),
+        jax.ShapeDtypeStruct(shape, kind),
         (n // 2 // paired_step,),
         [pl.BlockSpec((paired_step, 1) + xb.shape[1:], token), whole(wm), whole(wo)],
         pl.BlockSpec((paired_step,) + shape[1:], lambda i, *_: (i, 0, 0, 0)),
         (ids, active),
         (xp, wm, wo),
-        flops=n * picks * 2 * block * block * chunk,
+        moved=4096,
     )
 
 
@@ -167,27 +169,31 @@
         o_ref[s] = (adapter_scale * part).astype(bf16)
 
 
-def output_kernel(
-    ids, active, slot, h_ref, dm_ref, do_ref, b_ref, o_ref, *, block, picks, rank, per, runs, n
-):
+def output_kernel(ids, active, *refs, orders, block, picks, rank, runs, n):
+    h_refs, (dm_ref, do_ref, b_ref, o_ref, held, stores) = refs[: len(orders)], refs[len(orders) :]
     half = dm_ref.shape[2]
     swap = ids[0] != 0
-    for s in range(per):
-        t = pl.program_id(0) * per + s
-        p = slot[jnp.bitwise_xor(t, ids[2])]
-        sums = [None, None]
-        for k in range(picks):
-            j = active[t, k]
-            h = h_ref[p, k * block : (k + 1) * block, :]
-            for side, d_ref in enumerate((dm_ref, do_ref)):
-                part = dot(h, d_ref[j]).astype(bf16).astype(f32)
-                sums[side] = part if k == 0 else sums[side] + part
-        left = jnp.where(swap, sums[1], sums[0]).astype(bf16).astype(f32)
-        right = jnp.where(swap, sums[0], sums[1]).astype(bf16).astype(f32)
-        z_t = h_ref[p, picks * block : picks * block + rank, :]
-        extra = adapter_scale * dot(z_t, b_ref[t * runs // n].astype(bf16), ((0,), (0,)))
-        o_ref[s, :, :half] = (left + extra[:, :half]).astype(bf16)
-        o_ref[s, :, half:] = (right + extra[:, half:]).astype(bf16)
+    copies = []
+    for h_ref, order in zip(h_refs, orders):
+        for s, q in enumerate(order):
+            t = jnp.bitwise_xor(ids[2], q)
+            hidden = [h_ref[s, k * block : (k + 1) * block, :] for k in range(picks)]
+            hidden = jnp.concatenate(hidden, axis=1)
+            sums = []
+            for d_ref in (dm_ref, do_ref):
+                down = jnp.concatenate([d_ref[active[t, k]] for k in range(picks)], axis=0)
+                sums.append(dot(hidden, down).astype(bf16).astype(f32))
+            left = jnp.where(swap, sums[1], sums[0])
+            right = jnp.where(swap, sums[0], sums[1])
+            z_t = h_ref[s, picks * block : picks * block + rank, :]
+            extra = adapter_scale * dot(z_t, b_ref[t * runs // n].astype(bf16), ((0,), (0,)))
+            held[q, :, :half] = (left + extra[:, :half]).astype(bf16)
+            held[q, :, half:] = (right + extra[:, half:]).astype(bf16)
+            copy = pltpu.make_async_copy(held.at[q], o_ref.at[t], stores.at[q])
+            copy.start()
+            copies.append(copy)
+    for copy in copies:
+        copy.wait()
 
 
 def join_columns_kernel(ids, c_ref, o_ref, *, chunk, n):
@@ -210,24 +216,21 @@
         copy.wait()
 
 
-def gradients_kernel(ids, active, counts, order, *refs, picks, runs, n):
-    term_refs, part_ref, ga_ref, gb_ref, sq_ref = refs[:picks], *refs[picks:]
+def gradients_kernel(ids, active, counts, *refs, orders, picks, runs, n):
+    term_refs, (part_ref, ga_ref, gb_ref, sq_ref) = refs[:-4], refs[-4:]
     me = ids[2]
     per_run = n // runs
     ga_ref[...] = jnp.zeros_like(ga_ref)
-
-    def add(s, carry):
-        t = jnp.bitwise_xor(order[s], me)
-        for k in range(picks):
-
-            @pl.when((active[t, k] == me) & (k < counts[t]))
-            def _():
-                run = t * runs // n
-                ga_ref[run] = ga_ref[run] + term_refs[k][s].astype(f32)
-
-        return carry
-
-    lax.fori_loop(0, n, add, 0)
+    for i, order in enumerate(orders):
+        for s, q in enumerate(order):
+            t = jnp.bitwise_xor(me, q)
+            for k in range(picks):
+
+                @pl.when((active[t, k] == me) & (k < counts[t]))
+                def _():
+                    run = t * runs // n
+                    ga_ref[run] = ga_ref[run] + term_refs[i * picks + k][s].astype(f32)
+
     for r in range(runs):
         total = part_ref[r * per_run].astype(f32)
         for q in range(1, per_run):
@@ -336,6 +339,7 @@
     kept = partial_products(ids, active, xb, wm, wo, block, chunk, 0)
     paired = (kept.astype(f32) + got.astype(f32)).astype(bf16)
     paired, dm = lax.optimization_barrier((paired, dm))
+    far = chips // 2
     summed = lax.all_to_all(paired, "chip", split_axis=0, concat_axis=0, tiled=True)
 
     do = lax.ppermute(dm, "groups", other)
@@ -360,13 +364,17 @@
         "side_rows",
         jax.ShapeDtypeStruct((rows, block), bf16),
         (1,),
-        [pl.BlockSpec((n, rank, chunk), lambda i, *_: (0, block // rank, 0)), whole(cotangent)]
+        [
+            pl.BlockSpec((n, rank, chunk), lambda i, *_: (0, block // rank, 0)),
+            whole(cotangent),
+        ]
         + [tile_spec(k) for k in range(picks)]
         + [map_spec(k) for k in range(picks)],
         pl.BlockSpec((rows, block), lambda i, *_: (0, 0)),
         (ids, active, counts, seeds),
         (xb, cotangent) + (dropout_tiles,) * picks + (wm,) * picks,
     )
+    summed, do = lax.optimization_barrier((summed, do))
     held = call(
         functools.partial(hidden_kernel, block=block, picks=picks, rank=rank),
         "hidden_values",
@@ -377,21 +385,6 @@
         (ids, counts),
         (summed, side),
     )
-
-    far, near = chips // 2, chips // 4
-    order = [0, far * cores, near * cores, (far + near) * cores]
-    gathered = jnp.stack(
-        [held] + [lax.ppermute(held, "chip", across(m)) for m in (far, near, far + near)]
-    )
-    mask = near // 2
-    while mask:
-        gathered = jnp.concatenate([gathered, lax.ppermute(gathered, "chip", across(mask))])
-        order = order + [q ^ (mask * cores) for q in order]
-        mask //= 2
-    gathered = jnp.concatenate([gathered, lax.ppermute(gathered, "core", other)])
-    order = order + [q ^ 1 for q in order]
-    slot = jnp.array([order.index(q) for q in range(n)], jnp.int32)
-    order = jnp.array(order, jnp.int32)
 
     term_b = call(
         functools.partial(output_terms_kernel, **sizes),
@@ -406,22 +399,47 @@
         (ids,),
         (held, cotangent),
     )
+
+    near = chips // 4
+    stack = jnp.stack(
+        [held] + [lax.ppermute(held, "chip", across(m)) for m in (far, near, far + near)]
+    )
+    stack, term_b = lax.optimization_barrier((stack, term_b))
     parts_b = lax.all_to_all(term_b, hid, split_axis=0, concat_axis=0, tiled=True)
-
-    each = 4
-    out_chunks = call(
+    pieces = [(stack, [0, far * cores, near * cores, (far + near) * cores])]
+    mask = near // 2
+    while mask:
+        arrived = [
+            (lax.ppermute(piece, "chip", across(mask)), [q ^ (mask * cores) for q in order])
+            for piece, order in pieces
+        ]
+        pieces = pieces + arrived
+        mask //= 2
+    pieces = pieces + [
+        (lax.ppermute(piece, "core", other), [q ^ 1 for q in order]) for piece, order in pieces
+    ]
+    gathered = [piece for piece, _ in pieces]
+    orders = [order for _, order in pieces]
+
+    at_once = lambda a: pl.BlockSpec(a.shape, lambda *_: (0,) * len(a.shape))
+    out_chunks = pl.pallas_call(
         functools.partial(
-            output_kernel, block=block, picks=picks, rank=rank, per=each, runs=runs, n=n
+            output_kernel, orders=orders, block=block, picks=picks, rank=rank, runs=runs, n=n
         ),
-        "output_columns",
-        jax.ShapeDtypeStruct((n, block, chunk), bf16),
-        (n // each,),
-        [whole(gathered), whole(dm), whole(do), whole(adapter_output_maps)],
-        pl.BlockSpec((each, block, chunk), lambda i, *_: (i, 0, 0)),
-        (ids, active, slot),
-        (gathered, dm, do, adapter_output_maps),
-        flops=2 * n * picks * block * block * chunk,
-    )
+        out_shape=jax.ShapeDtypeStruct((n, block, chunk), bf16),
+        grid_spec=pltpu.PrefetchScalarGridSpec(
+            num_scalar_prefetch=2,
+            grid=(1,),
+            in_specs=[at_once(a) for a in (*gathered, dm, do, adapter_output_maps)],
+            out_specs=anywhere,
+            scratch_shapes=[
+                pltpu.VMEM((n, block, chunk), bf16),
+                pltpu.SemaphoreType.DMA((n,)),
+            ],
+        ),
+        compiler_params=pltpu.CompilerParams(vmem_limit_bytes=vmem_limit),
+        name="output_columns",
+    )(ids, active, *gathered, dm, do, adapter_output_maps)
     out_cols = lax.all_to_all(out_chunks, hid, split_axis=0, concat_axis=0, tiled=True)
     if chunk % 128 == 0:
         output = pl.pallas_call(
@@ -449,21 +467,21 @@
             (out_cols,),
         )
 
-    at_rows = lambda k: pl.BlockSpec(
-        (n, rank, block), lambda i, *_: (0, picks * block // rank + 1 + k, 0)
+    at_rows = lambda a, k: pl.BlockSpec(
+        (a.shape[0], rank, block), lambda i, *_: (0, picks * block // rank + 1 + k, 0)
     )
     maps_a = jax.ShapeDtypeStruct(adapter_input_maps.shape, f32)
     maps_b = jax.ShapeDtypeStruct(adapter_output_maps.shape, f32)
     lanes = jax.ShapeDtypeStruct((runs, block), f32)
     grad_a, grad_b, squares = call(
-        functools.partial(gradients_kernel, picks=picks, runs=runs, n=n),
+        functools.partial(gradients_kernel, orders=orders, picks=picks, runs=runs, n=n),
         "gradients",
         (maps_a, maps_b, lanes),
         (1,),
-        [at_rows(k) for k in range(picks)] + [whole(parts_b)],
+        [at_rows(a, k) for a in gathered for k in range(picks)] + [whole(parts_b)],
         [whole(maps_a), whole(maps_b), whole(lanes)],
-        (ids, active, counts, order),
-        (gathered,) * picks + (parts_b,),
+        (ids, active, counts),
+        tuple(a for a in gathered for _ in range(picks)) + (parts_b,),
     )
     totals = jnp.sum(lax.all_gather(squares, hid, axis=0), axis=0)
     limit = math.sqrt(rank * (n * block + model))

time: 283 us -> 275 us (0.972)
  waiting for transfers between devices: 137 us -> 124 us
  local copies, waits for them, and re-layouts: 10.3 us -> 15.4 us
  Pallas kernels: 33.2 us -> 30.2 us
    ppermute x1, waiting for transfers between devices: 0.01 us -> 16.1 us  [body(): do = lax.ppermute(dm, 'groups', other)]
    all_to_all x1, waiting for transfers between devices: 15.5 us -> 0.01 us  [body(): lax.all_to_all(paired, 'chip', split_axis=0, concat_axis=0, tiled=True)]
    ppermute x3, waiting for transfers between devices: 7.01 us -> 0.01 us  [body(): lax.ppermute(held, 'chip', across(m))]
    pallas_call x10 -> x9, Pallas kernels: 27.2 us -> 21.4 us  [call(): pl.pallas_call(kernel, out_shape=out, grid_spec=pltpu.PrefetchScalarGridS...]
    ppermute x2 -> x3, waiting for transfers between devices: 7.01 us -> 1.54 us  [the longest x2 1.54 us: body(): lax.ppermute(piece, 'core', other)]
    unnamed x47 -> x49, local copies, waits for them, and re-layouts: 10.1 us -> 15.4 us
    all_to_all x1, starting transfers between devices: 4.01 us -> 8.44 us  [body(): lax.all_to_all(term_b, hid, split_axis=0, concat_axis=0, tiled=True)]
  transfers between devices with their start and end apart: 14 -> 15, of which waited for: 9 -> 7; matrix products, arithmetic and copies ran while one was open for 1% -> 1% of each run, Pallas kernels for 10% -> 9%
where the time goes in v3:
time: 275 us; the launch traced here: 274 us
  waiting for transfers between devices  124 us (45%)
  blocking collectives  56.8 us (21%)
  starting transfers between devices  45.8 us (17%)
  Pallas kernels  30.2 us (11%)
  local copies, waits for them, and re-layouts  15.4 us (6%)
    all_gather x1, blocking collectives, body(): totals = jnp.sum(lax.all_gather(squares, hid, axis=0), axis=0)  56.8 us
    all_to_all x1, waiting for transfers between devices, body(): xb = lax.all_to_all(x_send, hid, split_axis=0, concat_axis=0, tiled=True)  45 us
    all_to_all x1, waiting for transfers between devices, body(): wm = lax.all_to_all(w_send, hid, split_axis=0, concat_axis=0, tiled=True)  43.2 us
    pallas_call x9, Pallas kernels, call(): pl.pallas_call(kernel, out_shape=out, grid_spec=pltpu.PrefetchScalarGridS...  21.4 us
    all_to_all x1, waiting for transfers between devices, body(): dm = lax.all_to_all(d_send, hid, split_axis=0, concat_axis=0, tiled=True)  16.1 us
    ppermute x1, waiting for transfers between devices, body(): do = lax.ppermute(dm, 'groups', other)  16.1 us
    unnamed x49, local copies, waits for them, and re-layouts  15.4 us
    all_to_all x1, starting transfers between devices, body(): lax.all_to_all(term_b, hid, split_axis=0, concat_axis=0, tiled=True)  8.44 us
  transfers between devices with their start and end apart: 15, of which 7 were waited for; matrix products, arithmetic and copies ran while one was open for 1% of the time, Pallas kernels for 9%

profile of v3, /device:TPU:9, one launch (start us, length us, event | category | flops | bytes accessed | tf_op | source)
XLA Modules:
  0.0 274.3 jit_solution(15952360638820226767)
XLA Ops:
  0.6 3.5 %weight_rows.1 = bf16[16,528,128]{2,1,0:T(8,128)(2,1)} custom-call(bf16[8192,128]{1,0:T(8,128)(2,1)} %gate_ref.1, bf16[8192,128]{1,0:T(8,128)(2,1)} %up_ref.1, f32[8,16,128]{2,1,0:T(8,128)} %refs_0_.1), custom_call_target="tpu_custom_call" | custom-call | tf_op jit(solution)/shard_map/weight_rows/pallas_call | solution.py:296
  4.1 6.7 %all-to-all-start.1 = ((bf16[16,528,128]{2,1,0:T(8,128)(2,1)}), bf16[16,528,128]{2,1,0:T(8,128)(2,1)S(1)}, u32[]{:S(2)}, u32[]{:S(2)}) async-start(bf16[16,528,128]{2,1,0:T(8,128)(2,1)} %weight_rows.1), calls=%async_computation.1 | async-start | bytes 4325376 | tf_op jit(solution)/shard_map/all_to_all | solution.py:309
  10.9 1.6 copy-done.6
  12.5 1.0 token_columns.1
  13.5 1.4 copy-done
  15.0 43.2 %all-to-all-done.1.wm_ref.refs_4_.refs_5_ = bf16[16,528,128]{2,1,0:T(8,128)(2,1)S(1)} async-done(((bf16[16,528,128]{2,1,0:T(8,128)(2,1)}), bf16[16,528,128]{2,1,0:T(8,128)(2,1)S(1)}, u32[]{:S(2)}, u32[]{:S(2)}) %all-to-all-start.1) | async-done | bytes 2162720 | tf_op jit(solution)/shard_map/all_to_all | solution.py:309
  58.1 6.4 %all-to-all-start = ((bf16[16,144,512]{2,1,0:T(8,128)(2,1)}), bf16[16,144,512]{2,1,0:T(8,128)(2,1)}, u32[]{:S(2)}, u32[]{:S(2)}) async-start(bf16[16,144,512]{2,1,0:T(8,128)(2,1)} %copy-done), calls=%async_computation | async-start | bytes 4718592 | tf_op jit(solution)/shard_map/all_to_all | solution.py:322
  64.6 1.2 collective-permute-start
  65.8 1.6 copy-done.7
  67.4 3.5 %down_columns.1 = bf16[16,128,256]{2,1,0:T(8,128)(2,1)} custom-call(s32[3]{0:T(128)S(1)} %pad_add_fusion.ids, bf16[128,8192]{1,0:T(8,128)(2,1)S(1)} %copy-done.7), custom_call_target="tpu_custom_call" | custom-call | bytes 3145728 | tf_op jit(solution)/shard_map/down_columns/pallas_call | solution.py:28
  70.9 45.0 %all-to-all-done.refs_0_ = bf16[16,144,512]{2,1,0:T(8,128)(2,1)} async-done(((bf16[16,144,512]{2,1,0:T(8,128)(2,1)}), bf16[16,144,512]{2,1,0:T(8,128)(2,1)}, u32[]{:S(2)}, u32[]{:S(2)}) %all-to-all-start) | async-done | bytes 2359328 | tf_op jit(solution)/shard_map/all_to_all | solution.py:322
  115.9 6.7 %all-to-all-start.2 = ((bf16[16,128,256]{2,1,0:T(8,128)(2,1)}), bf16[16,128,256]{2,1,0:T(8,128)(2,1)S(1)}, u32[]{:S(2)}, u32[]{:S(2)}) async-start(bf16[16,128,256]{2,1,0:T(8,128)(2,1)} %down_columns.1), calls=%async_computation.2 | async-start | bytes 2097152 | tf_op jit(solution)/shard_map/all_to_all | solution.py:335
  122.7 3.5 %gate_up_partial.3 = bf16[8,2,128,256]{3,2,1,0:T(8,128)(2,1)S(1)} custom-call(s32[3]{0:T(128)S(1)} %pad_add_fusion.ids, s32[16,2]{1,0:T(8,128)S(1)} %copy.25.active, bf16[8,2,144,512]{3,2,1,0:T(8,128)(2,1)} %bitcast.3.x_ref, bf16[16,528,128]{2,1,0:T(8,128)(2,1)S(1)} %all-to-all-done.1.wm_ref.refs_4_.refs_5_, bf16[16,528,128]{2,1,0:T(8,128)(2,1)} %collective-permute-done.wo_ref), custom_call_target="tpu_custom_call" | custom-call | bytes 4096 | tf_op jit(solution)/shard_map/gate_up_partial/pallas_call | solution.py:28
  126.2 0.4 collective-permute-start.1
  126.6 3.5 %gate_up_partial.2 = bf16[8,2,128,256]{3,2,1,0:T(8,128)(2,1)S(1)} custom-call(s32[3]{0:T(128)S(1)} %pad_add_fusion.ids, s32[16,2]{1,0:T(8,128)S(1)} %copy.25.active, bf16[8,2,144,512]{3,2,1,0:T(8,128)(2,1)} %bitcast.3.x_ref, bf16[16,528,128]{2,1,0:T(8,128)(2,1)S(1)} %all-to-all-done.1.wm_ref.refs_4_.refs_5_, bf16[16,528,128]{2,1,0:T(8,128)(2,1)} %collective-permute-done.wo_ref), custom_call_target="tpu_custom_call" | custom-call | bytes 4096 | tf_op jit(solution)/shard_map/gate_up_partial/pallas_call | solution.py:28
  130.1 1.3 add_convert_fusion
  131.4 16.1 %all-to-all-done.2.refs_4_ = bf16[16,128,256]{2,1,0:T(8,128)(2,1)S(1)} async-done(((bf16[16,128,256]{2,1,0:T(8,128)(2,1)}), bf16[16,128,256]{2,1,0:T(8,128)(2,1)S(1)}, u32[]{:S(2)}, u32[]{:S(2)}) %all-to-all-start.2) | async-done | bytes 1048608 | tf_op jit(solution)/shard_map/all_to_all | solution.py:335
  147.5 1.0 copy-done.3
  148.4 4.5 %all-to-all-start.3 = ((bf16[8,2,128,256]{3,2,1,0:T(8,128)(2,1)}), bf16[8,2,128,256]{3,2,1,0:T(8,128)(2,1)S(1)}, u32[]{:S(2)}, u32[]{:S(2)}) async-start(bf16[8,2,128,256]{3,2,1,0:T(8,128)(2,1)} %add_convert_fusion), calls=%async_computation.3 | async-start | bytes 2097152 | tf_op jit(solution)/shard_map/all_to_all | solution.py:343
  153.0 1.2 collective-permute-start.2
  154.2 1.6 copy-done.1
  155.8 0.9 copy-done.8
  156.8 0.7 copy-done.12
  157.5 0.7 copy-done.19
  158.1 0.7 copy-done.22
  158.8 2.3 side_rows.1.side_ref
  161.1 16.1 %collective-permute-done.2.refs_5_ = bf16[16,128,256]{2,1,0:T(8,128)(2,1)S(1)} collective-permute-done((bf16[16,128,256]{2,1,0:T(8,128)(2,1)}, bf16[16,128,256]{2,1,0:T(8,128)(2,1)S(1)}, u32[]{:S(2)}, u32[]{:S(2)}) %collective-permute-start.2) | collective-permute-done | bytes 1048608 | tf_op jit(solution)/shard_map/ppermute | solution.py:345
  177.1 1.0 copy-done.9
  178.1 0.7 copy-done.20
  178.8 0.8 hidden_values.1.z_ref
  179.6 2.1 collective-permute-start.3
  182.0 0.3 collective-permute-start.5
  182.3 1.6 copy-done.2
  183.9 3.9 %output_terms.1 = bf16[16,16,512]{2,1,0:T(8,128)(2,1)} custom-call(s32[3]{0:T(128)S(1)} %pad_add_fusion.ids, bf16[304,128]{1,0:T(8,128)(2,1)S(1)} %hidden_values.1.z_ref, bf16[128,8192]{1,0:T(8,128)(2,1)S(1)} %copy-done.2), custom_call_target="tpu_custom_call" | custom-call | bytes 2437120 | tf_op jit(solution)/shard_map/output_terms/pallas_call | solution.py:28
  187.8 1.2 collective-permute-start.6
  189.1 8.4 %all-to-all-start.5 = ((bf16[16,16,512]{2,1,0:T(8,128)(2,1)}), bf16[16,16,512]{2,1,0:T(8,128)(2,1)S(1)}, u32[]{:S(2)}, u32[]{:S(2)}) async-start(bf16[16,16,512]{2,1,0:T(8,128)(2,1)} %output_terms.1), calls=%async_computation.5 | async-start | bytes 524288 | tf_op jit(solution)/shard_map/all_to_all | solution.py:408
  197.5 0.4 collective-permute-start.7
  198.0 1.1 collective-permute-done.7.refs_2_.refs_4_.refs_5_
  199.1 0.4 collective-permute-done.8.refs_3_.refs_6_.refs_7_
  199.5 1.2 copy-done.10
  200.8 0.7 copy-done.13
  201.5 2.8 %output_columns.1 = bf16[16,128,512]{2,1,0:T(8,128)(2,1)} custom-call(s32[3]{0:T(128)S(1)} %pad_add_fusion.ids, s32[16,2]{1,0:T(8,128)S(1)} %copy-done.13, bf16[4,304,128]{2,1,0:T(8,128)(2,1)S(1)} %pad_maximum_fusion.refs_0_.refs_1_, bf16[4,304,128]{2,1,0:T(8,128)(2,1)S(1)} %collective-permute-done.6.refs_1_.refs_2_.refs_3_, ...), custom_call_target="tpu_custom_call" | custom-call | tf_op jit(solution)/shard_map/output_columns/pallas_call | solution.py:425
  204.2 1.9 all-to-all-done.5.refs_8_
  206.2 5.7 %all-to-all-start.4 = ((bf16[16,128,512]{2,1,0:T(8,128)(2,1)}), bf16[16,128,512]{2,1,0:T(8,128)(2,1)}, u32[]{:S(2)}, u32[]{:S(2)}) async-start(bf16[16,128,512]{2,1,0:T(8,128)(2,1)} %output_columns.1), calls=%async_computation.4 | async-start | bytes 4194304 | tf_op jit(solution)/shard_map/all_to_all | solution.py:443
  211.9 1.2 gradients.1
  213.1 56.8 %all-gather = f32[128,128]{1,0:T(8,128)S(1)} all-gather(f32[8,128]{1,0:T(8,128)S(1)} %get-tuple-element.32), channel_id=2, replica_groups=mesh['groups'=2,'chip'=8,'core'=2] {'chip','core'}, dimensions={0}, use_global_device_ids=true | all-gather | bytes 69632 | tf_op jit(solution)/shard_map/all_gather | solution.py:486
  269.9 1.8 adamw.1
  271.7 2.6 join_columns.1
  (48 shorter events, 0.8 us)
Async XLA Ops:
  4.1 6.8 %copy-start.5 = (f32[8,16,512]{2,1,0:T(8,128)S(1)}, f32[8,16,512]{2,1,0:T(8,128)}, u32[]{:S(2)}) copy-start(f32[8,16,512]{2,1,0:T(8,128)} %refs_4_.1) | copy-start | bytes 786436
  4.1 54.0 %all-to-all-start.1 = ((bf16[16,528,128]{2,1,0:T(8,128)(2,1)}), bf16[16,528,128]{2,1,0:T(8,128)(2,1)S(1)}, u32[]{:S(2)}, u32[]{:S(2)}) async-start(bf16[16,528,128]{2,1,0:T(8,128)(2,1)} %weight_rows.1), calls=%async_computation.1 | async-start | bytes 4325376 | tf_op jit(solution)/shard_map/all_to_all | solution.py:309
  10.9 1.6 copy-start.6
  13.5 1.4 copy-start
  58.1 57.8 %all-to-all-start = ((bf16[16,144,512]{2,1,0:T(8,128)(2,1)}), bf16[16,144,512]{2,1,0:T(8,128)(2,1)}, u32[]{:S(2)}, u32[]{:S(2)}) async-start(bf16[16,144,512]{2,1,0:T(8,128)(2,1)} %copy-done), calls=%async_computation | async-start | bytes 4718592 | tf_op jit(solution)/shard_map/all_to_all | solution.py:322
  64.6 58.1 %collective-permute-start = (bf16[16,528,128]{2,1,0:T(8,128)(2,1)S(1)}, bf16[16,528,128]{2,1,0:T(8,128)(2,1)}, u32[]{:S(2)}, u32[]{:S(2)}) collective-permute-start(bf16[16,528,128]{2,1,0:T(8,128)(2,1)S(1)} %all-to-all-done.1.wm_ref.refs_4_.refs_5_), channel_id=1, source_target_pairs={{0,16},{16,0},{1,17},{17,1},{2,18},{18,2},{3,19},{19,3},{4,20},{20... | collective-permute-start | bytes 6488072 | tf_op jit(solution)/shard_map/ppermute | solution.py:310
  65.8 1.6 copy-start.7
  67.4 55.2 %copy-start.23 = (s32[16,2]{0,1:T(2,128)S(1)}, s32[16,2]{0,1:T(2,128)}, u32[]{:S(2)}) copy-start(s32[16,2]{0,1:T(2,128)} %param.26) | copy-start | bytes 388
  115.9 31.5 %all-to-all-start.2 = ((bf16[16,128,256]{2,1,0:T(8,128)(2,1)}), bf16[16,128,256]{2,1,0:T(8,128)(2,1)S(1)}, u32[]{:S(2)}, u32[]{:S(2)}) async-start(bf16[16,128,256]{2,1,0:T(8,128)(2,1)} %down_columns.1), calls=%async_computation.2 | async-start | bytes 2097152 | tf_op jit(solution)/shard_map/all_to_all | solution.py:335
  122.7 3.9 %copy-start.11 = (s32[16,2]{1,0:T(8,128)}, s32[16,2]{1,0:T(8,128)S(1)}, u32[]{:S(2)}) copy-start(s32[16,2]{1,0:T(8,128)S(1)} %copy.25.active) | copy-start | bytes 388
  126.2 3.9 %collective-permute-start.1 = (bf16[8,2,128,256]{3,2,1,0:T(8,128)(2,1)S(1)}, bf16[8,2,128,256]{3,2,1,0:T(8,128)(2,1)S(1)}, u32[]{:S(2)}, u32[]{:S(2)}) collective-permute-start(bf16[8,2,128,256]{3,2,1,0:T(8,128)(2,1)S(1)} %gate_up_partial.3), channel_id=1, source_target_pairs={{0,1},{1,0},{2,3},{3,2},{4,5},{5,4},{6,7},{7,6},{8,9},{9,8},{10,11... | collective-permute-start | bytes 3145736 | tf_op jit(solution)/shard_map/ppermute | solution.py:338
  147.5 1.0 copy-start.3
  148.4 29.7 %all-to-all-start.3 = ((bf16[8,2,128,256]{3,2,1,0:T(8,128)(2,1)}), bf16[8,2,128,256]{3,2,1,0:T(8,128)(2,1)S(1)}, u32[]{:S(2)}, u32[]{:S(2)}) async-start(bf16[8,2,128,256]{3,2,1,0:T(8,128)(2,1)} %add_convert_fusion), calls=%async_computation.3 | async-start | bytes 2097152 | tf_op jit(solution)/shard_map/all_to_all | solution.py:343
  153.0 24.1 %collective-permute-start.2 = (bf16[16,128,256]{2,1,0:T(8,128)(2,1)}, bf16[16,128,256]{2,1,0:T(8,128)(2,1)S(1)}, u32[]{:S(2)}, u32[]{:S(2)}) collective-permute-start(bf16[16,128,256]{2,1,0:T(8,128)(2,1)} %copy-done.3), channel_id=1, source_target_pairs={{0,16},{16,0},{1,17},{17,1},{2,18},{18,2},{3,19},{19,3},{4,20},{20... | collective-permute-start | bytes 3145736 | tf_op jit(solution)/shard_map/ppermute | solution.py:345
  154.2 1.6 copy-start.1
  155.8 0.9 copy-start.8
  156.8 0.7 copy-start.12
  157.5 0.7 copy-start.19
  158.1 0.7 copy-start.22
  177.1 1.0 copy-start.9
  178.1 0.7 copy-start.20
  178.8 20.8 %copy-start.4 = (bf16[16,128,256]{2,1,0:T(8,128)(2,1)S(1)}, bf16[16,128,256]{2,1,0:T(8,128)(2,1)}, u32[]{:S(2)}) copy-start(bf16[16,128,256]{2,1,0:T(8,128)(2,1)} %copy-done.3) | copy-start | bytes 3145732
  179.6 8.1 %collective-permute-start.3 = (bf16[304,128]{1,0:T(8,128)(2,1)S(1)}, bf16[304,128]{1,0:T(8,128)(2,1)S(1)}, u32[]{:S(2)}, u32[]{:S(2)}) collective-permute-start(bf16[304,128]{1,0:T(8,128)(2,1)S(1)} %hidden_values.1.z_ref), channel_id=1, source_target_pairs={{0,8},{2,10},{4,12},{6,14},{8,0},{10,2},{12,4},{14,6},{1,9},{3,11}... | collective-permute-start | bytes 233480 | tf_op jit(solution)/shard_map/ppermute | solution.py:405
  181.7 6.0 %collective-permute-start.4 = (bf16[304,128]{1,0:T(8,128)(2,1)S(1)}, bf16[304,128]{1,0:T(8,128)(2,1)S(1)}, u32[]{:S(2)}, u32[]{:S(2)}) collective-permute-start(bf16[304,128]{1,0:T(8,128)(2,1)S(1)} %hidden_values.1.z_ref), channel_id=1, source_target_pairs={{0,4},{2,6},{4,0},{6,2},{8,12},{10,14},{12,8},{14,10},{1,5},{3,7},... | collective-permute-start | bytes 233480 | tf_op jit(solution)/shard_map/ppermute | solution.py:405
  182.0 5.8 %collective-permute-start.5 = (bf16[304,128]{1,0:T(8,128)(2,1)S(1)}, bf16[304,128]{1,0:T(8,128)(2,1)S(1)}, u32[]{:S(2)}, u32[]{:S(2)}) collective-permute-start(bf16[304,128]{1,0:T(8,128)(2,1)S(1)} %hidden_values.1.z_ref), channel_id=1, source_target_pairs={{0,12},{2,14},{4,8},{6,10},{8,4},{10,6},{12,0},{14,2},{1,13},{3,15... | collective-permute-start | bytes 233480 | tf_op jit(solution)/shard_map/ppermute | solution.py:405
  182.3 1.6 copy-start.2
  187.8 10.0 %collective-permute-start.6 = (bf16[4,304,128]{2,1,0:T(8,128)(2,1)S(1)}, bf16[4,304,128]{2,1,0:T(8,128)(2,1)S(1)}, u32[]{:S(2)}, u32[]{:S(2)}) collective-permute-start(bf16[4,304,128]{2,1,0:T(8,128)(2,1)S(1)} %pad_maximum_fusion.refs_0_.refs_1_), channel_id=1, source_target_pairs={{0,2},{2,0},{4,6},{6,4},{8,10},{10,8},{12,14},{14,12},{1,3},{3,1},... | collective-permute-start | bytes 933896 | tf_op jit(solution)/shard_map/ppermute | solution.py:413
  189.1 17.1 %all-to-all-start.5 = ((bf16[16,16,512]{2,1,0:T(8,128)(2,1)}), bf16[16,16,512]{2,1,0:T(8,128)(2,1)S(1)}, u32[]{:S(2)}, u32[]{:S(2)}) async-start(bf16[16,16,512]{2,1,0:T(8,128)(2,1)} %output_terms.1), calls=%async_computation.5 | async-start | bytes 524288 | tf_op jit(solution)/shard_map/all_to_all | solution.py:408
  197.5 1.6 collective-permute-start.7
  197.9 1.7 collective-permute-start.8
  199.5 1.2 copy-start.10
  200.8 0.7 copy-start.13
  204.2 7.6 %copy-start.21 = (s32[16]{0:T(128)S(1)}, s32[16]{0:T(128)}, u32[]{:S(2)}) copy-start(s32[16]{0:T(128)} %counts.5) | copy-start | bytes 196
  206.2 65.5 %all-to-all-start.4 = ((bf16[16,128,512]{2,1,0:T(8,128)(2,1)}), bf16[16,128,512]{2,1,0:T(8,128)(2,1)}, u32[]{:S(2)}, u32[]{:S(2)}) async-start(bf16[16,128,512]{2,1,0:T(8,128)(2,1)} %output_columns.1), calls=%async_computation.4 | async-start | bytes 4194304 | tf_op jit(solution)/shard_map/all_to_all | solution.py:443
  211.8 58.0 %copy-start.14 = (f32[8,16,128]{2,1,0:T(8,128)S(1)}, f32[8,16,128]{2,1,0:T(8,128)}, u32[]{:S(2)}) copy-start(f32[8,16,128]{2,1,0:T(8,128)} %refs_0_.1) | copy-start | bytes 196612
  211.8 58.0 %copy-start.15 = (f32[8,16,512]{2,1,0:T(8,128)S(1)}, f32[8,16,512]{2,1,0:T(8,128)}, u32[]{:S(2)}) copy-start(f32[8,16,512]{2,1,0:T(8,128)} %refs_5_.1) | copy-start | bytes 786436
  211.9 58.0 %copy-start.16 = (f32[8,16,512]{2,1,0:T(8,128)S(1)}, f32[8,16,512]{2,1,0:T(8,128)}, u32[]{:S(2)}) copy-start(f32[8,16,512]{2,1,0:T(8,128)} %refs_6_.3) | copy-start | bytes 786436
  211.9 58.0 %copy-start.17 = (f32[8,16,128]{2,1,0:T(8,128)S(1)}, f32[8,16,128]{2,1,0:T(8,128)}, u32[]{:S(2)}) copy-start(f32[8,16,128]{2,1,0:T(8,128)} %refs_1_.3) | copy-start | bytes 196612
  211.9 58.0 %copy-start.18 = (f32[8,16,128]{2,1,0:T(8,128)S(1)}, f32[8,16,128]{2,1,0:T(8,128)}, u32[]{:S(2)}) copy-start(f32[8,16,128]{2,1,0:T(8,128)} %refs_2_.3) | copy-start | bytes 196612

commit v4 on v3

--- a/solution.py
+++ b/solution.py
@@ -98,33 +98,59 @@
             o_ref[s] = d_ref[:, base + half : base + chunk]
 
 
-def partial_kernel(ids, active, x_ref, wm_ref, wo_ref, o_ref, *, block, chunk, picks, away):
-    side = jnp.bitwise_xor(ids[1], away)
-    for s in range(paired_step):
-        x = x_ref[s, 0, :block, :]
-        for k in range(picks):
-            j = active[2 * (paired_step * pl.program_id(0) + s) + side, k]
-            w = jnp.concatenate([wm_ref[j, :chunk, :], wo_ref[j, :chunk, :]], axis=1)
-            o_ref[s, k] = dot(x, w).astype(o_ref.dtype)
-
-
-def partial_products(ids, active, xb, wm, wo, block, chunk, away):
+def partial_kernel(ids, active, x_ref, wm_ref, wo_ref, *o_refs, block, chunk, picks, first, sides):
+    chip = ids[2] // 2
+    for i in range(o_refs[0].shape[0]):
+        for o_ref, side in zip(o_refs, sides):
+            t = 2 * jnp.bitwise_xor(chip, first + i) + jnp.bitwise_xor(ids[1], side)
+            x = x_ref[t, :block, :]
+            for k in range(picks):
+                j = active[t, k]
+                w = jnp.concatenate([wm_ref[j, :chunk, :], wo_ref[j, :chunk, :]], axis=1)
+                o_ref[i, k] = dot(x, w).astype(o_ref.dtype)
+
+
+def partial_products(ids, active, xb, wm, wo, block, chunk, first, count, sides):
     n, picks = active.shape
-    shape = (n // 2, picks, block, 2 * block)
-    kind = bf16
-    token = lambda i, ids, act: (i, jnp.bitwise_xor(ids[1], away), 0, 0)
-    xp = xb.reshape(n // 2, 2, *xb.shape[1:])
+    out = jax.ShapeDtypeStruct((count, picks, block, 2 * block), bf16)
     return call(
-        functools.partial(partial_kernel, block=block, chunk=chunk, picks=picks, away=away),
+        functools.partial(
+            partial_kernel, block=block, chunk=chunk, picks=picks, first=first, sides=sides
+        ),
         "gate_up_partial",
-        jax.ShapeDtypeStruct(shape, kind),
-        (n // 2 // paired_step,),
-        [pl.BlockSpec((paired_step, 1) + xb.shape[1:], token), whole(wm), whole(wo)],
-        pl.BlockSpec((paired_step,) + shape[1:], lambda i, *_: (i, 0, 0, 0)),
+        (out,) * len(sides),
+        (1,),
+        [pl.BlockSpec((n, block, chunk), lambda i, *_: (0, 0, 0)), whole(wm), whole(wo)],
+        [whole(out)] * len(sides),
         (ids, active),
-        (xp, wm, wo),
-        moved=4096,
-    )
+        (xb, wm, wo),
+        flops=count * len(sides) * picks * 4 * block * block * chunk,
+    )
+
+
+def pair_sum_kernel(kept_ref, got_ref, *refs):
+    o_refs, (held, stores) = refs[:-2], refs[-2:]
+    copies = []
+    for i, o_ref in enumerate(o_refs):
+        held[i] = (kept_ref[i].astype(f32) + got_ref[i].astype(f32)).astype(bf16)
+        copies.append(pltpu.make_async_copy(held.at[i], o_ref, stores.at[i]))
+        copies[i].start()
+    for copy in copies:
+        copy.wait()
+
+
+def pair_sums(kept, got):
+    count = kept.shape[0]
+    vmem = pl.BlockSpec(memory_space=pltpu.VMEM)
+    return pl.pallas_call(
+        pair_sum_kernel,
+        out_shape=(jax.ShapeDtypeStruct(kept.shape[1:], bf16),) * count,
+        in_specs=[vmem, vmem],
+        out_specs=(pl.BlockSpec(memory_space=pltpu.HBM),) * count,
+        scratch_shapes=[pltpu.VMEM(kept.shape, bf16), pltpu.SemaphoreType.DMA((count,))],
+        compiler_params=pltpu.CompilerParams(vmem_limit_bytes=vmem_limit),
+        name="pair_sums",
+    )(kept, got)
 
 
 def side_rows_kernel(ids, active, counts, seeds, *refs, block, chunk, picks, rank, n):
@@ -142,8 +168,11 @@
     o_ref[base : base + rank, :] = (adapter_scale * total).astype(bf16)
 
 
-def hidden_kernel(ids, counts, r_ref, side_ref, o_ref, *, block, picks, rank):
-    total = jnp.sum(r_ref[...].astype(f32), axis=0)
+def hidden_kernel(ids, counts, *refs, block, picks, rank):
+    part_refs, side_ref, o_ref = refs[:-2], refs[-2], refs[-1]
+    total = part_refs[0][...].astype(f32)
+    for part_ref in part_refs[1:]:
+        total = total + part_ref[...].astype(f32)
     swap = ids[0] != 0
     count = counts[ids[2]]
     low_t = jnp.zeros((rank, block), f32)
@@ -164,7 +193,7 @@
 
 
 def output_terms_kernel(ids, z_ref, dy_ref, o_ref, *, chunk, n):
-    for s in range(n // strips):
+    for s in range(n):
         part = dot(z_ref[...], dy_ref[:, s * chunk : (s + 1) * chunk])
         o_ref[s] = (adapter_scale * part).astype(bf16)
 
@@ -240,10 +269,13 @@
         sq_ref[r : r + 1, :] = jnp.full((1, sq_ref.shape[1]), square, f32)
 
 
-def adamw_kernel(ids, sq_ref, *refs, limit, runs):
-    ins, outs = refs[:8], refs[8:]
+def adamw_kernel(ids, *refs, limit, runs):
+    sq_refs, ins, outs = refs[:-14], refs[-14:-6], refs[-6:]
+    totals = sq_refs[0][...]
+    for sq_ref in sq_refs[1:]:
+        totals = totals + sq_ref[...]
     for r in range(runs):
-        factor = jnp.minimum(1.0, limit / jnp.sqrt(sq_ref[r : r + 1, :1]))
+        factor = jnp.minimum(1.0, limit / jnp.sqrt(totals[r : r + 1, :1]))
         for side in range(2):
             p_ref, m_ref, v_ref, g_ref = ins[4 * side : 4 * side + 4]
             grad = g_ref[r] * factor
@@ -334,14 +366,16 @@
     d_send, xb = lax.optimization_barrier((d_send, xb))
     dm = lax.all_to_all(d_send, hid, split_axis=0, concat_axis=0, tiled=True)
 
-    sent = partial_products(ids, active, xb, wm, wo, block, chunk, 1)
+    products = functools.partial(partial_products, ids, active, xb, wm, wo, block, chunk)
+    far = chips // 2
+    (sent,) = products(0, chips, (1,))
     got = lax.ppermute(sent, "core", other)
-    kept = partial_products(ids, active, xb, wm, wo, block, chunk, 0)
-    paired = (kept.astype(f32) + got.astype(f32)).astype(bf16)
-    paired, dm = lax.optimization_barrier((paired, dm))
-    far = chips // 2
-    summed = lax.all_to_all(paired, "chip", split_axis=0, concat_axis=0, tiled=True)
-
+    (kept,) = products(0, chips, (0,))
+    paired = pair_sums(kept, got)
+    summed = [paired[0]] + [
+        lax.ppermute(paired[c], "chip", across(c)) for c in range(1, chips)
+    ]
+    dm, _ = lax.optimization_barrier((dm, summed[1]))
     do = lax.ppermute(dm, "groups", other)
 
     rows = picks * block + rank * (1 + picks)
@@ -374,28 +408,27 @@
         (ids, active, counts, seeds),
         (xb, cotangent) + (dropout_tiles,) * picks + (wm,) * picks,
     )
-    summed, do = lax.optimization_barrier((summed, do))
     held = call(
         functools.partial(hidden_kernel, block=block, picks=picks, rank=rank),
         "hidden_values",
         jax.ShapeDtypeStruct((rows, block), bf16),
         (1,),
-        [whole(summed), whole(side)],
+        [whole(part) for part in summed] + [whole(side)],
         pl.BlockSpec((rows, block), lambda i, *_: (0, 0)),
         (ids, counts),
-        (summed, side),
+        (*summed, side),
     )
 
     term_b = call(
         functools.partial(output_terms_kernel, **sizes),
         "output_terms",
         jax.ShapeDtypeStruct((n, rank, chunk), bf16),
-        (strips,),
+        (1,),
         [
             pl.BlockSpec((rank, block), lambda i, ids: (picks * block // rank, 0)),
-            pl.BlockSpec((block, strip), lambda i, ids: (0, i)),
+            whole(cotangent),
         ],
-        pl.BlockSpec((per, rank, chunk), lambda i, ids: (i, 0, 0)),
+        pl.BlockSpec((n, rank, chunk), lambda i, ids: (0, 0, 0)),
         (ids,),
         (held, cotangent),
     )
@@ -483,18 +516,19 @@
         (ids, active, counts),
         tuple(a for a in gathered for _ in range(picks)) + (parts_b,),
     )
-    totals = jnp.sum(lax.all_gather(squares, hid, axis=0), axis=0)
+    squares = squares + lax.ppermute(squares, "core", other)
+    totals = [squares] + [lax.ppermute(squares, "chip", across(c)) for c in range(1, chips)]
     limit = math.sqrt(rank * (n * block + model))
     updated = call(
         functools.partial(adamw_kernel, limit=limit, runs=runs),
         "adamw",
         (maps_a,) * 3 + (maps_b,) * 3,
         (1,),
-        [whole(lanes)] + [whole(maps_a)] * 4 + [whole(maps_b)] * 4,
+        [whole(lanes)] * chips + [whole(maps_a)] * 4 + [whole(maps_b)] * 4,
         [whole(maps_a)] * 3 + [whole(maps_b)] * 3,
         (ids,),
         (
-            totals,
+            *totals,
             adapter_input_maps,
             first_moment_input,
             second_moment_input,

time: 275 us -> 261 us (0.949)
  blocking collectives: 56.8 us -> 0 us
  waiting for transfers between devices: 124 us -> 157 us
  starting transfers between devices: 45.8 us -> 59.2 us
  local copies, waits for them, and re-layouts: 15.4 us -> 8.64 us
    all_gather x1 -> x0, blocking collectives: 56.8 us -> none  [body(): totals = jnp.sum(lax.all_gather(squares, hid, axis=0), axis=0)]
    ppermute x0 -> x15, waiting for transfers between devices: none -> 51.1 us  [the longest x7 35.7 us: body(): lax.ppermute(squares, 'chip', across(c))]
    ppermute x0 -> x15, starting transfers between devices: none -> 18.2 us  [the longest x7 10.4 us: body(): lax.ppermute(squares, 'chip', across(c))]
    ppermute x1, waiting for transfers between devices: 16.1 us -> 0.01 us  [body(): do = lax.ppermute(dm, 'groups', other)]
    unnamed x49 -> x43, local copies, waits for them, and re-layouts: 15.4 us -> 8.64 us
    all_to_all x1 -> x0, starting transfers between devices: 4.54 us -> none  [body(): lax.all_to_all(paired, 'chip', split_axis=0, concat_axis=0, tiled=True)]
    all_to_all x1, waiting for transfers between devices: 16.1 us -> 12.7 us  [body(): dm = lax.all_to_all(d_send, hid, split_axis=0, concat_axis=0, tiled=True)]
  transfers between devices with their start and end apart: 15 -> 29, of which waited for: 7 -> 19; matrix products, arithmetic and copies ran while one was open for 1% -> 0% of each run, Pallas kernels for 9% -> 10%
where the time goes in v4:
time: 261 us; the launch traced here: 258 us
  waiting for transfers between devices  157 us (60%)
  starting transfers between devices  59.2 us (23%)
  Pallas kernels  31.8 us (12%)
  local copies, waits for them, and re-layouts  8.64 us (3%)
    all_to_all x1, waiting for transfers between devices, body(): xb = lax.all_to_all(x_send, hid, split_axis=0, concat_axis=0, tiled=True)  45 us
    all_to_all x1, waiting for transfers between devices, body(): wm = lax.all_to_all(w_send, hid, split_axis=0, concat_axis=0, tiled=True)  43.1 us
    ppermute x7, waiting for transfers between devices, body(): lax.ppermute(squares, 'chip', across(c))  35.7 us
    pallas_call x9, Pallas kernels, call(): pl.pallas_call(kernel, out_shape=out, grid_spec=pltpu.PrefetchScalarGridS...  20.7 us
    ppermute x7, waiting for transfers between devices, body(): lax.ppermute(paired[c], 'chip', across(c))  14.6 us
    all_to_all x1, waiting for transfers between devices, body(): dm = lax.all_to_all(d_send, hid, split_axis=0, concat_axis=0, tiled=True)  12.7 us
    ppermute x7, starting transfers between devices, body(): lax.ppermute(squares, 'chip', across(c))  10.4 us
    unnamed x43, local copies, waits for them, and re-layouts  8.64 us
  transfers between devices with their start and end apart: 29, of which 19 were waited for; matrix products, arithmetic and copies ran while one was open for 0% of the time, Pallas kernels for 10%

profile of v4, /device:TPU:9, one launch (start us, length us, event | category | flops | bytes accessed | tf_op | source)
XLA Modules:
  0.0 257.7 jit_solution(17198894721042842082)
XLA Ops:
  0.6 3.5 %weight_rows.1 = bf16[16,528,128]{2,1,0:T(8,128)(2,1)} custom-call(bf16[8192,128]{1,0:T(8,128)(2,1)} %gate_ref.1, bf16[8192,128]{1,0:T(8,128)(2,1)} %up_ref.1, f32[8,16,128]{2,1,0:T(8,128)} %refs_8_.1), custom_call_target="tpu_custom_call" | custom-call | tf_op jit(solution)/shard_map/weight_rows/pallas_call | solution.py:328
  4.1 6.7 %all-to-all-start.1 = ((bf16[16,528,128]{2,1,0:T(8,128)(2,1)}), bf16[16,528,128]{2,1,0:T(8,128)(2,1)S(1)}, u32[]{:S(2)}, u32[]{:S(2)}) async-start(bf16[16,528,128]{2,1,0:T(8,128)(2,1)} %weight_rows.1), calls=%async_computation.1 | async-start | bytes 4325376 | tf_op jit(solution)/shard_map/all_to_all | solution.py:341
  10.9 1.6 copy-done.4
  13.5 1.5 copy-done
  15.0 43.1 %all-to-all-done.1.wm_ref.refs_4_.refs_5_ = bf16[16,528,128]{2,1,0:T(8,128)(2,1)S(1)} async-done(((bf16[16,528,128]{2,1,0:T(8,128)(2,1)}), bf16[16,528,128]{2,1,0:T(8,128)(2,1)S(1)}, u32[]{:S(2)}, u32[]{:S(2)}) %all-to-all-start.1) | async-done | bytes 2162720 | tf_op jit(solution)/shard_map/all_to_all | solution.py:341
  58.1 6.4 %all-to-all-start = ((bf16[16,144,512]{2,1,0:T(8,128)(2,1)}), bf16[16,144,512]{2,1,0:T(8,128)(2,1)}, u32[]{:S(2)}, u32[]{:S(2)}) async-start(bf16[16,144,512]{2,1,0:T(8,128)(2,1)} %copy-done), calls=%async_computation | async-start | bytes 4718592 | tf_op jit(solution)/shard_map/all_to_all | solution.py:354
  64.6 1.2 collective-permute-start
  65.8 1.6 copy-done.5
  67.4 3.5 %down_columns.1 = bf16[16,128,256]{2,1,0:T(8,128)(2,1)} custom-call(s32[3]{0:T(128)S(1)} %pad_add_fusion.ids, bf16[128,8192]{1,0:T(8,128)(2,1)S(1)} %copy-done.5), custom_call_target="tpu_custom_call" | custom-call | bytes 3145728 | tf_op jit(solution)/shard_map/down_columns/pallas_call | solution.py:28
  70.9 45.0 %all-to-all-done.x_ref.refs_0_ = bf16[16,144,512]{2,1,0:T(8,128)(2,1)} async-done(((bf16[16,144,512]{2,1,0:T(8,128)(2,1)}), bf16[16,144,512]{2,1,0:T(8,128)(2,1)}, u32[]{:S(2)}, u32[]{:S(2)}) %all-to-all-start) | async-done | bytes 2359328 | tf_op jit(solution)/shard_map/all_to_all | solution.py:354
  115.9 6.7 %all-to-all-start.2 = ((bf16[16,128,256]{2,1,0:T(8,128)(2,1)}), bf16[16,128,256]{2,1,0:T(8,128)(2,1)S(1)}, u32[]{:S(2)}, u32[]{:S(2)}) async-start(bf16[16,128,256]{2,1,0:T(8,128)(2,1)} %down_columns.1), calls=%async_computation.2 | async-start | bytes 2097152 | tf_op jit(solution)/shard_map/all_to_all | solution.py:367
  122.7 3.7 %gate_up_partial.3 = bf16[8,2,128,256]{3,2,1,0:T(8,128)(2,1)S(1)} custom-call(s32[3]{0:T(128)S(1)} %pad_add_fusion.ids, s32[16,2]{1,0:T(8,128)S(1)} %copy.25.active, bf16[16,144,512]{2,1,0:T(8,128)(2,1)} %all-to-all-done.x_ref.refs_0_, bf16[16,528,128]{2,1,0:T(8,128)(2,1)S(1)} %all-to-all-done.1.wm_ref.refs_4_.refs_5_, ...), custom_call_target="tpu_custom_call" | custom-call | flops 536870912 | bytes 7733248 | tf_op jit(solution)/shard_map/gate_up_partial/pallas_call | solution.py:28
  126.8 3.7 %gate_up_partial.2.kept_ref = bf16[8,2,128,256]{3,2,1,0:T(8,128)(2,1)S(1)} custom-call(s32[3]{0:T(128)S(1)} %pad_add_fusion.ids, s32[16,2]{1,0:T(8,128)S(1)} %copy.25.active, bf16[16,144,512]{2,1,0:T(8,128)(2,1)} %all-to-all-done.x_ref.refs_0_, bf16[16,528,128]{2,1,0:T(8,128)(2,1)S(1)} %all-to-all-done.1.wm_ref.refs_4_.refs_5_, ...), custom_call_target="tpu_custom_call" | custom-call | flops 536870912 | bytes 7733248 | tf_op jit(solution)/shard_map/gate_up_partial/pallas_call | solution.py:28
  130.6 1.2 pair_sums.1
  133.1 1.2 collective-permute-start.2
  134.6 1.2 collective-permute-start.4
  135.8 12.7 %all-to-all-done.2.refs_4_ = bf16[16,128,256]{2,1,0:T(8,128)(2,1)S(1)} async-done(((bf16[16,128,256]{2,1,0:T(8,128)(2,1)}), bf16[16,128,256]{2,1,0:T(8,128)(2,1)S(1)}, u32[]{:S(2)}, u32[]{:S(2)}) %all-to-all-start.2) | async-done | bytes 1048608 | tf_op jit(solution)/shard_map/all_to_all | solution.py:367
  148.5 1.2 collective-permute-start.15
  149.7 2.8 %collective-permute-start.6 = (bf16[2,128,256]{2,1,0:T(8,128)(2,1)}, bf16[2,128,256]{2,1,0:T(8,128)(2,1)S(1)}, u32[]{:S(2)}, u32[]{:S(2)}) collective-permute-start(bf16[2,128,256]{2,1,0:T(8,128)(2,1)} %copy-done.18), channel_id=1, source_target_pairs={{0,10},{2,8},{4,14},{6,12},{8,2},{10,0},{12,6},{14,4},{1,11},{3,9}... | collective-permute-start | bytes 393224 | tf_op jit(solution)/shard_map/ppermute | solution.py:376
  152.5 1.9 collective-permute-start.8
  154.5 1.6 copy-done.1
  157.0 2.3 side_rows.1.refs_8_
  159.3 5.2 %collective-permute-done.5.refs_4_ = bf16[2,128,256]{2,1,0:T(8,128)(2,1)S(1)} collective-permute-done((bf16[2,128,256]{2,1,0:T(8,128)(2,1)}, bf16[2,128,256]{2,1,0:T(8,128)(2,1)S(1)}, u32[]{:S(2)}, u32[]{:S(2)}) %collective-permute-start.5) | collective-permute-done | bytes 131104 | tf_op jit(solution)/shard_map/ppermute | solution.py:376
  164.5 2.8 %collective-permute-done.6.refs_5_ = bf16[2,128,256]{2,1,0:T(8,128)(2,1)S(1)} collective-permute-done((bf16[2,128,256]{2,1,0:T(8,128)(2,1)}, bf16[2,128,256]{2,1,0:T(8,128)(2,1)S(1)}, u32[]{:S(2)}, u32[]{:S(2)}) %collective-permute-start.6) | collective-permute-done | bytes 131104 | tf_op jit(solution)/shard_map/ppermute | solution.py:376
  167.3 2.8 %collective-permute-done.7.refs_6_ = bf16[2,128,256]{2,1,0:T(8,128)(2,1)S(1)} collective-permute-done((bf16[2,128,256]{2,1,0:T(8,128)(2,1)}, bf16[2,128,256]{2,1,0:T(8,128)(2,1)S(1)}, u32[]{:S(2)}, u32[]{:S(2)}) %collective-permute-start.7) | collective-permute-done | bytes 131104 | tf_op jit(solution)/shard_map/ppermute | solution.py:376
  170.2 3.7 %collective-permute-done.8.refs_7_ = bf16[2,128,256]{2,1,0:T(8,128)(2,1)S(1)} collective-permute-done((bf16[2,128,256]{2,1,0:T(8,128)(2,1)}, bf16[2,128,256]{2,1,0:T(8,128)(2,1)S(1)}, u32[]{:S(2)}, u32[]{:S(2)}) %collective-permute-start.8) | collective-permute-done | bytes 131104 | tf_op jit(solution)/shard_map/ppermute | solution.py:376
  173.9 1.9 hidden_values.1.z_ref
  176.9 1.6 collective-permute-start.9
  178.5 1.6 output_terms.1
  180.3 1.1 collective-permute-done.9
  181.5 1.4 collective-permute-start.12
  182.8 7.5 %all-to-all-start.4 = ((bf16[16,16,512]{2,1,0:T(8,128)(2,1)}), bf16[16,16,512]{2,1,0:T(8,128)(2,1)S(1)}, u32[]{:S(2)}, u32[]{:S(2)}) async-start(bf16[16,16,512]{2,1,0:T(8,128)(2,1)} %output_terms.1), calls=%async_computation.4 | async-start | bytes 524288 | tf_op jit(solution)/shard_map/all_to_all | solution.py:441
  192.5 4.0 %output_columns.1 = bf16[16,128,512]{2,1,0:T(8,128)(2,1)} custom-call(s32[3]{0:T(128)S(1)} %pad_add_fusion.ids, s32[16,2]{1,0:T(8,128)S(1)} %copy.25.active, bf16[4,304,128]{2,1,0:T(8,128)(2,1)S(1)} %pad_maximum_fusion.refs_0_.refs_1_, bf16[4,304,128]{2,1,0:T(8,128)(2,1)S(1)} %collective-permute-done.12.refs_1_.refs_2_.refs_3_, ...), custom_call_target="tpu_custom_call" | custom-call | tf_op jit(solution)/shard_map/output_columns/pallas_call | solution.py:458
  196.5 2.5 all-to-all-done.4.refs_8_
  199.0 5.7 %all-to-all-start.3 = ((bf16[16,128,512]{2,1,0:T(8,128)(2,1)}), bf16[16,128,512]{2,1,0:T(8,128)(2,1)}, u32[]{:S(2)}, u32[]{:S(2)}) async-start(bf16[16,128,512]{2,1,0:T(8,128)(2,1)} %output_columns.1), calls=%async_computation.3 | async-start | bytes 4194304 | tf_op jit(solution)/shard_map/all_to_all | solution.py:476
  204.8 1.2 gradients.1
  207.2 1.2 collective-permute-start.17
  208.7 1.2 collective-permute-start.19
  209.9 2.1 collective-permute-start.20
  212.0 1.1 collective-permute-start.21
  213.1 2.2 collective-permute-done.17.refs_1_
  215.4 1.3 collective-permute-start.22
  216.6 23.4 %collective-permute-done.18.refs_2_ = f32[8,128]{1,0:T(8,128)S(1)} collective-permute-done((f32[8,128]{1,0:T(8,128)S(1)}, f32[8,128]{1,0:T(8,128)S(1)}, u32[]{:S(2)}, u32[]{:S(2)}) %collective-permute-start.18) | collective-permute-done | bytes 4128 | tf_op jit(solution)/shard_map/ppermute | solution.py:520
  240.0 3.2 %collective-permute-start.23 = (f32[8,128]{1,0:T(8,128)S(1)}, f32[8,128]{1,0:T(8,128)S(1)}, u32[]{:S(2)}, u32[]{:S(2)}) collective-permute-start(f32[8,128]{1,0:T(8,128)S(1)} %add.7.refs_0_), channel_id=1, source_target_pairs={{0,14},{2,12},{4,10},{6,8},{8,6},{10,4},{12,2},{14,0},{1,15},{3,13... | collective-permute-start | bytes 12296 | tf_op jit(solution)/shard_map/ppermute | solution.py:520
  243.2 7.3 %collective-permute-done.20.refs_4_ = f32[8,128]{1,0:T(8,128)S(1)} collective-permute-done((f32[8,128]{1,0:T(8,128)S(1)}, f32[8,128]{1,0:T(8,128)S(1)}, u32[]{:S(2)}, u32[]{:S(2)}) %collective-permute-start.20) | collective-permute-done | bytes 4128 | tf_op jit(solution)/shard_map/ppermute | solution.py:520
  250.5 1.7 collective-permute-done.22.refs_6_
  253.3 1.8 adamw.1
  255.1 2.6 join_columns.1
  (69 shorter events, 10.4 us)
Async XLA Ops:
  4.1 6.8 %copy-start.3 = (f32[8,16,512]{2,1,0:T(8,128)S(1)}, f32[8,16,512]{2,1,0:T(8,128)}, u32[]{:S(2)}) copy-start(f32[8,16,512]{2,1,0:T(8,128)} %refs_12_.1) | copy-start | bytes 786436
  4.1 54.0 %all-to-all-start.1 = ((bf16[16,528,128]{2,1,0:T(8,128)(2,1)}), bf16[16,528,128]{2,1,0:T(8,128)(2,1)S(1)}, u32[]{:S(2)}, u32[]{:S(2)}) async-start(bf16[16,528,128]{2,1,0:T(8,128)(2,1)} %weight_rows.1), calls=%async_computation.1 | async-start | bytes 4325376 | tf_op jit(solution)/shard_map/all_to_all | solution.py:341
  10.9 1.6 copy-start.4
  13.5 1.5 copy-start
  58.1 57.8 %all-to-all-start = ((bf16[16,144,512]{2,1,0:T(8,128)(2,1)}), bf16[16,144,512]{2,1,0:T(8,128)(2,1)}, u32[]{:S(2)}, u32[]{:S(2)}) async-start(bf16[16,144,512]{2,1,0:T(8,128)(2,1)} %copy-done), calls=%async_computation | async-start | bytes 4718592 | tf_op jit(solution)/shard_map/all_to_all | solution.py:354
  64.6 58.1 %collective-permute-start = (bf16[16,528,128]{2,1,0:T(8,128)(2,1)S(1)}, bf16[16,528,128]{2,1,0:T(8,128)(2,1)}, u32[]{:S(2)}, u32[]{:S(2)}) collective-permute-start(bf16[16,528,128]{2,1,0:T(8,128)(2,1)S(1)} %all-to-all-done.1.wm_ref.refs_4_.refs_5_), channel_id=1, source_target_pairs={{0,16},{16,0},{1,17},{17,1},{2,18},{18,2},{3,19},{19,3},{4,20},{20... | collective-permute-start | bytes 6488072 | tf_op jit(solution)/shard_map/ppermute | solution.py:342
  65.8 1.6 copy-start.5
  67.4 55.2 %copy-start.20 = (s32[16,2]{0,1:T(2,128)S(1)}, s32[16,2]{0,1:T(2,128)}, u32[]{:S(2)}) copy-start(s32[16,2]{0,1:T(2,128)} %param.26) | copy-start | bytes 388
  115.9 32.5 %all-to-all-start.2 = ((bf16[16,128,256]{2,1,0:T(8,128)(2,1)}), bf16[16,128,256]{2,1,0:T(8,128)(2,1)S(1)}, u32[]{:S(2)}, u32[]{:S(2)}) async-start(bf16[16,128,256]{2,1,0:T(8,128)(2,1)} %down_columns.1), calls=%async_computation.2 | async-start | bytes 2097152 | tf_op jit(solution)/shard_map/all_to_all | solution.py:367
  126.4 4.2 %collective-permute-start.1 = (bf16[8,2,128,256]{3,2,1,0:T(8,128)(2,1)S(1)}, bf16[8,2,128,256]{3,2,1,0:T(8,128)(2,1)S(1)}, u32[]{:S(2)}, u32[]{:S(2)}) collective-permute-start(bf16[8,2,128,256]{3,2,1,0:T(8,128)(2,1)S(1)} %gate_up_partial.3), channel_id=1, source_target_pairs={{0,1},{1,0},{2,3},{3,2},{4,5},{5,4},{6,7},{7,6},{8,9},{9,8},{10,11... | collective-permute-start | bytes 3145736 | tf_op jit(solution)/shard_map/ppermute | solution.py:372
  130.5 23.9 %copy-start.14 = (s32[16]{0:T(128)S(1)}, s32[16]{0:T(128)}, u32[]{:S(2)}) copy-start(s32[16]{0:T(128)} %counts.5) | copy-start | bytes 196
  130.6 23.9 %copy-start.15 = (s32[8]{0:T(128)S(1)}, s32[8]{0:T(128)}, u32[]{:S(2)}) copy-start(s32[8]{0:T(128)} %seeds.1) | copy-start | bytes 100
  133.1 1.5 copy-start.16
  133.1 1.5 copy-start.17
  133.1 1.5 copy-start.18
  133.1 15.4 %collective-permute-start.2 = (bf16[2,128,256]{2,1,0:T(8,128)(2,1)}, bf16[2,128,256]{2,1,0:T(8,128)(2,1)}, u32[]{:S(2)}, u32[]{:S(2)}) collective-permute-start(bf16[2,128,256]{2,1,0:T(8,128)(2,1)} %get-tuple-element.31), channel_id=1, source_target_pairs={{0,2},{2,0},{4,6},{6,4},{8,10},{10,8},{12,14},{14,12},{1,3},{3,1},... | collective-permute-start | bytes 393224 | tf_op jit(solution)/shard_map/ppermute | solution.py:376
  134.2 18.3 %collective-permute-start.3 = (bf16[2,128,256]{2,1,0:T(8,128)(2,1)}, bf16[2,128,256]{2,1,0:T(8,128)(2,1)}, u32[]{:S(2)}, u32[]{:S(2)}) collective-permute-start(bf16[2,128,256]{2,1,0:T(8,128)(2,1)} %get-tuple-element.32), channel_id=1, source_target_pairs={{0,4},{2,6},{4,0},{6,2},{8,12},{10,14},{12,8},{14,10},{1,5},{3,7},... | collective-permute-start | bytes 393224 | tf_op jit(solution)/shard_map/ppermute | solution.py:376
  134.6 18.0 %collective-permute-start.4 = (bf16[2,128,256]{2,1,0:T(8,128)(2,1)}, bf16[2,128,256]{2,1,0:T(8,128)(2,1)}, u32[]{:S(2)}, u32[]{:S(2)}) collective-permute-start(bf16[2,128,256]{2,1,0:T(8,128)(2,1)} %get-tuple-element.33), channel_id=1, source_target_pairs={{0,6},{2,4},{4,2},{6,0},{8,14},{10,12},{12,10},{14,8},{1,7},{3,5},... | collective-permute-start | bytes 393224 | tf_op jit(solution)/shard_map/ppermute | solution.py:376
  148.5 44.1 %collective-permute-start.15 = (bf16[16,128,256]{2,1,0:T(8,128)(2,1)S(1)}, bf16[16,128,256]{2,1,0:T(8,128)(2,1)}, u32[]{:S(2)}, u32[]{:S(2)}) collective-permute-start(bf16[16,128,256]{2,1,0:T(8,128)(2,1)S(1)} %all-to-all-done.2.refs_4_), channel_id=1, source_target_pairs={{0,16},{16,0},{1,17},{17,1},{2,18},{18,2},{3,19},{19,3},{4,20},{20... | collective-permute-start | bytes 3145736 | tf_op jit(solution)/shard_map/ppermute | solution.py:379
  149.7 14.8 %collective-permute-start.5 = (bf16[2,128,256]{2,1,0:T(8,128)(2,1)}, bf16[2,128,256]{2,1,0:T(8,128)(2,1)S(1)}, u32[]{:S(2)}, u32[]{:S(2)}) collective-permute-start(bf16[2,128,256]{2,1,0:T(8,128)(2,1)} %copy-done.19), channel_id=1, source_target_pairs={{0,8},{2,10},{4,12},{6,14},{8,0},{10,2},{12,4},{14,6},{1,9},{3,11}... | collective-permute-start | bytes 393224 | tf_op jit(solution)/shard_map/ppermute | solution.py:376
  149.7 17.6 %collective-permute-start.6 = (bf16[2,128,256]{2,1,0:T(8,128)(2,1)}, bf16[2,128,256]{2,1,0:T(8,128)(2,1)S(1)}, u32[]{:S(2)}, u32[]{:S(2)}) collective-permute-start(bf16[2,128,256]{2,1,0:T(8,128)(2,1)} %copy-done.18), channel_id=1, source_target_pairs={{0,10},{2,8},{4,14},{6,12},{8,2},{10,0},{12,6},{14,4},{1,11},{3,9}... | collective-permute-start | bytes 393224 | tf_op jit(solution)/shard_map/ppermute | solution.py:376
  152.5 17.6 %collective-permute-start.7 = (bf16[2,128,256]{2,1,0:T(8,128)(2,1)}, bf16[2,128,256]{2,1,0:T(8,128)(2,1)S(1)}, u32[]{:S(2)}, u32[]{:S(2)}) collective-permute-start(bf16[2,128,256]{2,1,0:T(8,128)(2,1)} %copy-done.17), channel_id=1, source_target_pairs={{0,12},{2,14},{4,8},{6,10},{8,4},{10,6},{12,0},{14,2},{1,13},{3,15... | collective-permute-start | bytes 393224 | tf_op jit(solution)/shard_map/ppermute | solution.py:376
  152.5 21.4 %collective-permute-start.8 = (bf16[2,128,256]{2,1,0:T(8,128)(2,1)}, bf16[2,128,256]{2,1,0:T(8,128)(2,1)S(1)}, u32[]{:S(2)}, u32[]{:S(2)}) collective-permute-start(bf16[2,128,256]{2,1,0:T(8,128)(2,1)} %copy-done.16), channel_id=1, source_target_pairs={{0,14},{2,12},{4,10},{6,8},{8,6},{10,4},{12,2},{14,0},{1,15},{3,13... | collective-permute-start | bytes 393224 | tf_op jit(solution)/shard_map/ppermute | solution.py:376
  154.5 1.6 copy-start.1
  156.1 0.9 copy-start.6
  157.0 16.9 %copy-start.11 = (bf16[2,128,256]{2,1,0:T(8,128)(2,1)S(1)}, bf16[2,128,256]{2,1,0:T(8,128)(2,1)}, u32[]{:S(2)}) copy-start(bf16[2,128,256]{2,1,0:T(8,128)(2,1)} %copy-done.10) | copy-start | bytes 393220
  157.0 21.4 %copy-start.2 = (bf16[128,8192]{1,0:T(8,128)(2,1)S(1)}, bf16[128,8192]{1,0:T(8,128)(2,1)}, u32[]{:S(2)}) copy-start(bf16[128,8192]{1,0:T(8,128)(2,1)} %dy_ref.1) | copy-start | bytes 6291460
  175.8 4.3 %collective-permute-start.11 = (bf16[304,128]{1,0:T(8,128)(2,1)S(1)}, bf16[304,128]{1,0:T(8,128)(2,1)S(1)}, u32[]{:S(2)}, u32[]{:S(2)}) collective-permute-start(bf16[304,128]{1,0:T(8,128)(2,1)S(1)} %hidden_values.1.z_ref), channel_id=1, source_target_pairs={{0,12},{2,14},{4,8},{6,10},{8,4},{10,6},{12,0},{14,2},{1,13},{3,15... | collective-permute-start | bytes 233480 | tf_op jit(solution)/shard_map/ppermute | solution.py:438
  176.9 3.5 %collective-permute-start.10 = (bf16[304,128]{1,0:T(8,128)(2,1)S(1)}, bf16[304,128]{1,0:T(8,128)(2,1)S(1)}, u32[]{:S(2)}, u32[]{:S(2)}) collective-permute-start(bf16[304,128]{1,0:T(8,128)(2,1)S(1)} %hidden_values.1.z_ref), channel_id=1, source_target_pairs={{0,4},{2,6},{4,0},{6,2},{8,12},{10,14},{12,8},{14,10},{1,5},{3,7},... | collective-permute-start | bytes 233480 | tf_op jit(solution)/shard_map/ppermute | solution.py:438
  176.9 4.6 %collective-permute-start.9 = (bf16[304,128]{1,0:T(8,128)(2,1)S(1)}, bf16[304,128]{1,0:T(8,128)(2,1)S(1)}, u32[]{:S(2)}, u32[]{:S(2)}) collective-permute-start(bf16[304,128]{1,0:T(8,128)(2,1)S(1)} %hidden_values.1.z_ref), channel_id=1, source_target_pairs={{0,8},{2,10},{4,12},{6,14},{8,0},{10,2},{12,4},{14,6},{1,9},{3,11}... | collective-permute-start | bytes 233480 | tf_op jit(solution)/shard_map/ppermute | solution.py:438
  181.5 9.2 %collective-permute-start.12 = (bf16[4,304,128]{2,1,0:T(8,128)(2,1)S(1)}, bf16[4,304,128]{2,1,0:T(8,128)(2,1)S(1)}, u32[]{:S(2)}, u32[]{:S(2)}) collective-permute-start(bf16[4,304,128]{2,1,0:T(8,128)(2,1)S(1)} %pad_maximum_fusion.refs_0_.refs_1_), channel_id=1, source_target_pairs={{0,2},{2,0},{4,6},{6,4},{8,10},{10,8},{12,14},{14,12},{1,3},{3,1},... | collective-permute-start | bytes 933896 | tf_op jit(solution)/shard_map/ppermute | solution.py:446
  182.8 16.2 %all-to-all-start.4 = ((bf16[16,16,512]{2,1,0:T(8,128)(2,1)}), bf16[16,16,512]{2,1,0:T(8,128)(2,1)S(1)}, u32[]{:S(2)}, u32[]{:S(2)}) async-start(bf16[16,16,512]{2,1,0:T(8,128)(2,1)} %output_terms.1), calls=%async_computation.4 | async-start | bytes 524288 | tf_op jit(solution)/shard_map/all_to_all | solution.py:441
  190.3 1.6 collective-permute-start.13
  190.7 1.8 collective-permute-start.14
  199.0 56.1 %all-to-all-start.3 = ((bf16[16,128,512]{2,1,0:T(8,128)(2,1)}), bf16[16,128,512]{2,1,0:T(8,128)(2,1)}, u32[]{:S(2)}, u32[]{:S(2)}) async-start(bf16[16,128,512]{2,1,0:T(8,128)(2,1)} %output_columns.1), calls=%async_computation.3 | async-start | bytes 4194304 | tf_op jit(solution)/shard_map/all_to_all | solution.py:476
  204.7 48.6 %copy-start.7 = (f32[8,16,128]{2,1,0:T(8,128)S(1)}, f32[8,16,128]{2,1,0:T(8,128)}, u32[]{:S(2)}) copy-start(f32[8,16,128]{2,1,0:T(8,128)} %refs_8_.1) | copy-start | bytes 196612
  204.7 48.6 %copy-start.8 = (f32[8,16,512]{2,1,0:T(8,128)S(1)}, f32[8,16,512]{2,1,0:T(8,128)}, u32[]{:S(2)}) copy-start(f32[8,16,512]{2,1,0:T(8,128)} %refs_13_.1) | copy-start | bytes 786436
  204.7 48.6 %copy-start.9 = (f32[8,16,512]{2,1,0:T(8,128)S(1)}, f32[8,16,512]{2,1,0:T(8,128)}, u32[]{:S(2)}) copy-start(f32[8,16,512]{2,1,0:T(8,128)} %refs_14_.1) | copy-start | bytes 786436
  204.7 48.6 %copy-start.12 = (f32[8,16,128]{2,1,0:T(8,128)S(1)}, f32[8,16,128]{2,1,0:T(8,128)}, u32[]{:S(2)}) copy-start(f32[8,16,128]{2,1,0:T(8,128)} %refs_9_.1) | copy-start | bytes 196612
  204.8 48.6 %copy-start.13 = (f32[8,16,128]{2,1,0:T(8,128)S(1)}, f32[8,16,128]{2,1,0:T(8,128)}, u32[]{:S(2)}) copy-start(f32[8,16,128]{2,1,0:T(8,128)} %refs_10_.1) | copy-start | bytes 196612
  205.9 1.3 collective-permute-start.16
  207.2 8.1 %collective-permute-start.17 = (f32[8,128]{1,0:T(8,128)S(1)}, f32[8,128]{1,0:T(8,128)S(1)}, u32[]{:S(2)}, u32[]{:S(2)}) collective-permute-start(f32[8,128]{1,0:T(8,128)S(1)} %add.7.refs_0_), channel_id=1, source_target_pairs={{0,2},{2,0},{4,6},{6,4},{8,10},{10,8},{12,14},{14,12},{1,3},{3,1},... | collective-permute-start | bytes 12296 | tf_op jit(solution)/shard_map/ppermute | solution.py:520
  208.4 31.6 %collective-permute-start.18 = (f32[8,128]{1,0:T(8,128)S(1)}, f32[8,128]{1,0:T(8,128)S(1)}, u32[]{:S(2)}, u32[]{:S(2)}) collective-permute-start(f32[8,128]{1,0:T(8,128)S(1)} %add.7.refs_0_), channel_id=1, source_target_pairs={{0,4},{2,6},{4,0},{6,2},{8,12},{10,14},{12,8},{14,10},{1,5},{3,7},... | collective-permute-start | bytes 12296 | tf_op jit(solution)/shard_map/ppermute | solution.py:520
  208.7 34.5 %collective-permute-start.19 = (f32[8,128]{1,0:T(8,128)S(1)}, f32[8,128]{1,0:T(8,128)S(1)}, u32[]{:S(2)}, u32[]{:S(2)}) collective-permute-start(f32[8,128]{1,0:T(8,128)S(1)} %add.7.refs_0_), channel_id=1, source_target_pairs={{0,6},{2,4},{4,2},{6,0},{8,14},{10,12},{12,10},{14,8},{1,7},{3,5},... | collective-permute-start | bytes 12296 | tf_op jit(solution)/shard_map/ppermute | solution.py:520
  209.9 40.6 %collective-permute-start.20 = (f32[8,128]{1,0:T(8,128)S(1)}, f32[8,128]{1,0:T(8,128)S(1)}, u32[]{:S(2)}, u32[]{:S(2)}) collective-permute-start(f32[8,128]{1,0:T(8,128)S(1)} %add.7.refs_0_), channel_id=1, source_target_pairs={{0,8},{2,10},{4,12},{6,14},{8,0},{10,2},{12,4},{14,6},{1,9},{3,11}... | collective-permute-start | bytes 12296 | tf_op jit(solution)/shard_map/ppermute | solution.py:520
  212.0 38.5 %collective-permute-start.21 = (f32[8,128]{1,0:T(8,128)S(1)}, f32[8,128]{1,0:T(8,128)S(1)}, u32[]{:S(2)}, u32[]{:S(2)}) collective-permute-start(f32[8,128]{1,0:T(8,128)S(1)} %add.7.refs_0_), channel_id=1, source_target_pairs={{0,10},{2,8},{4,14},{6,12},{8,2},{10,0},{12,6},{14,4},{1,11},{3,9}... | collective-permute-start | bytes 12296 | tf_op jit(solution)/shard_map/ppermute | solution.py:520
  215.4 36.9 %collective-permute-start.22 = (f32[8,128]{1,0:T(8,128)S(1)}, f32[8,128]{1,0:T(8,128)S(1)}, u32[]{:S(2)}, u32[]{:S(2)}) collective-permute-start(f32[8,128]{1,0:T(8,128)S(1)} %add.7.refs_0_), channel_id=1, source_target_pairs={{0,12},{2,14},{4,8},{6,10},{8,4},{10,6},{12,0},{14,2},{1,13},{3,15... | collective-permute-start | bytes 12296 | tf_op jit(solution)/shard_map/ppermute | solution.py:520
  240.0 13.3 %collective-permute-start.23 = (f32[8,128]{1,0:T(8,128)S(1)}, f32[8,128]{1,0:T(8,128)S(1)}, u32[]{:S(2)}, u32[]{:S(2)}) collective-permute-start(f32[8,128]{1,0:T(8,128)S(1)} %add.7.refs_0_), channel_id=1, source_target_pairs={{0,14},{2,12},{4,10},{6,8},{8,6},{10,4},{12,2},{14,0},{1,15},{3,13... | collective-permute-start | bytes 12296 | tf_op jit(solution)/shard_map/ppermute | solution.py:520
  (2 other events, 1.3 us)

commit v5 on v4

--- a/solution.py
+++ b/solution.py
@@ -128,25 +128,26 @@
     )
 
 
-def pair_sum_kernel(kept_ref, got_ref, *refs):
+def pair_sum_kernel(kept_ref, got_ref, *refs, places):
     o_refs, (held, stores) = refs[:-2], refs[-2:]
     copies = []
-    for i, o_ref in enumerate(o_refs):
+    for i, (out, at) in enumerate(places):
         held[i] = (kept_ref[i].astype(f32) + got_ref[i].astype(f32)).astype(bf16)
-        copies.append(pltpu.make_async_copy(held.at[i], o_ref, stores.at[i]))
+        copies.append(pltpu.make_async_copy(held.at[i], o_refs[out].at[at], stores.at[i]))
         copies[i].start()
     for copy in copies:
         copy.wait()
 
 
-def pair_sums(kept, got):
+def pair_sums(kept, got, places):
     count = kept.shape[0]
+    outs = 1 + max(out for out, _ in places)
     vmem = pl.BlockSpec(memory_space=pltpu.VMEM)
     return pl.pallas_call(
-        pair_sum_kernel,
-        out_shape=(jax.ShapeDtypeStruct(kept.shape[1:], bf16),) * count,
+        functools.partial(pair_sum_kernel, places=places),
+        out_shape=(jax.ShapeDtypeStruct((count // outs,) + kept.shape[1:], bf16),) * outs,
         in_specs=[vmem, vmem],
-        out_specs=(pl.BlockSpec(memory_space=pltpu.HBM),) * count,
+        out_specs=(pl.BlockSpec(memory_space=pltpu.HBM),) * outs,
         scratch_shapes=[pltpu.VMEM(kept.shape, bf16), pltpu.SemaphoreType.DMA((count,))],
         compiler_params=pltpu.CompilerParams(vmem_limit_bytes=vmem_limit),
         name="pair_sums",
@@ -170,9 +171,9 @@
 
 def hidden_kernel(ids, counts, *refs, block, picks, rank):
     part_refs, side_ref, o_ref = refs[:-2], refs[-2], refs[-1]
-    total = part_refs[0][...].astype(f32)
+    total = part_refs[0][0].astype(f32)
     for part_ref in part_refs[1:]:
-        total = total + part_ref[...].astype(f32)
+        total = total + part_ref[0].astype(f32)
     swap = ids[0] != 0
     count = counts[ids[2]]
     low_t = jnp.zeros((rank, block), f32)
@@ -371,11 +372,13 @@
     (sent,) = products(0, chips, (1,))
     got = lax.ppermute(sent, "core", other)
     (kept,) = products(0, chips, (0,))
-    paired = pair_sums(kept, got)
+    x_kept, x_sent = pair_sums(kept, got, [(c % 2, c // 2) for c in range(chips)])
+    x_got = lax.ppermute(x_sent, "chip", across(1))
+    paired = pair_sums(x_kept, x_got, [(c, 0) for c in range(chips // 2)])
     summed = [paired[0]] + [
-        lax.ppermute(paired[c], "chip", across(c)) for c in range(1, chips)
+        lax.ppermute(paired[c], "chip", across(2 * c)) for c in range(1, chips // 2)
     ]
-    dm, _ = lax.optimization_barrier((dm, summed[1]))
+    dm, _ = lax.optimization_barrier((dm, x_got))
     do = lax.ppermute(dm, "groups", other)
 
     rows = picks * block + rank * (1 + picks)
@@ -517,14 +520,21 @@
         tuple(a for a in gathered for _ in range(picks)) + (parts_b,),
     )
     squares = squares + lax.ppermute(squares, "core", other)
-    totals = [squares] + [lax.ppermute(squares, "chip", across(c)) for c in range(1, chips)]
+    mask = 1
+    while mask < near:
+        squares = squares + lax.ppermute(squares, "chip", across(mask))
+        mask *= 2
+    totals = [squares] + [
+        lax.ppermute(squares, "chip", across(m)) for m in (far, near, far + near)
+    ]
+    totals, output = lax.optimization_barrier((totals, output))
     limit = math.sqrt(rank * (n * block + model))
     updated = call(
         functools.partial(adamw_kernel, limit=limit, runs=runs),
         "adamw",
         (maps_a,) * 3 + (maps_b,) * 3,
         (1,),
-        [whole(lanes)] * chips + [whole(maps_a)] * 4 + [whole(maps_b)] * 4,
+        [whole(lanes)] * len(totals) + [whole(maps_a)] * 4 + [whole(maps_b)] * 4,
         [whole(maps_a)] * 3 + [whole(maps_b)] * 3,
         (ids,),
         (

time: 261 us -> 254 us (0.973)
  starting transfers between devices: 59.2 us -> 50.6 us
    ppermute x14 -> x8, waiting for transfers between devices: 50.3 us -> 17.1 us  [the longest x1 7.02 us: body(): squares = squares + lax.ppermute(squares, 'chip', across(mask))]
    all_to_all x1, waiting for transfers between devices: 0.01 us -> 32.5 us  [body(): lax.all_to_all(out_chunks, hid, split_axis=0, concat_axis=0, tiled=True)]
    ppermute x14 -> x8, starting transfers between devices: 17.8 us -> 8.22 us  [the longest x3 3.12 us: body(): lax.ppermute(squares, 'chip', across(m))]
    unnamed x43 -> x35, local copies, waits for them, and re-layouts: 8.64 us -> 9.11 us
  transfers between devices with their start and end apart: 29 -> 23, of which waited for: 19 -> 14; matrix products, arithmetic and copies ran while one was open for 0% -> 0% of each run, Pallas kernels for 10% -> 11%
where the time goes in v5:
time: 254 us; the launch traced here: 252 us
  waiting for transfers between devices  158 us (62%)
  starting transfers between devices  50.6 us (20%)
  Pallas kernels  33.2 us (13%)
  local copies, waits for them, and re-layouts  9.11 us (4%)
    all_to_all x1, waiting for transfers between devices, body(): xb = lax.all_to_all(x_send, hid, split_axis=0, concat_axis=0, tiled=True)  45 us
    all_to_all x1, waiting for transfers between devices, body(): wm = lax.all_to_all(w_send, hid, split_axis=0, concat_axis=0, tiled=True)  43.2 us
    all_to_all x1, waiting for transfers between devices, body(): lax.all_to_all(out_chunks, hid, split_axis=0, concat_axis=0, tiled=True)  32.5 us
    pallas_call x9, Pallas kernels, call(): pl.pallas_call(kernel, out_shape=out, grid_spec=pltpu.PrefetchScalarGridS...  19.6 us
    all_to_all x1, waiting for transfers between devices, body(): dm = lax.all_to_all(d_send, hid, split_axis=0, concat_axis=0, tiled=True)  13.2 us
    unnamed x35, local copies, waits for them, and re-layouts  9.11 us
    all_to_all x1, starting transfers between devices, body(): lax.all_to_all(term_b, hid, split_axis=0, concat_axis=0, tiled=True)  9 us
    ppermute x1, waiting for transfers between devices, body(): squares = squares + lax.ppermute(squares, 'chip', across(mask))  7.02 us
  transfers between devices with their start and end apart: 23, of which 14 were waited for; matrix products, arithmetic and copies ran while one was open for 0% of the time, Pallas kernels for 11%

profile of v5, /device:TPU:9, one launch (start us, length us, event | category | flops | bytes accessed | tf_op | source)
XLA Modules:
  0.0 251.9 jit_solution(8848388690786178368)
XLA Ops:
  0.6 3.5 %weight_rows.1 = bf16[16,528,128]{2,1,0:T(8,128)(2,1)} custom-call(bf16[8192,128]{1,0:T(8,128)(2,1)} %gate_ref.1, bf16[8192,128]{1,0:T(8,128)(2,1)} %up_ref.1, f32[8,16,128]{2,1,0:T(8,128)} %refs_4_.1), custom_call_target="tpu_custom_call" | custom-call | tf_op jit(solution)/shard_map/weight_rows/pallas_call | solution.py:329
  4.1 6.7 %all-to-all-start.1 = ((bf16[16,528,128]{2,1,0:T(8,128)(2,1)}), bf16[16,528,128]{2,1,0:T(8,128)(2,1)S(1)}, u32[]{:S(2)}, u32[]{:S(2)}) async-start(bf16[16,528,128]{2,1,0:T(8,128)(2,1)} %weight_rows.1), calls=%async_computation.1 | async-start | bytes 4325376 | tf_op jit(solution)/shard_map/all_to_all | solution.py:342
  10.9 1.6 copy-done.4
  12.5 1.0 token_columns.1
  13.5 1.4 copy-done
  15.0 43.2 %all-to-all-done.1.wm_ref.refs_4_.refs_5_ = bf16[16,528,128]{2,1,0:T(8,128)(2,1)S(1)} async-done(((bf16[16,528,128]{2,1,0:T(8,128)(2,1)}), bf16[16,528,128]{2,1,0:T(8,128)(2,1)S(1)}, u32[]{:S(2)}, u32[]{:S(2)}) %all-to-all-start.1) | async-done | bytes 2162720 | tf_op jit(solution)/shard_map/all_to_all | solution.py:342
  58.1 6.4 %all-to-all-start = ((bf16[16,144,512]{2,1,0:T(8,128)(2,1)}), bf16[16,144,512]{2,1,0:T(8,128)(2,1)}, u32[]{:S(2)}, u32[]{:S(2)}) async-start(bf16[16,144,512]{2,1,0:T(8,128)(2,1)} %copy-done), calls=%async_computation | async-start | bytes 4718592 | tf_op jit(solution)/shard_map/all_to_all | solution.py:355
  64.6 1.2 collective-permute-start
  65.8 1.6 copy-done.5
  67.4 3.5 %down_columns.1 = bf16[16,128,256]{2,1,0:T(8,128)(2,1)} custom-call(s32[3]{0:T(128)S(1)} %pad_add_fusion.ids, bf16[128,8192]{1,0:T(8,128)(2,1)S(1)} %copy-done.5), custom_call_target="tpu_custom_call" | custom-call | bytes 3145728 | tf_op jit(solution)/shard_map/down_columns/pallas_call | solution.py:28
  70.9 45.0 %all-to-all-done.x_ref.refs_0_ = bf16[16,144,512]{2,1,0:T(8,128)(2,1)} async-done(((bf16[16,144,512]{2,1,0:T(8,128)(2,1)}), bf16[16,144,512]{2,1,0:T(8,128)(2,1)}, u32[]{:S(2)}, u32[]{:S(2)}) %all-to-all-start) | async-done | bytes 2359328 | tf_op jit(solution)/shard_map/all_to_all | solution.py:355
  115.9 6.7 %all-to-all-start.3 = ((bf16[16,128,256]{2,1,0:T(8,128)(2,1)}), bf16[16,128,256]{2,1,0:T(8,128)(2,1)S(1)}, u32[]{:S(2)}, u32[]{:S(2)}) async-start(bf16[16,128,256]{2,1,0:T(8,128)(2,1)} %down_columns.1), calls=%async_computation.3 | async-start | bytes 2097152 | tf_op jit(solution)/shard_map/all_to_all | solution.py:368
  122.7 3.7 %gate_up_partial.3 = bf16[8,2,128,256]{3,2,1,0:T(8,128)(2,1)S(1)} custom-call(s32[3]{0:T(128)S(1)} %pad_add_fusion.ids, s32[16,2]{1,0:T(8,128)S(1)} %copy.25.active, bf16[16,144,512]{2,1,0:T(8,128)(2,1)} %all-to-all-done.x_ref.refs_0_, bf16[16,528,128]{2,1,0:T(8,128)(2,1)S(1)} %all-to-all-done.1.wm_ref.refs_4_.refs_5_, ...), custom_call_target="tpu_custom_call" | custom-call | flops 536870912 | bytes 7733248 | tf_op jit(solution)/shard_map/gate_up_partial/pallas_call | solution.py:28
  126.8 3.7 %gate_up_partial.2.kept_ref = bf16[8,2,128,256]{3,2,1,0:T(8,128)(2,1)S(1)} custom-call(s32[3]{0:T(128)S(1)} %pad_add_fusion.ids, s32[16,2]{1,0:T(8,128)S(1)} %copy.25.active, bf16[16,144,512]{2,1,0:T(8,128)(2,1)} %all-to-all-done.x_ref.refs_0_, bf16[16,528,128]{2,1,0:T(8,128)(2,1)S(1)} %all-to-all-done.1.wm_ref.refs_4_.refs_5_, ...), custom_call_target="tpu_custom_call" | custom-call | flops 536870912 | bytes 7733248 | tf_op jit(solution)/shard_map/gate_up_partial/pallas_call | solution.py:28
  130.6 1.7 pair_sums.2
  132.3 0.8 copy-done.7
  133.1 1.2 collective-permute-start.2
  134.3 13.2 %all-to-all-done.3.refs_4_ = bf16[16,128,256]{2,1,0:T(8,128)(2,1)S(1)} async-done(((bf16[16,128,256]{2,1,0:T(8,128)(2,1)}), bf16[16,128,256]{2,1,0:T(8,128)(2,1)S(1)}, u32[]{:S(2)}, u32[]{:S(2)}) %all-to-all-start.3) | async-done | bytes 1048608 | tf_op jit(solution)/shard_map/all_to_all | solution.py:368
  147.5 3.9 %collective-permute-done.2.got_ref = bf16[4,2,128,256]{3,2,1,0:T(8,128)(2,1)} collective-permute-done((bf16[4,2,128,256]{3,2,1,0:T(8,128)(2,1)}, bf16[4,2,128,256]{3,2,1,0:T(8,128)(2,1)}, u32[]{:S(2)}, u32[]{:S(2)}) %collective-permute-start.2) | collective-permute-done | bytes 524320 | tf_op jit(solution)/shard_map/ppermute | solution.py:376
  151.4 1.3 collective-permute-start.17
  152.6 1.0 copy-done.8
  153.7 1.9 pair_sums.3
  155.6 2.6 %collective-permute-start.4 = (bf16[1,2,128,256]{3,2,1,0:T(8,128)(2,1)S(1)}, bf16[1,2,128,256]{3,2,1,0:T(8,128)(2,1)S(1)}, u32[]{:S(2)}, u32[]{:S(2)}) collective-permute-start(bf16[1,2,128,256]{3,2,1,0:T(8,128)(2,1)S(1)} %get-tuple-element.37), channel_id=1, source_target_pairs={{0,8},{2,10},{4,12},{6,14},{8,0},{10,2},{12,4},{14,6},{1,9},{3,11}... | collective-permute-start | bytes 393224 | tf_op jit(solution)/shard_map/ppermute | solution.py:379
  158.3 1.6 copy-done.1
  159.9 0.9 copy-done.6
  160.8 2.3 side_rows.1.refs_4_
  163.1 3.2 %collective-permute-done.4.refs_2_ = bf16[1,2,128,256]{3,2,1,0:T(8,128)(2,1)S(1)} collective-permute-done((bf16[1,2,128,256]{3,2,1,0:T(8,128)(2,1)S(1)}, bf16[1,2,128,256]{3,2,1,0:T(8,128)(2,1)S(1)}, u32[]{:S(2)}, u32[]{:S(2)}) %collective-permute-start.4) | collective-permute-done | bytes 131104 | tf_op jit(solution)/shard_map/ppermute | solution.py:379
  166.3 3.0 %collective-permute-done.5.refs_3_ = bf16[1,2,128,256]{3,2,1,0:T(8,128)(2,1)S(1)} collective-permute-done((bf16[1,2,128,256]{3,2,1,0:T(8,128)(2,1)S(1)}, bf16[1,2,128,256]{3,2,1,0:T(8,128)(2,1)S(1)}, u32[]{:S(2)}, u32[]{:S(2)}) %collective-permute-start.5) | collective-permute-done | bytes 131104 | tf_op jit(solution)/shard_map/ppermute | solution.py:379
  169.2 0.8 hidden_values.1.z_ref
  170.0 2.3 collective-permute-start.8
  172.3 1.3 collective-permute-start.6
  173.6 1.6 output_terms.1
  175.2 1.5 collective-permute-done.7
  176.7 0.6 collective-permute-done.6
  177.4 0.5 collective-permute-start.9
  177.8 9.0 %all-to-all-start.2 = ((bf16[16,16,512]{2,1,0:T(8,128)(2,1)}), bf16[16,16,512]{2,1,0:T(8,128)(2,1)S(1)}, u32[]{:S(2)}, u32[]{:S(2)}) async-start(bf16[16,16,512]{2,1,0:T(8,128)(2,1)} %output_terms.1), calls=%async_computation.2 | async-start | bytes 524288 | tf_op jit(solution)/shard_map/all_to_all | solution.py:444
  187.3 1.1 collective-permute-done.10.refs_4_.refs_5_.refs_2_
  188.9 4.0 %output_columns.1 = bf16[16,128,512]{2,1,0:T(8,128)(2,1)} custom-call(s32[3]{0:T(128)S(1)} %pad_add_fusion.ids, s32[16,2]{1,0:T(8,128)S(1)} %copy.25.active, bf16[4,304,128]{2,1,0:T(8,128)(2,1)S(1)} %pad_maximum_fusion.refs_0_.refs_1_, bf16[4,304,128]{2,1,0:T(8,128)(2,1)S(1)} %collective-permute-done.9.refs_2_.refs_3_.refs_1_, ...), custom_call_target="tpu_custom_call" | custom-call | tf_op jit(solution)/shard_map/output_columns/pallas_call | solution.py:461
  192.9 2.6 %all-to-all-done.2.refs_8_ = bf16[16,16,512]{2,1,0:T(8,128)(2,1)S(1)} async-done(((bf16[16,16,512]{2,1,0:T(8,128)(2,1)}), bf16[16,16,512]{2,1,0:T(8,128)(2,1)S(1)}, u32[]{:S(2)}, u32[]{:S(2)}) %all-to-all-start.2) | async-done | bytes 262176 | tf_op jit(solution)/shard_map/all_to_all | solution.py:444
  195.5 5.7 %all-to-all-start.4 = ((bf16[16,128,512]{2,1,0:T(8,128)(2,1)}), bf16[16,128,512]{2,1,0:T(8,128)(2,1)}, u32[]{:S(2)}, u32[]{:S(2)}) async-start(bf16[16,128,512]{2,1,0:T(8,128)(2,1)} %output_columns.1), calls=%async_computation.4 | async-start | bytes 4194304 | tf_op jit(solution)/shard_map/all_to_all | solution.py:479
  201.2 1.2 gradients.1
  202.8 0.8 collective-permute-done.12
  203.6 1.2 collective-permute-start.13
  204.8 7.0 %collective-permute-done.13 = f32[8,128]{1,0:T(8,128)S(1)} collective-permute-done((f32[8,128]{1,0:T(8,128)S(1)}, f32[8,128]{1,0:T(8,128)S(1)}, u32[]{:S(2)}, u32[]{:S(2)}) %collective-permute-start.13) | collective-permute-done | bytes 4128 | tf_op jit(solution)/shard_map/ppermute | solution.py:525
  211.9 2.8 %collective-permute-start.14 = (f32[8,128]{1,0:T(8,128)S(1)}, f32[8,128]{1,0:T(8,128)S(1)}, u32[]{:S(2)}, u32[]{:S(2)}) collective-permute-start(f32[8,128]{1,0:T(8,128)S(1)} %add.11.refs_0_), channel_id=1, source_target_pairs={{0,8},{2,10},{4,12},{6,14},{8,0},{10,2},{12,4},{14,6},{1,9},{3,11}... | collective-permute-start | bytes 12296 | tf_op jit(solution)/shard_map/ppermute | solution.py:528
  215.0 32.5 %all-to-all-done.4.c_ref = bf16[16,128,512]{2,1,0:T(8,128)(2,1)} async-done(((bf16[16,128,512]{2,1,0:T(8,128)(2,1)}), bf16[16,128,512]{2,1,0:T(8,128)(2,1)}, u32[]{:S(2)}, u32[]{:S(2)}) %all-to-all-start.4) | async-done | bytes 2097184 | tf_op jit(solution)/shard_map/all_to_all | solution.py:479
  247.5 2.6 %join_columns.1 = bf16[128,8192]{1,0:T(8,128)(2,1)} custom-call(bf16[16,128,512]{2,1,0:T(8,128)(2,1)} %all-to-all-done.4.c_ref), custom_call_target="tpu_custom_call" | custom-call | tf_op jit(solution)/shard_map/join_columns/pallas_call | solution.py:481
  250.1 1.8 adamw.1
  (51 shorter events, 2.6 us)
Async XLA Ops:
  4.1 6.8 %copy-start.3 = (f32[8,16,512]{2,1,0:T(8,128)S(1)}, f32[8,16,512]{2,1,0:T(8,128)}, u32[]{:S(2)}) copy-start(f32[8,16,512]{2,1,0:T(8,128)} %refs_8_.1) | copy-start | bytes 786436
  4.1 54.0 %all-to-all-start.1 = ((bf16[16,528,128]{2,1,0:T(8,128)(2,1)}), bf16[16,528,128]{2,1,0:T(8,128)(2,1)S(1)}, u32[]{:S(2)}, u32[]{:S(2)}) async-start(bf16[16,528,128]{2,1,0:T(8,128)(2,1)} %weight_rows.1), calls=%async_computation.1 | async-start | bytes 4325376 | tf_op jit(solution)/shard_map/all_to_all | solution.py:342
  10.9 1.6 copy-start.4
  13.5 1.4 copy-start
  58.1 57.8 %all-to-all-start = ((bf16[16,144,512]{2,1,0:T(8,128)(2,1)}), bf16[16,144,512]{2,1,0:T(8,128)(2,1)}, u32[]{:S(2)}, u32[]{:S(2)}) async-start(bf16[16,144,512]{2,1,0:T(8,128)(2,1)} %copy-done), calls=%async_computation | async-start | bytes 4718592 | tf_op jit(solution)/shard_map/all_to_all | solution.py:355
  64.6 58.1 %collective-permute-start = (bf16[16,528,128]{2,1,0:T(8,128)(2,1)S(1)}, bf16[16,528,128]{2,1,0:T(8,128)(2,1)}, u32[]{:S(2)}, u32[]{:S(2)}) collective-permute-start(bf16[16,528,128]{2,1,0:T(8,128)(2,1)S(1)} %all-to-all-done.1.wm_ref.refs_4_.refs_5_), channel_id=1, source_target_pairs={{0,16},{16,0},{1,17},{17,1},{2,18},{18,2},{3,19},{19,3},{4,20},{20... | collective-permute-start | bytes 6488072 | tf_op jit(solution)/shard_map/ppermute | solution.py:343
  65.8 1.6 copy-start.5
  67.4 55.2 %copy-start.16 = (s32[16,2]{0,1:T(2,128)S(1)}, s32[16,2]{0,1:T(2,128)}, u32[]{:S(2)}) copy-start(s32[16,2]{0,1:T(2,128)} %param.26) | copy-start | bytes 388
  115.9 31.5 %all-to-all-start.3 = ((bf16[16,128,256]{2,1,0:T(8,128)(2,1)}), bf16[16,128,256]{2,1,0:T(8,128)(2,1)S(1)}, u32[]{:S(2)}, u32[]{:S(2)}) async-start(bf16[16,128,256]{2,1,0:T(8,128)(2,1)} %down_columns.1), calls=%async_computation.3 | async-start | bytes 2097152 | tf_op jit(solution)/shard_map/all_to_all | solution.py:368
  126.4 4.2 %collective-permute-start.1 = (bf16[8,2,128,256]{3,2,1,0:T(8,128)(2,1)S(1)}, bf16[8,2,128,256]{3,2,1,0:T(8,128)(2,1)S(1)}, u32[]{:S(2)}, u32[]{:S(2)}) collective-permute-start(bf16[8,2,128,256]{3,2,1,0:T(8,128)(2,1)S(1)} %gate_up_partial.3), channel_id=1, source_target_pairs={{0,1},{1,0},{2,3},{3,2},{4,5},{5,4},{6,7},{7,6},{8,9},{9,8},{10,11... | collective-permute-start | bytes 3145736 | tf_op jit(solution)/shard_map/ppermute | solution.py:373
  130.6 27.7 %copy-start.14 = (s32[16]{0:T(128)S(1)}, s32[16]{0:T(128)}, u32[]{:S(2)}) copy-start(s32[16]{0:T(128)} %counts.5) | copy-start | bytes 196
  130.6 27.7 %copy-start.15 = (s32[8]{0:T(128)S(1)}, s32[8]{0:T(128)}, u32[]{:S(2)}) copy-start(s32[8]{0:T(128)} %seeds.1) | copy-start | bytes 100
  132.3 0.8 copy-start.7
  133.1 18.3 %collective-permute-start.2 = (bf16[4,2,128,256]{3,2,1,0:T(8,128)(2,1)}, bf16[4,2,128,256]{3,2,1,0:T(8,128)(2,1)}, u32[]{:S(2)}, u32[]{:S(2)}) collective-permute-start(bf16[4,2,128,256]{3,2,1,0:T(8,128)(2,1)} %get-tuple-element.34), channel_id=1, source_target_pairs={{0,2},{2,0},{4,6},{6,4},{8,10},{10,8},{12,14},{14,12},{1,3},{3,1},... | collective-permute-start | bytes 1572872 | tf_op jit(solution)/shard_map/ppermute | solution.py:376
  151.4 37.5 %collective-permute-start.17 = (bf16[16,128,256]{2,1,0:T(8,128)(2,1)S(1)}, bf16[16,128,256]{2,1,0:T(8,128)(2,1)}, u32[]{:S(2)}, u32[]{:S(2)}) collective-permute-start(bf16[16,128,256]{2,1,0:T(8,128)(2,1)S(1)} %all-to-all-done.3.refs_4_), channel_id=1, source_target_pairs={{0,16},{16,0},{1,17},{17,1},{2,18},{18,2},{3,19},{19,3},{4,20},{20... | collective-permute-start | bytes 3145736 | tf_op jit(solution)/shard_map/ppermute | solution.py:382
  152.6 1.0 copy-start.8
  155.6 7.5 %collective-permute-start.3 = (bf16[1,2,128,256]{3,2,1,0:T(8,128)(2,1)S(1)}, bf16[1,2,128,256]{3,2,1,0:T(8,128)(2,1)S(1)}, u32[]{:S(2)}, u32[]{:S(2)}) collective-permute-start(bf16[1,2,128,256]{3,2,1,0:T(8,128)(2,1)S(1)} %get-tuple-element.36), channel_id=1, source_target_pairs={{0,4},{2,6},{4,0},{6,2},{8,12},{10,14},{12,8},{14,10},{1,5},{3,7},... | collective-permute-start | bytes 393224 | tf_op jit(solution)/shard_map/ppermute | solution.py:379
  155.6 10.6 %collective-permute-start.4 = (bf16[1,2,128,256]{3,2,1,0:T(8,128)(2,1)S(1)}, bf16[1,2,128,256]{3,2,1,0:T(8,128)(2,1)S(1)}, u32[]{:S(2)}, u32[]{:S(2)}) collective-permute-start(bf16[1,2,128,256]{3,2,1,0:T(8,128)(2,1)S(1)} %get-tuple-element.37), channel_id=1, source_target_pairs={{0,8},{2,10},{4,12},{6,14},{8,0},{10,2},{12,4},{14,6},{1,9},{3,11}... | collective-permute-start | bytes 393224 | tf_op jit(solution)/shard_map/ppermute | solution.py:379
  158.3 11.0 %collective-permute-start.5 = (bf16[1,2,128,256]{3,2,1,0:T(8,128)(2,1)S(1)}, bf16[1,2,128,256]{3,2,1,0:T(8,128)(2,1)S(1)}, u32[]{:S(2)}, u32[]{:S(2)}) collective-permute-start(bf16[1,2,128,256]{3,2,1,0:T(8,128)(2,1)S(1)} %get-tuple-element.38), channel_id=1, source_target_pairs={{0,12},{2,14},{4,8},{6,10},{8,4},{10,6},{12,0},{14,2},{1,13},{3,15... | collective-permute-start | bytes 393224 | tf_op jit(solution)/shard_map/ppermute | solution.py:379
  158.3 1.6 copy-start.1
  159.9 0.9 copy-start.6
  160.8 12.8 %copy-start.2 = (bf16[128,8192]{1,0:T(8,128)(2,1)S(1)}, bf16[128,8192]{1,0:T(8,128)(2,1)}, u32[]{:S(2)}) copy-start(bf16[128,8192]{1,0:T(8,128)(2,1)} %dy_ref.1) | copy-start | bytes 6291460
  170.0 5.2 %collective-permute-start.8 = (bf16[304,128]{1,0:T(8,128)(2,1)S(1)}, bf16[304,128]{1,0:T(8,128)(2,1)S(1)}, u32[]{:S(2)}, u32[]{:S(2)}) collective-permute-start(bf16[304,128]{1,0:T(8,128)(2,1)S(1)} %hidden_values.1.z_ref), channel_id=1, source_target_pairs={{0,12},{2,14},{4,8},{6,10},{8,4},{10,6},{12,0},{14,2},{1,13},{3,15... | collective-permute-start | bytes 233480 | tf_op jit(solution)/shard_map/ppermute | solution.py:441
  172.3 4.4 %collective-permute-start.7 = (bf16[304,128]{1,0:T(8,128)(2,1)S(1)}, bf16[304,128]{1,0:T(8,128)(2,1)S(1)}, u32[]{:S(2)}, u32[]{:S(2)}) collective-permute-start(bf16[304,128]{1,0:T(8,128)(2,1)S(1)} %hidden_values.1.z_ref), channel_id=1, source_target_pairs={{0,4},{2,6},{4,0},{6,2},{8,12},{10,14},{12,8},{14,10},{1,5},{3,7},... | collective-permute-start | bytes 233480 | tf_op jit(solution)/shard_map/ppermute | solution.py:441
  172.3 5.0 %collective-permute-start.6 = (bf16[304,128]{1,0:T(8,128)(2,1)S(1)}, bf16[304,128]{1,0:T(8,128)(2,1)S(1)}, u32[]{:S(2)}, u32[]{:S(2)}) collective-permute-start(bf16[304,128]{1,0:T(8,128)(2,1)S(1)} %hidden_values.1.z_ref), channel_id=1, source_target_pairs={{0,8},{2,10},{4,12},{6,14},{8,0},{10,2},{12,4},{14,6},{1,9},{3,11}... | collective-permute-start | bytes 233480 | tf_op jit(solution)/shard_map/ppermute | solution.py:441
  177.4 9.8 %collective-permute-start.9 = (bf16[4,304,128]{2,1,0:T(8,128)(2,1)S(1)}, bf16[4,304,128]{2,1,0:T(8,128)(2,1)S(1)}, u32[]{:S(2)}, u32[]{:S(2)}) collective-permute-start(bf16[4,304,128]{2,1,0:T(8,128)(2,1)S(1)} %pad_maximum_fusion.refs_0_.refs_1_), channel_id=1, source_target_pairs={{0,2},{2,0},{4,6},{6,4},{8,10},{10,8},{12,14},{14,12},{1,3},{3,1},... | collective-permute-start | bytes 933896 | tf_op jit(solution)/shard_map/ppermute | solution.py:449
  177.8 17.7 %all-to-all-start.2 = ((bf16[16,16,512]{2,1,0:T(8,128)(2,1)}), bf16[16,16,512]{2,1,0:T(8,128)(2,1)S(1)}, u32[]{:S(2)}, u32[]{:S(2)}) async-start(bf16[16,16,512]{2,1,0:T(8,128)(2,1)} %output_terms.1), calls=%async_computation.2 | async-start | bytes 524288 | tf_op jit(solution)/shard_map/all_to_all | solution.py:444
  186.8 1.6 collective-permute-start.10
  187.2 1.7 collective-permute-start.11
  195.5 52.0 %all-to-all-start.4 = ((bf16[16,128,512]{2,1,0:T(8,128)(2,1)}), bf16[16,128,512]{2,1,0:T(8,128)(2,1)}, u32[]{:S(2)}, u32[]{:S(2)}) async-start(bf16[16,128,512]{2,1,0:T(8,128)(2,1)} %output_columns.1), calls=%async_computation.4 | async-start | bytes 4194304 | tf_op jit(solution)/shard_map/all_to_all | solution.py:479
  202.3 1.3 collective-permute-start.12
  203.6 8.2 %collective-permute-start.13 = (f32[8,128]{1,0:T(8,128)S(1)}, f32[8,128]{1,0:T(8,128)S(1)}, u32[]{:S(2)}, u32[]{:S(2)}) collective-permute-start(f32[8,128]{1,0:T(8,128)S(1)} %add.10), channel_id=1, source_target_pairs={{0,2},{2,0},{4,6},{6,4},{8,10},{10,8},{12,14},{14,12},{1,3},{3,1},... | collective-permute-start | bytes 12296 | tf_op jit(solution)/shard_map/ppermute | solution.py:525
  211.8 38.3 %copy-start.9 = (f32[8,16,128]{2,1,0:T(8,128)S(1)}, f32[8,16,128]{2,1,0:T(8,128)}, u32[]{:S(2)}) copy-start(f32[8,16,128]{2,1,0:T(8,128)} %refs_4_.1) | copy-start | bytes 196612
  211.8 38.3 %copy-start.10 = (f32[8,16,512]{2,1,0:T(8,128)S(1)}, f32[8,16,512]{2,1,0:T(8,128)}, u32[]{:S(2)}) copy-start(f32[8,16,512]{2,1,0:T(8,128)} %refs_9_.1) | copy-start | bytes 786436
  211.8 38.3 %copy-start.11 = (f32[8,16,512]{2,1,0:T(8,128)S(1)}, f32[8,16,512]{2,1,0:T(8,128)}, u32[]{:S(2)}) copy-start(f32[8,16,512]{2,1,0:T(8,128)} %refs_10_.1) | copy-start | bytes 786436
  211.8 38.3 %copy-start.12 = (f32[8,16,128]{2,1,0:T(8,128)S(1)}, f32[8,16,128]{2,1,0:T(8,128)}, u32[]{:S(2)}) copy-start(f32[8,16,128]{2,1,0:T(8,128)} %refs_5_.1) | copy-start | bytes 196612
  211.8 38.3 %copy-start.13 = (f32[8,16,128]{2,1,0:T(8,128)S(1)}, f32[8,16,128]{2,1,0:T(8,128)}, u32[]{:S(2)}) copy-start(f32[8,16,128]{2,1,0:T(8,128)} %refs_6_.3) | copy-start | bytes 196612
  211.9 38.2 %collective-permute-start.14 = (f32[8,128]{1,0:T(8,128)S(1)}, f32[8,128]{1,0:T(8,128)S(1)}, u32[]{:S(2)}, u32[]{:S(2)}) collective-permute-start(f32[8,128]{1,0:T(8,128)S(1)} %add.11.refs_0_), channel_id=1, source_target_pairs={{0,8},{2,10},{4,12},{6,14},{8,0},{10,2},{12,4},{14,6},{1,9},{3,11}... | collective-permute-start | bytes 12296 | tf_op jit(solution)/shard_map/ppermute | solution.py:528
  214.6 35.4 %collective-permute-start.15 = (f32[8,128]{1,0:T(8,128)S(1)}, f32[8,128]{1,0:T(8,128)S(1)}, u32[]{:S(2)}, u32[]{:S(2)}) collective-permute-start(f32[8,128]{1,0:T(8,128)S(1)} %add.11.refs_0_), channel_id=1, source_target_pairs={{0,4},{2,6},{4,0},{6,2},{8,12},{10,14},{12,8},{14,10},{1,5},{3,7},... | collective-permute-start | bytes 12296 | tf_op jit(solution)/shard_map/ppermute | solution.py:528
  214.6 35.4 %collective-permute-start.16 = (f32[8,128]{1,0:T(8,128)S(1)}, f32[8,128]{1,0:T(8,128)S(1)}, u32[]{:S(2)}, u32[]{:S(2)}) collective-permute-start(f32[8,128]{1,0:T(8,128)S(1)} %add.11.refs_0_), channel_id=1, source_target_pairs={{0,12},{2,14},{4,8},{6,10},{8,4},{10,6},{12,0},{14,2},{1,13},{3,15... | collective-permute-start | bytes 12296 | tf_op jit(solution)/shard_map/ppermute | solution.py:528

commit v6 on v5

--- a/solution.py
+++ b/solution.py
@@ -45,7 +45,9 @@
     return pl.BlockSpec(a.shape, lambda i, *_: zeros)
 
 
-def weight_rows_kernel(gate_ref, up_ref, a_ref, o_ref, held, loads, stores, *, chunk, n, runs):
+def weight_rows_kernel(
+    gate_ref, up_ref, a_ref, o_ref, held, maps, loads, stores, *, chunk, n, runs
+):
     group = lax.axis_index("groups")
 
     def copies(w_ref):
@@ -66,8 +68,11 @@
         for copy in copies(up_ref):
             copy.start()
 
+    fetch = pltpu.make_async_copy(a_ref, maps, loads.at[n])
+    fetch.start()
+    fetch.wait()
     for s in range(n):
-        held[s, chunk:, :] = a_ref[s * runs // n].astype(bf16)
+        held[s, chunk:, :] = maps[s * runs // n].astype(bf16)
     out = [pltpu.make_async_copy(held.at[s], o_ref.at[s], stores.at[s]) for s in range(n)]
     for s, copy in enumerate(copies(gate_ref)):
         copy.wait()
@@ -76,26 +81,28 @@
         copy.wait()
 
 
-def token_columns_kernel(ids, x_ref, b_ref, o_ref, *, block, chunk, n, runs):
+def token_columns_kernel(ids, x_ref, o_ref, *, chunk, n):
+    for s in range(n // strips):
+        o_ref[s] = x_ref[:, s * chunk : (s + 1) * chunk]
+
+
+def down_columns_kernel(ids, d_ref, b_ref, o_ref, *, block, chunk, rank, n, runs):
+    half, part = chunk // 2, rank // 2
     per = n // strips
     for s in range(per):
-        o_ref[s, :block, :] = x_ref[:, s * chunk : (s + 1) * chunk]
-        run = (pl.program_id(0) * per + s) * runs // n
-        o_ref[s, block:, :] = b_ref[run].astype(bf16)
-
-
-def down_columns_kernel(ids, d_ref, o_ref, *, chunk, n):
-    half = chunk // 2
-    for s in range(n // strips):
         base = s * chunk
 
         @pl.when(ids[0] == 0)
         def _():
-            o_ref[s] = d_ref[:, base : base + half]
+            o_ref[s, :block, :] = d_ref[:, base : base + half]
 
         @pl.when(ids[0] != 0)
         def _():
-            o_ref[s] = d_ref[:, base + half : base + chunk]
+            o_ref[s, :block, :] = d_ref[:, base + half : base + chunk]
+
+        run = (pl.program_id(0) * per + s) * runs // n
+        mine = b_ref[run, (s % 2) * part : (s % 2 + 1) * part, :]
+        o_ref[s, block:, :] = jnp.concatenate([mine[:, :half], mine[:, half:]]).astype(bf16)
 
 
 def partial_kernel(ids, active, x_ref, wm_ref, wo_ref, *o_refs, block, chunk, picks, first, sides):
@@ -155,12 +162,20 @@
 
 
 def side_rows_kernel(ids, active, counts, seeds, *refs, block, chunk, picks, rank, n):
-    b_ref, dy_ref = refs[:2]
-    tile_refs, a_refs, o_ref = refs[2 : 2 + picks], refs[2 + picks : -1], refs[-1]
-    total = None
+    own_ref, got_ref, dy_ref = refs[:3]
+    tile_refs, a_refs, o_ref = refs[3 : 3 + picks], refs[3 + picks : -1], refs[-1]
+    half, part = chunk // 2, rank // 2
+    left = jnp.zeros((2 * rank, block), f32)
+    right = jnp.zeros((2 * rank, block), f32)
     for e in range(n):
-        part = dot(b_ref[e], dy_ref[:, e * chunk : (e + 1) * chunk], ((1,), (1,)))
-        total = part if total is None else total + part
+        maps = jnp.concatenate([own_ref[e], got_ref[e]])
+        base = e * chunk
+        left += dot(maps, dy_ref[:, base : base + half], ((1,), (1,)))
+        right += dot(maps, dy_ref[:, base + half : base + chunk], ((1,), (1,)))
+    own = left[:part] + right[part:rank]
+    got = left[rank : rank + part] + right[rank + part :]
+    first, second = jnp.where(ids[1] == 0, own, got), jnp.where(ids[1] == 0, got, own)
+    total = jnp.concatenate([first, second])
     for k in range(picks):
         o_ref[k * block : (k + 1) * block, :] = tile_refs[k][0].astype(f32).astype(bf16)
         base = picks * block + rank * (1 + k)
@@ -211,7 +226,7 @@
             hidden = jnp.concatenate(hidden, axis=1)
             sums = []
             for d_ref in (dm_ref, do_ref):
-                down = jnp.concatenate([d_ref[active[t, k]] for k in range(picks)], axis=0)
+                down = jnp.concatenate([d_ref[active[t, k], :block] for k in range(picks)])
                 sums.append(dot(hidden, down).astype(bf16).astype(f32))
             left = jnp.where(swap, sums[1], sums[0])
             right = jnp.where(swap, sums[0], sums[1])
@@ -329,11 +344,12 @@
     w_send = pl.pallas_call(
         functools.partial(weight_rows_kernel, runs=runs, **sizes),
         out_shape=jax.ShapeDtypeStruct((n, chunk + rank, block), bf16),
-        in_specs=[anywhere, anywhere, pl.BlockSpec(memory_space=pltpu.VMEM)],
+        in_specs=[anywhere] * 3,
         out_specs=anywhere,
         scratch_shapes=[
             pltpu.VMEM((n, chunk + rank, block), bf16),
-            pltpu.SemaphoreType.DMA((n,)),
+            pltpu.VMEM(adapter_input_maps.shape, f32),
+            pltpu.SemaphoreType.DMA((n + 1,)),
             pltpu.SemaphoreType.DMA((n,)),
         ],
         compiler_params=pltpu.CompilerParams(vmem_limit_bytes=vmem_full),
@@ -343,26 +359,26 @@
     wo = lax.ppermute(wm, "groups", other)
 
     x_send = call(
-        functools.partial(token_columns_kernel, block=block, runs=runs, **sizes),
+        functools.partial(token_columns_kernel, **sizes),
         "token_columns",
-        jax.ShapeDtypeStruct((n, block + rank, chunk), bf16),
+        jax.ShapeDtypeStruct((n, block, chunk), bf16),
+        (strips,),
+        [pl.BlockSpec((block, strip), lambda i, ids: (0, i))],
+        pl.BlockSpec((per, block, chunk), lambda i, ids: (i, 0, 0)),
+        (ids,),
+        (tokens,),
+    )
+    xb = lax.all_to_all(x_send, hid, split_axis=0, concat_axis=0, tiled=True)
+
+    d_send = call(
+        functools.partial(down_columns_kernel, block=block, rank=rank, runs=runs, **sizes),
+        "down_columns",
+        jax.ShapeDtypeStruct((n, block + rank, half), bf16),
         (strips,),
         [pl.BlockSpec((block, strip), lambda i, ids: (0, i)), whole(adapter_output_maps)],
-        pl.BlockSpec((per, block + rank, chunk), lambda i, ids: (i, 0, 0)),
+        pl.BlockSpec((per, block + rank, half), lambda i, ids: (i, 0, 0)),
         (ids,),
-        (tokens, adapter_output_maps),
-    )
-    xb = lax.all_to_all(x_send, hid, split_axis=0, concat_axis=0, tiled=True)
-
-    d_send = call(
-        functools.partial(down_columns_kernel, **sizes),
-        "down_columns",
-        jax.ShapeDtypeStruct((n, block, half), bf16),
-        (strips,),
-        [pl.BlockSpec((block, strip), lambda i, ids: (0, i))],
-        pl.BlockSpec((per, block, half), lambda i, ids: (i, 0, 0)),
-        (ids,),
-        (down_weight,),
+        (down_weight, adapter_output_maps),
     )
     d_send, xb = lax.optimization_barrier((d_send, xb))
     dm = lax.all_to_all(d_send, hid, split_axis=0, concat_axis=0, tiled=True)
@@ -380,6 +396,7 @@
     ]
     dm, _ = lax.optimization_barrier((dm, x_got))
     do = lax.ppermute(dm, "groups", other)
+    b_got = lax.ppermute(dm[:, block:], "core", other)
 
     rows = picks * block + rank * (1 + picks)
 
@@ -402,14 +419,15 @@
         jax.ShapeDtypeStruct((rows, block), bf16),
         (1,),
         [
-            pl.BlockSpec((n, rank, chunk), lambda i, *_: (0, block // rank, 0)),
+            pl.BlockSpec((n, rank, half), lambda i, *_: (0, block // rank, 0)),
+            whole(b_got),
             whole(cotangent),
         ]
         + [tile_spec(k) for k in range(picks)]
         + [map_spec(k) for k in range(picks)],
         pl.BlockSpec((rows, block), lambda i, *_: (0, 0)),
         (ids, active, counts, seeds),
-        (xb, cotangent) + (dropout_tiles,) * picks + (wm,) * picks,
+        (dm, b_got, cotangent) + (dropout_tiles,) * picks + (wm,) * picks,
     )
     held = call(
         functools.partial(hidden_kernel, block=block, picks=picks, rank=rank),

time: 254 us -> 251 us (0.988)
  Pallas kernels: 33.2 us -> 29.8 us
  waiting for transfers between devices: 158 us -> 155 us
    all_to_all x1, waiting for transfers between devices: 45 us -> 40.9 us  [body(): xb = lax.all_to_all(x_send, hid, split_axis=0, concat_axis=0, tiled=True)]
    pallas_call x9, Pallas kernels: 19.6 us -> 16.4 us  [call(): pl.pallas_call(kernel, out_shape=out, grid_spec=pltpu.PrefetchScalarGridS...]
    all_to_all x1, waiting for transfers between devices: 13.2 us -> 15.9 us  [body(): dm = lax.all_to_all(d_send, hid, split_axis=0, concat_axis=0, tiled=True)]
    unnamed x35 -> x39, local copies, waits for them, and re-layouts: 9.11 us -> 10 us
  transfers between devices with their start and end apart: 23 -> 24, of which waited for: 14 -> 15; matrix products, arithmetic and copies ran while one was open for 0% -> 0% of each run, Pallas kernels for 11% -> 10%
where the time goes in v6:
time: 251 us; the launch traced here: 248 us
  waiting for transfers between devices  155 us (62%)
  starting transfers between devices  52.8 us (21%)
  Pallas kernels  29.8 us (12%)
  local copies, waits for them, and re-layouts  10 us (4%)
    all_to_all x1, waiting for transfers between devices, body(): wm = lax.all_to_all(w_send, hid, split_axis=0, concat_axis=0, tiled=True)  43.3 us
    all_to_all x1, waiting for transfers between devices, body(): xb = lax.all_to_all(x_send, hid, split_axis=0, concat_axis=0, tiled=True)  40.9 us
    all_to_all x1, waiting for transfers between devices, body(): lax.all_to_all(out_chunks, hid, split_axis=0, concat_axis=0, tiled=True)  31.7 us
    pallas_call x9, Pallas kernels, call(): pl.pallas_call(kernel, out_shape=out, grid_spec=pltpu.PrefetchScalarGridS...  16.4 us
    all_to_all x1, waiting for transfers between devices, body(): dm = lax.all_to_all(d_send, hid, split_axis=0, concat_axis=0, tiled=True)  15.9 us
    unnamed x39, local copies, waits for them, and re-layouts  10 us
    all_to_all x1, starting transfers between devices, body(): lax.all_to_all(term_b, hid, split_axis=0, concat_axis=0, tiled=True)  7.98 us
    ppermute x3, waiting for transfers between devices, body(): lax.ppermute(paired[c], 'chip', across(2 * c))  7.23 us
  transfers between devices with their start and end apart: 24, of which 15 were waited for; matrix products, arithmetic and copies ran while one was open for 0% of the time, Pallas kernels for 10%

profile of v6, /device:TPU:9, one launch (start us, length us, event | category | flops | bytes accessed | tf_op | source)
XLA Modules:
  0.0 248.5 jit_solution(7699598122992398753)
XLA Ops:
  0.6 3.2 %weight_rows.1 = bf16[16,528,128]{2,1,0:T(8,128)(2,1)} custom-call(bf16[8192,128]{1,0:T(8,128)(2,1)} %gate_ref.1, bf16[8192,128]{1,0:T(8,128)(2,1)} %up_ref.1, f32[8,16,128]{2,1,0:T(8,128)} %refs_4_.3), custom_call_target="tpu_custom_call" | custom-call | tf_op jit(solution)/shard_map/weight_rows/pallas_call | solution.py:344
  3.9 6.6 %all-to-all-start.1 = ((bf16[16,528,128]{2,1,0:T(8,128)(2,1)}), bf16[16,528,128]{2,1,0:T(8,128)(2,1)S(1)}, u32[]{:S(2)}, u32[]{:S(2)}) async-start(bf16[16,528,128]{2,1,0:T(8,128)(2,1)} %weight_rows.1), calls=%async_computation.1 | async-start | bytes 4325376 | tf_op jit(solution)/shard_map/all_to_all | solution.py:358
  10.5 1.6 copy-done.6
  12.1 1.0 token_columns.1
  13.1 1.3 copy-done
  14.4 43.3 %all-to-all-done.1.wm_ref.refs_5_.refs_6_ = bf16[16,528,128]{2,1,0:T(8,128)(2,1)S(1)} async-done(((bf16[16,528,128]{2,1,0:T(8,128)(2,1)}), bf16[16,528,128]{2,1,0:T(8,128)(2,1)S(1)}, u32[]{:S(2)}, u32[]{:S(2)}) %all-to-all-start.1) | async-done | bytes 2162720 | tf_op jit(solution)/shard_map/all_to_all | solution.py:358
  57.8 6.4 %all-to-all-start = ((bf16[16,128,512]{2,1,0:T(8,128)(2,1)}), bf16[16,128,512]{2,1,0:T(8,128)(2,1)}, u32[]{:S(2)}, u32[]{:S(2)}) async-start(bf16[16,128,512]{2,1,0:T(8,128)(2,1)} %copy-done), calls=%async_computation | async-start | bytes 4194304 | tf_op jit(solution)/shard_map/all_to_all | solution.py:371
  64.2 1.3 collective-permute-start
  65.5 1.6 copy-done.7
  67.0 1.2 down_columns.1
  68.3 1.0 copy-done.3
  69.3 40.9 %all-to-all-done.x_ref = bf16[16,128,512]{2,1,0:T(8,128)(2,1)} async-done(((bf16[16,128,512]{2,1,0:T(8,128)(2,1)}), bf16[16,128,512]{2,1,0:T(8,128)(2,1)}, u32[]{:S(2)}, u32[]{:S(2)}) %all-to-all-start) | async-done | bytes 2097184 | tf_op jit(solution)/shard_map/all_to_all | solution.py:371
  110.3 6.3 %all-to-all-start.2 = ((bf16[16,144,256]{2,1,0:T(8,128)(2,1)}), bf16[16,144,256]{2,1,0:T(8,128)(2,1)S(1)}, u32[]{:S(2)}, u32[]{:S(2)}) async-start(bf16[16,144,256]{2,1,0:T(8,128)(2,1)} %copy-done.3), calls=%async_computation.2 | async-start | bytes 2359296 | tf_op jit(solution)/shard_map/all_to_all | solution.py:384
  116.7 3.7 %gate_up_partial.3 = bf16[8,2,128,256]{3,2,1,0:T(8,128)(2,1)S(1)} custom-call(s32[3]{0:T(128)S(1)} %pad_add_fusion.ids, s32[16,2]{1,0:T(8,128)S(1)} %copy.25.active, bf16[16,128,512]{2,1,0:T(8,128)(2,1)} %all-to-all-done.x_ref, bf16[16,528,128]{2,1,0:T(8,128)(2,1)S(1)} %all-to-all-done.1.wm_ref.refs_5_.refs_6_, bf16[16,528,128]{2,1,0:T(8,128)(2,1)} %collective-permute-done.wo_ref), custom_call_target="tpu_custom_call" | custom-call | flops 536870912 | bytes 7471104 | tf_op jit(solution)/shard_map/gate_up_partial/pallas_call | solution.py:28
  120.9 3.7 %gate_up_partial.2.kept_ref = bf16[8,2,128,256]{3,2,1,0:T(8,128)(2,1)S(1)} custom-call(s32[3]{0:T(128)S(1)} %pad_add_fusion.ids, s32[16,2]{1,0:T(8,128)S(1)} %copy.25.active, bf16[16,128,512]{2,1,0:T(8,128)(2,1)} %all-to-all-done.x_ref, bf16[16,528,128]{2,1,0:T(8,128)(2,1)S(1)} %all-to-all-done.1.wm_ref.refs_5_.refs_6_, ...), custom_call_target="tpu_custom_call" | custom-call | flops 536870912 | bytes 7471104 | tf_op jit(solution)/shard_map/gate_up_partial/pallas_call | solution.py:28
  124.6 1.7 pair_sums.2
  127.1 1.2 collective-permute-start.2
  128.3 15.9 %all-to-all-done.2.refs_0_.refs_4_ = bf16[16,144,256]{2,1,0:T(8,128)(2,1)S(1)} async-done(((bf16[16,144,256]{2,1,0:T(8,128)(2,1)}), bf16[16,144,256]{2,1,0:T(8,128)(2,1)S(1)}, u32[]{:S(2)}, u32[]{:S(2)}) %all-to-all-start.2) | async-done | bytes 1179680 | tf_op jit(solution)/shard_map/all_to_all | solution.py:384
  144.2 1.9 collective-permute-done.2.got_ref
  146.1 1.2 collective-permute-start.18
  147.3 1.3 collective-permute-start.6
  148.7 1.0 copy-done.10
  149.7 1.9 pair_sums.3
  151.7 3.3 %collective-permute-start.4 = (bf16[1,2,128,256]{3,2,1,0:T(8,128)(2,1)S(1)}, bf16[1,2,128,256]{3,2,1,0:T(8,128)(2,1)S(1)}, u32[]{:S(2)}, u32[]{:S(2)}) collective-permute-start(bf16[1,2,128,256]{3,2,1,0:T(8,128)(2,1)S(1)} %get-tuple-element.37), channel_id=1, source_target_pairs={{0,8},{2,10},{4,12},{6,14},{8,0},{10,2},{12,4},{14,6},{1,9},{3,11}... | collective-permute-start | bytes 393224 | tf_op jit(solution)/shard_map/ppermute | solution.py:395
  155.0 1.6 copy-done.1
  156.6 0.9 copy-done.8
  157.5 1.5 side_rows.1.refs_4_
  159.0 4.4 %collective-permute-done.4.refs_2_ = bf16[1,2,128,256]{3,2,1,0:T(8,128)(2,1)S(1)} collective-permute-done((bf16[1,2,128,256]{3,2,1,0:T(8,128)(2,1)S(1)}, bf16[1,2,128,256]{3,2,1,0:T(8,128)(2,1)S(1)}, u32[]{:S(2)}, u32[]{:S(2)}) %collective-permute-start.4) | collective-permute-done | bytes 131104 | tf_op jit(solution)/shard_map/ppermute | solution.py:395
  163.4 2.8 %collective-permute-done.5.refs_3_ = bf16[1,2,128,256]{3,2,1,0:T(8,128)(2,1)S(1)} collective-permute-done((bf16[1,2,128,256]{3,2,1,0:T(8,128)(2,1)S(1)}, bf16[1,2,128,256]{3,2,1,0:T(8,128)(2,1)S(1)}, u32[]{:S(2)}, u32[]{:S(2)}) %collective-permute-start.5) | collective-permute-done | bytes 131104 | tf_op jit(solution)/shard_map/ppermute | solution.py:395
  167.0 2.3 collective-permute-start.9
  169.3 1.3 collective-permute-start.7
  170.6 1.6 output_terms.1
  173.3 0.9 collective-permute-done.7
  174.2 1.2 collective-permute-start.10
  175.4 8.0 %all-to-all-start.3 = ((bf16[16,16,512]{2,1,0:T(8,128)(2,1)}), bf16[16,16,512]{2,1,0:T(8,128)(2,1)S(1)}, u32[]{:S(2)}, u32[]{:S(2)}) async-start(bf16[16,16,512]{2,1,0:T(8,128)(2,1)} %output_terms.1), calls=%async_computation.3 | async-start | bytes 524288 | tf_op jit(solution)/shard_map/all_to_all | solution.py:462
  184.1 0.9 collective-permute-done.11.refs_4_.refs_5_.refs_2_
  185.5 4.0 %output_columns.1 = bf16[16,128,512]{2,1,0:T(8,128)(2,1)} custom-call(s32[3]{0:T(128)S(1)} %pad_add_fusion.ids, s32[16,2]{1,0:T(8,128)S(1)} %copy.25.active, bf16[4,304,128]{2,1,0:T(8,128)(2,1)S(1)} %pad_maximum_fusion.refs_0_.refs_1_, bf16[4,304,128]{2,1,0:T(8,128)(2,1)S(1)} %collective-permute-done.10.refs_2_.refs_3_.refs_1_, ...), custom_call_target="tpu_custom_call" | custom-call | tf_op jit(solution)/shard_map/output_columns/pallas_call | solution.py:479
  189.5 2.6 %all-to-all-done.3.refs_8_ = bf16[16,16,512]{2,1,0:T(8,128)(2,1)S(1)} async-done(((bf16[16,16,512]{2,1,0:T(8,128)(2,1)}), bf16[16,16,512]{2,1,0:T(8,128)(2,1)S(1)}, u32[]{:S(2)}, u32[]{:S(2)}) %all-to-all-start.3) | async-done | bytes 262176 | tf_op jit(solution)/shard_map/all_to_all | solution.py:462
  192.1 5.6 %all-to-all-start.4 = ((bf16[16,128,512]{2,1,0:T(8,128)(2,1)}), bf16[16,128,512]{2,1,0:T(8,128)(2,1)}, u32[]{:S(2)}, u32[]{:S(2)}) async-start(bf16[16,128,512]{2,1,0:T(8,128)(2,1)} %output_columns.1), calls=%async_computation.4 | async-start | bytes 4194304 | tf_op jit(solution)/shard_map/all_to_all | solution.py:497
  197.7 1.2 gradients.1
  199.3 0.8 collective-permute-done.13
  200.2 1.2 collective-permute-start.14
  201.4 7.0 %collective-permute-done.14 = f32[8,128]{1,0:T(8,128)S(1)} collective-permute-done((f32[8,128]{1,0:T(8,128)S(1)}, f32[8,128]{1,0:T(8,128)S(1)}, u32[]{:S(2)}, u32[]{:S(2)}) %collective-permute-start.14) | collective-permute-done | bytes 4128 | tf_op jit(solution)/shard_map/ppermute | solution.py:543
  208.4 1.3 collective-permute-start.17
  209.8 2.6 %collective-permute-start.16 = (f32[8,128]{1,0:T(8,128)S(1)}, f32[8,128]{1,0:T(8,128)S(1)}, u32[]{:S(2)}, u32[]{:S(2)}) collective-permute-start(f32[8,128]{1,0:T(8,128)S(1)} %add.11.refs_0_), channel_id=1, source_target_pairs={{0,4},{2,6},{4,0},{6,2},{8,12},{10,14},{12,8},{14,10},{1,5},{3,7},... | collective-permute-start | bytes 12296 | tf_op jit(solution)/shard_map/ppermute | solution.py:546
  212.4 31.7 %all-to-all-done.4.c_ref = bf16[16,128,512]{2,1,0:T(8,128)(2,1)} async-done(((bf16[16,128,512]{2,1,0:T(8,128)(2,1)}), bf16[16,128,512]{2,1,0:T(8,128)(2,1)}, u32[]{:S(2)}, u32[]{:S(2)}) %all-to-all-start.4) | async-done | bytes 2097184 | tf_op jit(solution)/shard_map/all_to_all | solution.py:497
  244.0 2.6 %join_columns.1 = bf16[128,8192]{1,0:T(8,128)(2,1)} custom-call(bf16[16,128,512]{2,1,0:T(8,128)(2,1)} %all-to-all-done.4.c_ref), custom_call_target="tpu_custom_call" | custom-call | tf_op jit(solution)/shard_map/join_columns/pallas_call | solution.py:499
  246.7 1.8 adamw.1
  (58 shorter events, 5.0 us)
Async XLA Ops:
  3.9 53.9 %all-to-all-start.1 = ((bf16[16,528,128]{2,1,0:T(8,128)(2,1)}), bf16[16,528,128]{2,1,0:T(8,128)(2,1)S(1)}, u32[]{:S(2)}, u32[]{:S(2)}) async-start(bf16[16,528,128]{2,1,0:T(8,128)(2,1)} %weight_rows.1), calls=%async_computation.1 | async-start | bytes 4325376 | tf_op jit(solution)/shard_map/all_to_all | solution.py:358
  10.5 1.6 copy-start.6
  13.1 1.3 copy-start
  14.4 51.0 %copy-start.4 = (f32[8,16,512]{2,1,0:T(8,128)S(1)}, f32[8,16,512]{2,1,0:T(8,128)}, u32[]{:S(2)}) copy-start(f32[8,16,512]{2,1,0:T(8,128)} %refs_8_.1) | copy-start | bytes 786436
  57.8 52.5 %all-to-all-start = ((bf16[16,128,512]{2,1,0:T(8,128)(2,1)}), bf16[16,128,512]{2,1,0:T(8,128)(2,1)}, u32[]{:S(2)}, u32[]{:S(2)}) async-start(bf16[16,128,512]{2,1,0:T(8,128)(2,1)} %copy-done), calls=%async_computation | async-start | bytes 4194304 | tf_op jit(solution)/shard_map/all_to_all | solution.py:371
  64.2 52.5 %collective-permute-start = (bf16[16,528,128]{2,1,0:T(8,128)(2,1)S(1)}, bf16[16,528,128]{2,1,0:T(8,128)(2,1)}, u32[]{:S(2)}, u32[]{:S(2)}) collective-permute-start(bf16[16,528,128]{2,1,0:T(8,128)(2,1)S(1)} %all-to-all-done.1.wm_ref.refs_5_.refs_6_), channel_id=1, source_target_pairs={{0,16},{16,0},{1,17},{17,1},{2,18},{18,2},{3,19},{19,3},{4,20},{20... | collective-permute-start | bytes 6488072 | tf_op jit(solution)/shard_map/ppermute | solution.py:359
  65.5 1.6 copy-start.7
  67.0 49.6 %copy-start.18 = (s32[16,2]{0,1:T(2,128)S(1)}, s32[16,2]{0,1:T(2,128)}, u32[]{:S(2)}) copy-start(s32[16,2]{0,1:T(2,128)} %param.26) | copy-start | bytes 388
  68.3 1.1 copy-start.3
  110.3 33.9 %all-to-all-start.2 = ((bf16[16,144,256]{2,1,0:T(8,128)(2,1)}), bf16[16,144,256]{2,1,0:T(8,128)(2,1)S(1)}, u32[]{:S(2)}, u32[]{:S(2)}) async-start(bf16[16,144,256]{2,1,0:T(8,128)(2,1)} %copy-done.3), calls=%async_computation.2 | async-start | bytes 2359296 | tf_op jit(solution)/shard_map/all_to_all | solution.py:384
  120.4 4.2 %collective-permute-start.1 = (bf16[8,2,128,256]{3,2,1,0:T(8,128)(2,1)S(1)}, bf16[8,2,128,256]{3,2,1,0:T(8,128)(2,1)S(1)}, u32[]{:S(2)}, u32[]{:S(2)}) collective-permute-start(bf16[8,2,128,256]{3,2,1,0:T(8,128)(2,1)S(1)} %gate_up_partial.3), channel_id=1, source_target_pairs={{0,1},{1,0},{2,3},{3,2},{4,5},{5,4},{6,7},{7,6},{8,9},{9,8},{10,11... | collective-permute-start | bytes 3145736 | tf_op jit(solution)/shard_map/ppermute | solution.py:389
  124.6 30.4 %copy-start.16 = (s32[16]{0:T(128)S(1)}, s32[16]{0:T(128)}, u32[]{:S(2)}) copy-start(s32[16]{0:T(128)} %counts.5) | copy-start | bytes 196
  124.6 30.4 %copy-start.17 = (s32[8]{0:T(128)S(1)}, s32[8]{0:T(128)}, u32[]{:S(2)}) copy-start(s32[8]{0:T(128)} %seeds.1) | copy-start | bytes 100
  126.3 0.8 copy-start.9
  127.1 19.0 %collective-permute-start.2 = (bf16[4,2,128,256]{3,2,1,0:T(8,128)(2,1)}, bf16[4,2,128,256]{3,2,1,0:T(8,128)(2,1)}, u32[]{:S(2)}, u32[]{:S(2)}) collective-permute-start(bf16[4,2,128,256]{3,2,1,0:T(8,128)(2,1)} %get-tuple-element.34), channel_id=1, source_target_pairs={{0,2},{2,0},{4,6},{6,4},{8,10},{10,8},{12,14},{14,12},{1,3},{3,1},... | collective-permute-start | bytes 1572872 | tf_op jit(solution)/shard_map/ppermute | solution.py:392
  146.1 39.4 %collective-permute-start.18 = (bf16[16,144,256]{2,1,0:T(8,128)(2,1)S(1)}, bf16[16,144,256]{2,1,0:T(8,128)(2,1)}, u32[]{:S(2)}, u32[]{:S(2)}) collective-permute-start(bf16[16,144,256]{2,1,0:T(8,128)(2,1)S(1)} %all-to-all-done.2.refs_0_.refs_4_), channel_id=1, source_target_pairs={{0,16},{16,0},{1,17},{17,1},{2,18},{18,2},{3,19},{19,3},{4,20},{20... | collective-permute-start | bytes 3538952 | tf_op jit(solution)/shard_map/ppermute | solution.py:398
  147.3 7.6 %collective-permute-start.6 = (bf16[16,16,256]{2,1,0:T(8,128)(2,1)S(1)}, bf16[16,16,256]{2,1,0:T(8,128)(2,1)S(1)}, u32[]{:S(2)}, u32[]{:S(2)}) collective-permute-start(bf16[16,16,256]{2,1,0:T(8,128)(2,1)S(1)} %slice.3), channel_id=1, source_target_pairs={{0,1},{1,0},{2,3},{3,2},{4,5},{5,4},{6,7},{7,6},{8,9},{9,8},{10,11... | collective-permute-start | bytes 393224 | tf_op jit(solution)/shard_map/ppermute | solution.py:399
  148.7 1.0 copy-start.10
  151.6 7.4 %collective-permute-start.3 = (bf16[1,2,128,256]{3,2,1,0:T(8,128)(2,1)S(1)}, bf16[1,2,128,256]{3,2,1,0:T(8,128)(2,1)S(1)}, u32[]{:S(2)}, u32[]{:S(2)}) collective-permute-start(bf16[1,2,128,256]{3,2,1,0:T(8,128)(2,1)S(1)} %get-tuple-element.36), channel_id=1, source_target_pairs={{0,4},{2,6},{4,0},{6,2},{8,12},{10,14},{12,8},{14,10},{1,5},{3,7},... | collective-permute-start | bytes 393224 | tf_op jit(solution)/shard_map/ppermute | solution.py:395
  151.7 11.7 %collective-permute-start.4 = (bf16[1,2,128,256]{3,2,1,0:T(8,128)(2,1)S(1)}, bf16[1,2,128,256]{3,2,1,0:T(8,128)(2,1)S(1)}, u32[]{:S(2)}, u32[]{:S(2)}) collective-permute-start(bf16[1,2,128,256]{3,2,1,0:T(8,128)(2,1)S(1)} %get-tuple-element.37), channel_id=1, source_target_pairs={{0,8},{2,10},{4,12},{6,14},{8,0},{10,2},{12,4},{14,6},{1,9},{3,11}... | collective-permute-start | bytes 393224 | tf_op jit(solution)/shard_map/ppermute | solution.py:395
  155.0 11.3 %collective-permute-start.5 = (bf16[1,2,128,256]{3,2,1,0:T(8,128)(2,1)S(1)}, bf16[1,2,128,256]{3,2,1,0:T(8,128)(2,1)S(1)}, u32[]{:S(2)}, u32[]{:S(2)}) collective-permute-start(bf16[1,2,128,256]{3,2,1,0:T(8,128)(2,1)S(1)} %get-tuple-element.38), channel_id=1, source_target_pairs={{0,12},{2,14},{4,8},{6,10},{8,4},{10,6},{12,0},{14,2},{1,13},{3,15... | collective-permute-start | bytes 393224 | tf_op jit(solution)/shard_map/ppermute | solution.py:395
  155.0 1.6 copy-start.1
  156.6 0.9 copy-start.8
  157.5 13.1 %copy-start.2 = (bf16[128,8192]{1,0:T(8,128)(2,1)S(1)}, bf16[128,8192]{1,0:T(8,128)(2,1)}, u32[]{:S(2)}) copy-start(bf16[128,8192]{1,0:T(8,128)(2,1)} %dy_ref.1) | copy-start | bytes 6291460
  166.2 19.3 %copy-start.5 = (f32[8,16,512]{2,1,0:T(8,128)S(1)}, f32[8,16,512]{2,1,0:T(8,128)}, u32[]{:S(2)}) copy-start(f32[8,16,512]{2,1,0:T(8,128)} %refs_8_.1) | copy-start | bytes 786436
  167.0 5.8 %collective-permute-start.9 = (bf16[304,128]{1,0:T(8,128)(2,1)S(1)}, bf16[304,128]{1,0:T(8,128)(2,1)S(1)}, u32[]{:S(2)}, u32[]{:S(2)}) collective-permute-start(bf16[304,128]{1,0:T(8,128)(2,1)S(1)} %hidden_values.1.z_ref), channel_id=1, source_target_pairs={{0,12},{2,14},{4,8},{6,10},{8,4},{10,6},{12,0},{14,2},{1,13},{3,15... | collective-permute-start | bytes 233480 | tf_op jit(solution)/shard_map/ppermute | solution.py:459
  169.3 4.0 %collective-permute-start.8 = (bf16[304,128]{1,0:T(8,128)(2,1)S(1)}, bf16[304,128]{1,0:T(8,128)(2,1)S(1)}, u32[]{:S(2)}, u32[]{:S(2)}) collective-permute-start(bf16[304,128]{1,0:T(8,128)(2,1)S(1)} %hidden_values.1.z_ref), channel_id=1, source_target_pairs={{0,4},{2,6},{4,0},{6,2},{8,12},{10,14},{12,8},{14,10},{1,5},{3,7},... | collective-permute-start | bytes 233480 | tf_op jit(solution)/shard_map/ppermute | solution.py:459
  169.3 4.9 %collective-permute-start.7 = (bf16[304,128]{1,0:T(8,128)(2,1)S(1)}, bf16[304,128]{1,0:T(8,128)(2,1)S(1)}, u32[]{:S(2)}, u32[]{:S(2)}) collective-permute-start(bf16[304,128]{1,0:T(8,128)(2,1)S(1)} %hidden_values.1.z_ref), channel_id=1, source_target_pairs={{0,8},{2,10},{4,12},{6,14},{8,0},{10,2},{12,4},{14,6},{1,9},{3,11}... | collective-permute-start | bytes 233480 | tf_op jit(solution)/shard_map/ppermute | solution.py:459
  174.2 9.5 %collective-permute-start.10 = (bf16[4,304,128]{2,1,0:T(8,128)(2,1)S(1)}, bf16[4,304,128]{2,1,0:T(8,128)(2,1)S(1)}, u32[]{:S(2)}, u32[]{:S(2)}) collective-permute-start(bf16[4,304,128]{2,1,0:T(8,128)(2,1)S(1)} %pad_maximum_fusion.refs_0_.refs_1_), channel_id=1, source_target_pairs={{0,2},{2,0},{4,6},{6,4},{8,10},{10,8},{12,14},{14,12},{1,3},{3,1},... | collective-permute-start | bytes 933896 | tf_op jit(solution)/shard_map/ppermute | solution.py:467
  175.4 16.7 %all-to-all-start.3 = ((bf16[16,16,512]{2,1,0:T(8,128)(2,1)}), bf16[16,16,512]{2,1,0:T(8,128)(2,1)S(1)}, u32[]{:S(2)}, u32[]{:S(2)}) async-start(bf16[16,16,512]{2,1,0:T(8,128)(2,1)} %output_terms.1), calls=%async_computation.3 | async-start | bytes 524288 | tf_op jit(solution)/shard_map/all_to_all | solution.py:462
  183.4 1.6 collective-permute-start.11
  183.8 1.7 collective-permute-start.12
  192.1 51.9 %all-to-all-start.4 = ((bf16[16,128,512]{2,1,0:T(8,128)(2,1)}), bf16[16,128,512]{2,1,0:T(8,128)(2,1)}, u32[]{:S(2)}, u32[]{:S(2)}) async-start(bf16[16,128,512]{2,1,0:T(8,128)(2,1)} %output_columns.1), calls=%async_computation.4 | async-start | bytes 4194304 | tf_op jit(solution)/shard_map/all_to_all | solution.py:497
  198.9 1.2 collective-permute-start.13
  200.2 8.2 %collective-permute-start.14 = (f32[8,128]{1,0:T(8,128)S(1)}, f32[8,128]{1,0:T(8,128)S(1)}, u32[]{:S(2)}, u32[]{:S(2)}) collective-permute-start(f32[8,128]{1,0:T(8,128)S(1)} %add.10), channel_id=1, source_target_pairs={{0,2},{2,0},{4,6},{6,4},{8,10},{10,8},{12,14},{14,12},{1,3},{3,1},... | collective-permute-start | bytes 12296 | tf_op jit(solution)/shard_map/ppermute | solution.py:543
  208.4 38.3 %copy-start.11 = (f32[8,16,128]{2,1,0:T(8,128)S(1)}, f32[8,16,128]{2,1,0:T(8,128)}, u32[]{:S(2)}) copy-start(f32[8,16,128]{2,1,0:T(8,128)} %refs_4_.3) | copy-start | bytes 196612
  208.4 38.3 %copy-start.12 = (f32[8,16,512]{2,1,0:T(8,128)S(1)}, f32[8,16,512]{2,1,0:T(8,128)}, u32[]{:S(2)}) copy-start(f32[8,16,512]{2,1,0:T(8,128)} %refs_9_.1) | copy-start | bytes 786436
  208.4 38.3 %copy-start.13 = (f32[8,16,512]{2,1,0:T(8,128)S(1)}, f32[8,16,512]{2,1,0:T(8,128)}, u32[]{:S(2)}) copy-start(f32[8,16,512]{2,1,0:T(8,128)} %refs_10_.1) | copy-start | bytes 786436
  208.4 38.3 %copy-start.14 = (f32[8,16,128]{2,1,0:T(8,128)S(1)}, f32[8,16,128]{2,1,0:T(8,128)}, u32[]{:S(2)}) copy-start(f32[8,16,128]{2,1,0:T(8,128)} %refs_5_.1) | copy-start | bytes 196612
  208.4 38.3 %copy-start.15 = (f32[8,16,128]{2,1,0:T(8,128)S(1)}, f32[8,16,128]{2,1,0:T(8,128)}, u32[]{:S(2)}) copy-start(f32[8,16,128]{2,1,0:T(8,128)} %refs_6_.3) | copy-start | bytes 196612
  208.4 38.2 %collective-permute-start.17 = (f32[8,128]{1,0:T(8,128)S(1)}, f32[8,128]{1,0:T(8,128)S(1)}, u32[]{:S(2)}, u32[]{:S(2)}) collective-permute-start(f32[8,128]{1,0:T(8,128)S(1)} %add.11.refs_0_), channel_id=1, source_target_pairs={{0,12},{2,14},{4,8},{6,10},{8,4},{10,6},{12,0},{14,2},{1,13},{3,15... | collective-permute-start | bytes 12296 | tf_op jit(solution)/shard_map/ppermute | solution.py:546
  209.8 36.9 %collective-permute-start.16 = (f32[8,128]{1,0:T(8,128)S(1)}, f32[8,128]{1,0:T(8,128)S(1)}, u32[]{:S(2)}, u32[]{:S(2)}) collective-permute-start(f32[8,128]{1,0:T(8,128)S(1)} %add.11.refs_0_), channel_id=1, source_target_pairs={{0,4},{2,6},{4,0},{6,2},{8,12},{10,14},{12,8},{14,10},{1,5},{3,7},... | collective-permute-start | bytes 12296 | tf_op jit(solution)/shard_map/ppermute | solution.py:546
  212.4 34.3 %collective-permute-start.15 = (f32[8,128]{1,0:T(8,128)S(1)}, f32[8,128]{1,0:T(8,128)S(1)}, u32[]{:S(2)}, u32[]{:S(2)}) collective-permute-start(f32[8,128]{1,0:T(8,128)S(1)} %add.11.refs_0_), channel_id=1, source_target_pairs={{0,8},{2,10},{4,12},{6,14},{8,0},{10,2},{12,4},{14,6},{1,9},{3,11}... | collective-permute-start | bytes 12296 | tf_op jit(solution)/shard_map/ppermute | solution.py:546

commit v7 on v6

--- a/solution.py
+++ b/solution.py
@@ -11,7 +11,7 @@
 adapter_scale = 2.0 / 0.9
 bf16 = jnp.bfloat16
 f32 = jnp.float32
-vmem_limit = 48 * 1024 * 1024
+vmem_limit = 24 * 1024 * 1024
 vmem_full = 62 * 1024 * 1024
 strips = 8
 paired_step = 4
@@ -204,8 +204,8 @@
         dropped = hidden * side_ref[rows, :]
         low_t += dot(side_ref[pair, :], dropped, ((1,), (1,))).astype(bf16).astype(f32)
         o_ref[rows, :] = hidden
-        o_ref[pair, :] = dot(side_ref[own, :], dropped).astype(bf16)
     o_ref[own, :] = low_t.astype(bf16)
+    o_ref[picks * block + rank :, :] = side_ref[own, :]
 
 
 def output_terms_kernel(ids, z_ref, dy_ref, o_ref, *, chunk, n):
@@ -246,36 +246,42 @@
         o_ref[:, s * chunk : (s + 1) * chunk] = c_ref[s]
 
 
-def join_copies_kernel(c_ref, o_ref, held, loads, stores, *, chunk, n):
-    into = [pltpu.make_async_copy(c_ref.at[s], held.at[s], loads.at[s]) for s in range(n)]
-    out = [
-        pltpu.make_async_copy(held.at[s], o_ref.at[:, pl.ds(s * chunk, chunk)], stores.at[s])
+def join_copies_kernel(c_ref, o_ref, stores, *, chunk, n):
+    copies = [
+        pltpu.make_async_copy(c_ref.at[s], o_ref.at[:, pl.ds(s * chunk, chunk)], stores.at[s])
         for s in range(n)
     ]
-    for copy in into:
+    for copy in copies:
         copy.start()
-    for first, second in zip(into, out):
-        first.wait()
-        second.start()
-    for copy in out:
+    for copy in copies:
         copy.wait()
 
 
-def gradients_kernel(ids, active, counts, *refs, orders, picks, runs, n):
-    term_refs, (part_ref, ga_ref, gb_ref, sq_ref) = refs[:-4], refs[-4:]
+def gradients_kernel(ids, active, counts, seeds, order, *refs, sizes, block, picks, rank, runs, n):
+    h_refs, (tile_ref, part_ref, ga_ref, gb_ref, sq_ref) = refs[:-5], refs[-5:]
     me = ids[2]
     per_run = n // runs
     ga_ref[...] = jnp.zeros_like(ga_ref)
-    for i, order in enumerate(orders):
-        for s, q in enumerate(order):
-            t = jnp.bitwise_xor(me, q)
-            for k in range(picks):
-
-                @pl.when((active[t, k] == me) & (k < counts[t]))
-                def _():
-                    run = t * runs // n
-                    ga_ref[run] = ga_ref[run] + term_refs[i * picks + k][s].astype(f32)
-
+
+    def add(h_ref, base, s, carry):
+        t = jnp.bitwise_xor(me, order[base + s])
+        run = lax.div(t * runs, n)
+        tile = lax.rem(seeds[run] + t + 3 * me, tile_ref.shape[0])
+        for k in range(picks):
+
+            @pl.when((active[t, k] == me) & (k < counts[t]))
+            def _():
+                kept = tile_ref[tile].astype(f32).astype(bf16)
+                dropped = h_ref[s, k * block : (k + 1) * block, :] * kept
+                dz_t = h_ref[s, picks * block + rank : picks * block + 2 * rank, :]
+                ga_ref[run] = ga_ref[run] + dot(dz_t, dropped)
+
+        return carry
+
+    base = 0
+    for h_ref, size in zip(h_refs, sizes):
+        lax.fori_loop(0, size, functools.partial(add, h_ref, base), 0)
+        base += size
     for r in range(runs):
         total = part_ref[r * per_run].astype(f32)
         for q in range(1, per_run):
@@ -341,6 +347,7 @@
     sizes = dict(chunk=chunk, n=n)
 
     anywhere = pl.BlockSpec(memory_space=pl.ANY)
+    vmem = pl.BlockSpec(memory_space=pltpu.VMEM)
     w_send = pl.pallas_call(
         functools.partial(weight_rows_kernel, runs=runs, **sizes),
         out_shape=jax.ShapeDtypeStruct((n, chunk + rank, block), bf16),
@@ -399,6 +406,7 @@
     b_got = lax.ppermute(dm[:, block:], "core", other)
 
     rows = picks * block + rank * (1 + picks)
+    kept_rows = picks * block + 2 * rank
 
     def tile_spec(k):
         def at(i, ids, active, counts, seeds):
@@ -432,10 +440,10 @@
     held = call(
         functools.partial(hidden_kernel, block=block, picks=picks, rank=rank),
         "hidden_values",
-        jax.ShapeDtypeStruct((rows, block), bf16),
+        jax.ShapeDtypeStruct((kept_rows, block), bf16),
         (1,),
         [whole(part) for part in summed] + [whole(side)],
-        pl.BlockSpec((rows, block), lambda i, *_: (0, 0)),
+        pl.BlockSpec((kept_rows, block), lambda i, *_: (0, 0)),
         (ids, counts),
         (*summed, side),
     )
@@ -458,7 +466,7 @@
     stack = jnp.stack(
         [held] + [lax.ppermute(held, "chip", across(m)) for m in (far, near, far + near)]
     )
-    stack, term_b = lax.optimization_barrier((stack, term_b))
+    stack, _ = lax.optimization_barrier((stack, term_b))
     parts_b = lax.all_to_all(term_b, hid, split_axis=0, concat_axis=0, tiled=True)
     pieces = [(stack, [0, far * cores, near * cores, (far + near) * cores])]
     mask = near // 2
@@ -475,22 +483,17 @@
     gathered = [piece for piece, _ in pieces]
     orders = [order for _, order in pieces]
 
-    at_once = lambda a: pl.BlockSpec(a.shape, lambda *_: (0,) * len(a.shape))
     out_chunks = pl.pallas_call(
         functools.partial(
             output_kernel, orders=orders, block=block, picks=picks, rank=rank, runs=runs, n=n
         ),
         out_shape=jax.ShapeDtypeStruct((n, block, chunk), bf16),
-        grid_spec=pltpu.PrefetchScalarGridSpec(
-            num_scalar_prefetch=2,
-            grid=(1,),
-            in_specs=[at_once(a) for a in (*gathered, dm, do, adapter_output_maps)],
-            out_specs=anywhere,
-            scratch_shapes=[
-                pltpu.VMEM((n, block, chunk), bf16),
-                pltpu.SemaphoreType.DMA((n,)),
-            ],
-        ),
+        in_specs=[pl.BlockSpec(memory_space=pltpu.SMEM)] * 2 + [vmem] * (len(gathered) + 3),
+        out_specs=anywhere,
+        scratch_shapes=[
+            pltpu.VMEM((n, block, chunk), bf16),
+            pltpu.SemaphoreType.DMA((n,)),
+        ],
         compiler_params=pltpu.CompilerParams(vmem_limit_bytes=vmem_limit),
         name="output_columns",
     )(ids, active, *gathered, dm, do, adapter_output_maps)
@@ -499,14 +502,10 @@
         output = pl.pallas_call(
             functools.partial(join_copies_kernel, **sizes),
             out_shape=jax.ShapeDtypeStruct((block, model), bf16),
-            in_specs=[anywhere],
+            in_specs=[vmem],
             out_specs=anywhere,
-            scratch_shapes=[
-                pltpu.VMEM((n, block, chunk), bf16),
-                pltpu.SemaphoreType.DMA((n,)),
-                pltpu.SemaphoreType.DMA((n,)),
-            ],
-            compiler_params=pltpu.CompilerParams(vmem_limit_bytes=vmem_full),
+            scratch_shapes=[pltpu.SemaphoreType.DMA((n,))],
+            compiler_params=pltpu.CompilerParams(vmem_limit_bytes=8 * 1024 * 1024),
             name="join_columns",
         )(out_cols)
     else:
@@ -521,21 +520,26 @@
             (out_cols,),
         )
 
-    at_rows = lambda a, k: pl.BlockSpec(
-        (a.shape[0], rank, block), lambda i, *_: (0, picks * block // rank + 1 + k, 0)
-    )
     maps_a = jax.ShapeDtypeStruct(adapter_input_maps.shape, f32)
     maps_b = jax.ShapeDtypeStruct(adapter_output_maps.shape, f32)
     lanes = jax.ShapeDtypeStruct((runs, block), f32)
     grad_a, grad_b, squares = call(
-        functools.partial(gradients_kernel, orders=orders, picks=picks, runs=runs, n=n),
+        functools.partial(
+            gradients_kernel,
+            sizes=[len(order) for order in orders],
+            block=block,
+            picks=picks,
+            rank=rank,
+            runs=runs,
+            n=n,
+        ),
         "gradients",
         (maps_a, maps_b, lanes),
         (1,),
-        [at_rows(a, k) for a in gathered for k in range(picks)] + [whole(parts_b)],
+        [whole(a) for a in (*gathered, dropout_tiles, parts_b)],
         [whole(maps_a), whole(maps_b), whole(lanes)],
-        (ids, active, counts),
-        tuple(a for a in gathered for _ in range(picks)) + (parts_b,),
+        (ids, active, counts, seeds, jnp.array(sum(orders, []), jnp.int32)),
+        (*gathered, dropout_tiles, parts_b),
     )
     squares = squares + lax.ppermute(squares, "core", other)
     mask = 1

time: 251 us -> 250 us (level)
  local copies, waits for them, and re-layouts: 10 us -> 14.7 us
  waiting for transfers between devices: 155 us -> 151 us
    unnamed x39 -> x59, local copies, waits for them, and re-layouts: 10 us -> 14.7 us
    ppermute x1, waiting for transfers between devices: 7.02 us -> 3.41 us  [body(): squares = squares + lax.ppermute(squares, 'chip', across(mask))]
  transfers between devices with their start and end apart: 24 -> 24, of which waited for: 15 -> 15; matrix products, arithmetic and copies ran while one was open for 0% -> 0% of each run, Pallas kernels for 10% -> 9%
where the time goes in v7:
time: 250 us; the launch traced here: 247 us
  waiting for transfers between devices  151 us (60%)
  starting transfers between devices  51.7 us (21%)
  Pallas kernels  28.3 us (11%)
  local copies, waits for them, and re-layouts  14.7 us (6%)
    all_to_all x1, waiting for transfers between devices, body(): wm = lax.all_to_all(w_send, hid, split_axis=0, concat_axis=0, tiled=True)  43.3 us
    all_to_all x1, waiting for transfers between devices, body(): xb = lax.all_to_all(x_send, hid, split_axis=0, concat_axis=0, tiled=True)  41 us
    all_to_all x1, waiting for transfers between devices, body(): lax.all_to_all(out_chunks, hid, split_axis=0, concat_axis=0, tiled=True)  31.6 us
    pallas_call x9, Pallas kernels, call(): pl.pallas_call(kernel, out_shape=out, grid_spec=pltpu.PrefetchScalarGridS...  16.7 us
    all_to_all x1, waiting for transfers between devices, body(): dm = lax.all_to_all(d_send, hid, split_axis=0, concat_axis=0, tiled=True)  16 us
    unnamed x59, local copies, waits for them, and re-layouts  14.7 us
    all_to_all x1, starting transfers between devices, body(): lax.all_to_all(term_b, hid, split_axis=0, concat_axis=0, tiled=True)  7.92 us
    ppermute x3, waiting for transfers between devices, body(): lax.ppermute(paired[c], 'chip', across(2 * c))  7.23 us
  transfers between devices with their start and end apart: 24, of which 15 were waited for; matrix products, arithmetic and copies ran while one was open for 0% of the time, Pallas kernels for 9%

profile of v7, /device:TPU:9, one launch (start us, length us, event | category | flops | bytes accessed | tf_op | source)
XLA Modules:
  0.0 247.0 jit_solution(5936714129607299692)
XLA Ops:
  0.6 3.2 %weight_rows.1 = bf16[16,528,128]{2,1,0:T(8,128)(2,1)} custom-call(bf16[8192,128]{1,0:T(8,128)(2,1)} %gate_ref.1, bf16[8192,128]{1,0:T(8,128)(2,1)} %up_ref.1, f32[8,16,128]{2,1,0:T(8,128)} %refs_4_.5), custom_call_target="tpu_custom_call" | custom-call | tf_op jit(solution)/shard_map/weight_rows/pallas_call | solution.py:351
  3.9 6.6 %all-to-all-start.1 = ((bf16[16,528,128]{2,1,0:T(8,128)(2,1)}), bf16[16,528,128]{2,1,0:T(8,128)(2,1)S(1)}, u32[]{:S(2)}, u32[]{:S(2)}) async-start(bf16[16,528,128]{2,1,0:T(8,128)(2,1)} %weight_rows.1), calls=%async_computation.1 | async-start | bytes 4325376 | tf_op jit(solution)/shard_map/all_to_all | solution.py:365
  10.5 1.6 copy-done.8
  12.1 1.0 token_columns.1
  13.1 1.3 copy-done
  14.5 43.3 %all-to-all-done.1.wm_ref.refs_5_.refs_6_ = bf16[16,528,128]{2,1,0:T(8,128)(2,1)S(1)} async-done(((bf16[16,528,128]{2,1,0:T(8,128)(2,1)}), bf16[16,528,128]{2,1,0:T(8,128)(2,1)S(1)}, u32[]{:S(2)}, u32[]{:S(2)}) %all-to-all-start.1) | async-done | bytes 2162720 | tf_op jit(solution)/shard_map/all_to_all | solution.py:365
  57.8 6.4 %all-to-all-start = ((bf16[16,128,512]{2,1,0:T(8,128)(2,1)}), bf16[16,128,512]{2,1,0:T(8,128)(2,1)}, u32[]{:S(2)}, u32[]{:S(2)}) async-start(bf16[16,128,512]{2,1,0:T(8,128)(2,1)} %copy-done), calls=%async_computation | async-start | bytes 4194304 | tf_op jit(solution)/shard_map/all_to_all | solution.py:378
  64.2 1.3 collective-permute-start
  65.5 1.6 copy-done.9
  67.0 1.2 down_columns.1
  68.3 1.0 copy-done.3
  69.3 41.0 %all-to-all-done.x_ref = bf16[16,128,512]{2,1,0:T(8,128)(2,1)} async-done(((bf16[16,128,512]{2,1,0:T(8,128)(2,1)}), bf16[16,128,512]{2,1,0:T(8,128)(2,1)}, u32[]{:S(2)}, u32[]{:S(2)}) %all-to-all-start) | async-done | bytes 2097184 | tf_op jit(solution)/shard_map/all_to_all | solution.py:378
  110.3 6.3 %all-to-all-start.2 = ((bf16[16,144,256]{2,1,0:T(8,128)(2,1)}), bf16[16,144,256]{2,1,0:T(8,128)(2,1)S(1)}, u32[]{:S(2)}, u32[]{:S(2)}) async-start(bf16[16,144,256]{2,1,0:T(8,128)(2,1)} %copy-done.3), calls=%async_computation.2 | async-start | bytes 2359296 | tf_op jit(solution)/shard_map/all_to_all | solution.py:391
  116.7 3.7 %gate_up_partial.3 = bf16[8,2,128,256]{3,2,1,0:T(8,128)(2,1)S(1)} custom-call(s32[3]{0:T(128)S(1)} %pad_add_fusion.ids, s32[16,2]{1,0:T(8,128)S(1)} %copy.26.active, bf16[16,128,512]{2,1,0:T(8,128)(2,1)} %all-to-all-done.x_ref, bf16[16,528,128]{2,1,0:T(8,128)(2,1)S(1)} %all-to-all-done.1.wm_ref.refs_5_.refs_6_, bf16[16,528,128]{2,1,0:T(8,128)(2,1)} %collective-permute-done.wo_ref), custom_call_target="tpu_custom_call" | custom-call | flops 536870912 | bytes 7471104 | tf_op jit(solution)/shard_map/gate_up_partial/pallas_call | solution.py:28
  120.8 3.7 %gate_up_partial.2.kept_ref = bf16[8,2,128,256]{3,2,1,0:T(8,128)(2,1)S(1)} custom-call(s32[3]{0:T(128)S(1)} %pad_add_fusion.ids, s32[16,2]{1,0:T(8,128)S(1)} %copy.26.active, bf16[16,128,512]{2,1,0:T(8,128)(2,1)} %all-to-all-done.x_ref, bf16[16,528,128]{2,1,0:T(8,128)(2,1)S(1)} %all-to-all-done.1.wm_ref.refs_5_.refs_6_, ...), custom_call_target="tpu_custom_call" | custom-call | flops 536870912 | bytes 7471104 | tf_op jit(solution)/shard_map/gate_up_partial/pallas_call | solution.py:28
  124.6 1.7 pair_sums.2
  127.0 1.2 collective-permute-start.2
  128.2 16.0 %all-to-all-done.2.refs_0_.refs_4_ = bf16[16,144,256]{2,1,0:T(8,128)(2,1)S(1)} async-done(((bf16[16,144,256]{2,1,0:T(8,128)(2,1)}), bf16[16,144,256]{2,1,0:T(8,128)(2,1)S(1)}, u32[]{:S(2)}, u32[]{:S(2)}) %all-to-all-start.2) | async-done | bytes 1179680 | tf_op jit(solution)/shard_map/all_to_all | solution.py:391
  144.2 1.9 collective-permute-done.2.got_ref
  146.1 1.3 collective-permute-start.18
  147.4 1.3 collective-permute-start.6
  148.7 1.0 copy-done.15
  149.7 1.9 pair_sums.3
  151.7 3.3 %collective-permute-start.4 = (bf16[1,2,128,256]{3,2,1,0:T(8,128)(2,1)S(1)}, bf16[1,2,128,256]{3,2,1,0:T(8,128)(2,1)S(1)}, u32[]{:S(2)}, u32[]{:S(2)}) collective-permute-start(bf16[1,2,128,256]{3,2,1,0:T(8,128)(2,1)S(1)} %get-tuple-element.36), channel_id=1, source_target_pairs={{0,8},{2,10},{4,12},{6,14},{8,0},{10,2},{12,4},{14,6},{1,9},{3,11}... | collective-permute-start | bytes 393224 | tf_op jit(solution)/shard_map/ppermute | solution.py:402
  155.0 1.6 copy-done.1
  156.6 0.9 copy-done.4
  157.5 1.5 side_rows.1.refs_4_
  159.0 4.4 %collective-permute-done.4.refs_2_ = bf16[1,2,128,256]{3,2,1,0:T(8,128)(2,1)S(1)} collective-permute-done((bf16[1,2,128,256]{3,2,1,0:T(8,128)(2,1)S(1)}, bf16[1,2,128,256]{3,2,1,0:T(8,128)(2,1)S(1)}, u32[]{:S(2)}, u32[]{:S(2)}) %collective-permute-start.4) | collective-permute-done | bytes 131104 | tf_op jit(solution)/shard_map/ppermute | solution.py:402
  163.4 2.8 %collective-permute-done.5.refs_3_ = bf16[1,2,128,256]{3,2,1,0:T(8,128)(2,1)S(1)} collective-permute-done((bf16[1,2,128,256]{3,2,1,0:T(8,128)(2,1)S(1)}, bf16[1,2,128,256]{3,2,1,0:T(8,128)(2,1)S(1)}, u32[]{:S(2)}, u32[]{:S(2)}) %collective-permute-start.5) | collective-permute-done | bytes 131104 | tf_op jit(solution)/shard_map/ppermute | solution.py:402
  167.0 2.3 collective-permute-start.9
  169.3 1.2 collective-permute-start.7
  170.6 1.6 output_terms.1
  174.1 1.0 collective-permute-start.10
  175.2 7.9 %all-to-all-start.3 = ((bf16[16,16,512]{2,1,0:T(8,128)(2,1)}), bf16[16,16,512]{2,1,0:T(8,128)(2,1)S(1)}, u32[]{:S(2)}, u32[]{:S(2)}) async-start(bf16[16,16,512]{2,1,0:T(8,128)(2,1)} %output_terms.1), calls=%async_computation.3 | async-start | bytes 524288 | tf_op jit(solution)/shard_map/all_to_all | solution.py:470
  183.6 1.0 collective-permute-done.11.refs_2_
  185.1 3.4 %output_columns.1 = bf16[16,128,512]{2,1,0:T(8,128)(2,1)} custom-call(s32[3]{0:T(128)S(1)} %pad_add_fusion.ids, s32[16,2]{1,0:T(8,128)S(1)} %copy.26.active, bf16[4,288,128]{2,1,0:T(8,128)(2,1)S(1)} %pad_maximum_fusion.refs_0_, bf16[4,288,128]{2,1,0:T(8,128)(2,1)S(1)} %collective-permute-done.10.refs_1_, ...), custom_call_target="tpu_custom_call" | custom-call | tf_op jit(solution)/shard_map/output_columns/pallas_call | solution.py:486
  189.2 2.6 %all-to-all-done.3.refs_5_ = bf16[16,16,512]{2,1,0:T(8,128)(2,1)S(1)} async-done(((bf16[16,16,512]{2,1,0:T(8,128)(2,1)}), bf16[16,16,512]{2,1,0:T(8,128)(2,1)S(1)}, u32[]{:S(2)}, u32[]{:S(2)}) %all-to-all-start.3) | async-done | bytes 262176 | tf_op jit(solution)/shard_map/all_to_all | solution.py:470
  192.5 5.0 %all-to-all-start.4 = ((bf16[16,128,512]{2,1,0:T(8,128)(2,1)}), bf16[16,128,512]{2,1,0:T(8,128)(2,1)S(1)}, u32[]{:S(2)}, u32[]{:S(2)}) async-start(bf16[16,128,512]{2,1,0:T(8,128)(2,1)} %output_columns.1), calls=%async_computation.4 | async-start | bytes 4194304 | tf_op jit(solution)/shard_map/all_to_all | solution.py:500
  197.5 1.0 copy-done.11
  198.4 0.9 copy-done.13
  199.4 1.4 gradients.1
  203.4 1.2 collective-permute-start.14
  204.6 3.4 %collective-permute-done.14 = f32[8,128]{1,0:T(8,128)S(1)} collective-permute-done((f32[8,128]{1,0:T(8,128)S(1)}, f32[8,128]{1,0:T(8,128)S(1)}, u32[]{:S(2)}, u32[]{:S(2)}) %collective-permute-start.14) | collective-permute-done | bytes 4128 | tf_op jit(solution)/shard_map/ppermute | solution.py:547
  208.1 1.3 collective-permute-start.17
  209.4 2.6 %collective-permute-start.16 = (f32[8,128]{1,0:T(8,128)S(1)}, f32[8,128]{1,0:T(8,128)S(1)}, u32[]{:S(2)}, u32[]{:S(2)}) collective-permute-start(f32[8,128]{1,0:T(8,128)S(1)} %add.11.refs_0_), channel_id=1, source_target_pairs={{0,4},{2,6},{4,0},{6,2},{8,12},{10,14},{12,8},{14,10},{1,5},{3,7},... | collective-permute-start | bytes 12296 | tf_op jit(solution)/shard_map/ppermute | solution.py:550
  212.0 31.6 %all-to-all-done.4.c_ref = bf16[16,128,512]{2,1,0:T(8,128)(2,1)S(1)} async-done(((bf16[16,128,512]{2,1,0:T(8,128)(2,1)}), bf16[16,128,512]{2,1,0:T(8,128)(2,1)S(1)}, u32[]{:S(2)}, u32[]{:S(2)}) %all-to-all-start.4) | async-done | bytes 2097184 | tf_op jit(solution)/shard_map/all_to_all | solution.py:500
  243.7 1.4 join_columns.1
  245.2 1.8 adamw.1
  (78 shorter events, 9.2 us)
Async XLA Ops:
  3.9 53.9 %all-to-all-start.1 = ((bf16[16,528,128]{2,1,0:T(8,128)(2,1)}), bf16[16,528,128]{2,1,0:T(8,128)(2,1)S(1)}, u32[]{:S(2)}, u32[]{:S(2)}) async-start(bf16[16,528,128]{2,1,0:T(8,128)(2,1)} %weight_rows.1), calls=%async_computation.1 | async-start | bytes 4325376 | tf_op jit(solution)/shard_map/all_to_all | solution.py:365
  10.5 1.6 copy-start.8
  13.1 1.3 copy-start
  14.5 51.0 %copy-start.6 = (f32[8,16,512]{2,1,0:T(8,128)S(1)}, f32[8,16,512]{2,1,0:T(8,128)}, u32[]{:S(2)}) copy-start(f32[8,16,512]{2,1,0:T(8,128)} %refs_8_.1) | copy-start | bytes 786436
  57.8 52.5 %all-to-all-start = ((bf16[16,128,512]{2,1,0:T(8,128)(2,1)}), bf16[16,128,512]{2,1,0:T(8,128)(2,1)}, u32[]{:S(2)}, u32[]{:S(2)}) async-start(bf16[16,128,512]{2,1,0:T(8,128)(2,1)} %copy-done), calls=%async_computation | async-start | bytes 4194304 | tf_op jit(solution)/shard_map/all_to_all | solution.py:378
  64.2 52.5 %collective-permute-start = (bf16[16,528,128]{2,1,0:T(8,128)(2,1)S(1)}, bf16[16,528,128]{2,1,0:T(8,128)(2,1)}, u32[]{:S(2)}, u32[]{:S(2)}) collective-permute-start(bf16[16,528,128]{2,1,0:T(8,128)(2,1)S(1)} %all-to-all-done.1.wm_ref.refs_5_.refs_6_), channel_id=1, source_target_pairs={{0,16},{16,0},{1,17},{17,1},{2,18},{18,2},{3,19},{19,3},{4,20},{20... | collective-permute-start | bytes 6488072 | tf_op jit(solution)/shard_map/ppermute | solution.py:366
  65.5 1.6 copy-start.9
  67.0 49.6 %copy-start.28 = (s32[16,2]{0,1:T(2,128)S(1)}, s32[16,2]{0,1:T(2,128)}, u32[]{:S(2)}) copy-start(s32[16,2]{0,1:T(2,128)} %param.27) | copy-start | bytes 388
  68.3 1.0 copy-start.3
  110.3 33.9 %all-to-all-start.2 = ((bf16[16,144,256]{2,1,0:T(8,128)(2,1)}), bf16[16,144,256]{2,1,0:T(8,128)(2,1)S(1)}, u32[]{:S(2)}, u32[]{:S(2)}) async-start(bf16[16,144,256]{2,1,0:T(8,128)(2,1)} %copy-done.3), calls=%async_computation.2 | async-start | bytes 2359296 | tf_op jit(solution)/shard_map/all_to_all | solution.py:391
  120.4 4.1 %collective-permute-start.1 = (bf16[8,2,128,256]{3,2,1,0:T(8,128)(2,1)S(1)}, bf16[8,2,128,256]{3,2,1,0:T(8,128)(2,1)S(1)}, u32[]{:S(2)}, u32[]{:S(2)}) collective-permute-start(bf16[8,2,128,256]{3,2,1,0:T(8,128)(2,1)S(1)} %gate_up_partial.3), channel_id=1, source_target_pairs={{0,1},{1,0},{2,3},{3,2},{4,5},{5,4},{6,7},{7,6},{8,9},{9,8},{10,11... | collective-permute-start | bytes 3145736 | tf_op jit(solution)/shard_map/ppermute | solution.py:396
  124.5 30.4 %copy-start.25 = (s32[16]{0:T(128)S(1)}, s32[16]{0:T(128)}, u32[]{:S(2)}) copy-start(s32[16]{0:T(128)} %counts.5) | copy-start | bytes 196
  124.5 30.4 %copy-start.26 = (s32[8]{0:T(128)S(1)}, s32[8]{0:T(128)}, u32[]{:S(2)}) copy-start(s32[8]{0:T(128)} %seeds.3) | copy-start | bytes 100
  127.0 19.0 %collective-permute-start.2 = (bf16[4,2,128,256]{3,2,1,0:T(8,128)(2,1)}, bf16[4,2,128,256]{3,2,1,0:T(8,128)(2,1)}, u32[]{:S(2)}, u32[]{:S(2)}) collective-permute-start(bf16[4,2,128,256]{3,2,1,0:T(8,128)(2,1)} %get-tuple-element.33), channel_id=1, source_target_pairs={{0,2},{2,0},{4,6},{6,4},{8,10},{10,8},{12,14},{14,12},{1,3},{3,1},... | collective-permute-start | bytes 1572872 | tf_op jit(solution)/shard_map/ppermute | solution.py:399
  146.1 39.0 %collective-permute-start.18 = (bf16[16,144,256]{2,1,0:T(8,128)(2,1)S(1)}, bf16[16,144,256]{2,1,0:T(8,128)(2,1)}, u32[]{:S(2)}, u32[]{:S(2)}) collective-permute-start(bf16[16,144,256]{2,1,0:T(8,128)(2,1)S(1)} %all-to-all-done.2.refs_0_.refs_4_), channel_id=1, source_target_pairs={{0,16},{16,0},{1,17},{17,1},{2,18},{18,2},{3,19},{19,3},{4,20},{20... | collective-permute-start | bytes 3538952 | tf_op jit(solution)/shard_map/ppermute | solution.py:405
  147.4 7.6 %collective-permute-start.6 = (bf16[16,16,256]{2,1,0:T(8,128)(2,1)S(1)}, bf16[16,16,256]{2,1,0:T(8,128)(2,1)S(1)}, u32[]{:S(2)}, u32[]{:S(2)}) collective-permute-start(bf16[16,16,256]{2,1,0:T(8,128)(2,1)S(1)} %slice.3), channel_id=1, source_target_pairs={{0,1},{1,0},{2,3},{3,2},{4,5},{5,4},{6,7},{7,6},{8,9},{9,8},{10,11... | collective-permute-start | bytes 393224 | tf_op jit(solution)/shard_map/ppermute | solution.py:406
  148.7 1.0 copy-start.15
  151.6 7.4 %collective-permute-start.3 = (bf16[1,2,128,256]{3,2,1,0:T(8,128)(2,1)S(1)}, bf16[1,2,128,256]{3,2,1,0:T(8,128)(2,1)S(1)}, u32[]{:S(2)}, u32[]{:S(2)}) collective-permute-start(bf16[1,2,128,256]{3,2,1,0:T(8,128)(2,1)S(1)} %get-tuple-element.35), channel_id=1, source_target_pairs={{0,4},{2,6},{4,0},{6,2},{8,12},{10,14},{12,8},{14,10},{1,5},{3,7},... | collective-permute-start | bytes 393224 | tf_op jit(solution)/shard_map/ppermute | solution.py:402
  151.7 11.7 %collective-permute-start.4 = (bf16[1,2,128,256]{3,2,1,0:T(8,128)(2,1)S(1)}, bf16[1,2,128,256]{3,2,1,0:T(8,128)(2,1)S(1)}, u32[]{:S(2)}, u32[]{:S(2)}) collective-permute-start(bf16[1,2,128,256]{3,2,1,0:T(8,128)(2,1)S(1)} %get-tuple-element.36), channel_id=1, source_target_pairs={{0,8},{2,10},{4,12},{6,14},{8,0},{10,2},{12,4},{14,6},{1,9},{3,11}... | collective-permute-start | bytes 393224 | tf_op jit(solution)/shard_map/ppermute | solution.py:402
  155.0 11.3 %collective-permute-start.5 = (bf16[1,2,128,256]{3,2,1,0:T(8,128)(2,1)S(1)}, bf16[1,2,128,256]{3,2,1,0:T(8,128)(2,1)S(1)}, u32[]{:S(2)}, u32[]{:S(2)}) collective-permute-start(bf16[1,2,128,256]{3,2,1,0:T(8,128)(2,1)S(1)} %get-tuple-element.37), channel_id=1, source_target_pairs={{0,12},{2,14},{4,8},{6,10},{8,4},{10,6},{12,0},{14,2},{1,13},{3,15... | collective-permute-start | bytes 393224 | tf_op jit(solution)/shard_map/ppermute | solution.py:402
  155.0 1.6 copy-start.1
  156.6 0.9 copy-start.4
  157.5 13.0 %copy-start.2 = (bf16[128,8192]{1,0:T(8,128)(2,1)S(1)}, bf16[128,8192]{1,0:T(8,128)(2,1)}, u32[]{:S(2)}) copy-start(bf16[128,8192]{1,0:T(8,128)(2,1)} %dy_ref.1) | copy-start | bytes 6291460
  166.2 18.9 %copy-start.7 = (f32[8,16,512]{2,1,0:T(8,128)S(1)}, f32[8,16,512]{2,1,0:T(8,128)}, u32[]{:S(2)}) copy-start(f32[8,16,512]{2,1,0:T(8,128)} %refs_8_.1) | copy-start | bytes 786436
  167.0 5.6 %collective-permute-start.9 = (bf16[288,128]{1,0:T(8,128)(2,1)S(1)}, bf16[288,128]{1,0:T(8,128)(2,1)S(1)}, u32[]{:S(2)}, u32[]{:S(2)}) collective-permute-start(bf16[288,128]{1,0:T(8,128)(2,1)S(1)} %hidden_values.1.z_ref), channel_id=1, source_target_pairs={{0,12},{2,14},{4,8},{6,10},{8,4},{10,6},{12,0},{14,2},{1,13},{3,15... | collective-permute-start | bytes 221192 | tf_op jit(solution)/shard_map/ppermute | solution.py:467
  169.3 3.9 %collective-permute-start.8 = (bf16[288,128]{1,0:T(8,128)(2,1)S(1)}, bf16[288,128]{1,0:T(8,128)(2,1)S(1)}, u32[]{:S(2)}, u32[]{:S(2)}) collective-permute-start(bf16[288,128]{1,0:T(8,128)(2,1)S(1)} %hidden_values.1.z_ref), channel_id=1, source_target_pairs={{0,4},{2,6},{4,0},{6,2},{8,12},{10,14},{12,8},{14,10},{1,5},{3,7},... | collective-permute-start | bytes 221192 | tf_op jit(solution)/shard_map/ppermute | solution.py:467
  169.3 4.8 %collective-permute-start.7 = (bf16[288,128]{1,0:T(8,128)(2,1)S(1)}, bf16[288,128]{1,0:T(8,128)(2,1)S(1)}, u32[]{:S(2)}, u32[]{:S(2)}) collective-permute-start(bf16[288,128]{1,0:T(8,128)(2,1)S(1)} %hidden_values.1.z_ref), channel_id=1, source_target_pairs={{0,8},{2,10},{4,12},{6,14},{8,0},{10,2},{12,4},{14,6},{1,9},{3,11}... | collective-permute-start | bytes 221192 | tf_op jit(solution)/shard_map/ppermute | solution.py:467
  174.1 9.3 %collective-permute-start.10 = (bf16[4,288,128]{2,1,0:T(8,128)(2,1)S(1)}, bf16[4,288,128]{2,1,0:T(8,128)(2,1)S(1)}, u32[]{:S(2)}, u32[]{:S(2)}) collective-permute-start(bf16[4,288,128]{2,1,0:T(8,128)(2,1)S(1)} %pad_maximum_fusion.refs_0_), channel_id=1, source_target_pairs={{0,2},{2,0},{4,6},{6,4},{8,10},{10,8},{12,14},{14,12},{1,3},{3,1},... | collective-permute-start | bytes 884744 | tf_op jit(solution)/shard_map/ppermute | solution.py:475
  175.2 16.6 %all-to-all-start.3 = ((bf16[16,16,512]{2,1,0:T(8,128)(2,1)}), bf16[16,16,512]{2,1,0:T(8,128)(2,1)S(1)}, u32[]{:S(2)}, u32[]{:S(2)}) async-start(bf16[16,16,512]{2,1,0:T(8,128)(2,1)} %output_terms.1), calls=%async_computation.3 | async-start | bytes 524288 | tf_op jit(solution)/shard_map/all_to_all | solution.py:470
  183.1 1.6 collective-permute-start.11
  183.4 1.6 collective-permute-start.12
  189.2 8.3 %copy-start.5 = (s32[4,128,128]{2,1,0:T(8,128)S(1)}, s32[4,128,128]{2,1,0:T(8,128)}, u32[]{:S(2)}) copy-start(s32[4,128,128]{2,1,0:T(8,128)} %refs_4_.4) | copy-start | bytes 786436
  189.2 8.3 %copy-start.27 = (s32[16]{0:T(128)S(1)}, s32[16]{0:T(128)}, u32[]{:S(2)}) copy-start(s32[16]{0:T(128)} %constant.16.clone.order) | copy-start | bytes 196
  192.5 51.2 %all-to-all-start.4 = ((bf16[16,128,512]{2,1,0:T(8,128)(2,1)}), bf16[16,128,512]{2,1,0:T(8,128)(2,1)S(1)}, u32[]{:S(2)}, u32[]{:S(2)}) async-start(bf16[16,128,512]{2,1,0:T(8,128)(2,1)} %output_columns.1), calls=%async_computation.4 | async-start | bytes 4194304 | tf_op jit(solution)/shard_map/all_to_all | solution.py:500
  197.5 1.0 copy-start.11
  198.4 0.9 copy-start.13
  202.2 1.2 collective-permute-start.13
  203.4 4.6 %collective-permute-start.14 = (f32[8,128]{1,0:T(8,128)S(1)}, f32[8,128]{1,0:T(8,128)S(1)}, u32[]{:S(2)}, u32[]{:S(2)}) collective-permute-start(f32[8,128]{1,0:T(8,128)S(1)} %add.10), channel_id=1, source_target_pairs={{0,2},{2,0},{4,6},{6,4},{8,10},{10,8},{12,14},{14,12},{1,3},{3,1},... | collective-permute-start | bytes 12296 | tf_op jit(solution)/shard_map/ppermute | solution.py:547
  208.0 37.1 %copy-start.16 = (f32[8,16,128]{2,1,0:T(8,128)S(1)}, f32[8,16,128]{2,1,0:T(8,128)}, u32[]{:S(2)}) copy-start(f32[8,16,128]{2,1,0:T(8,128)} %refs_4_.5) | copy-start | bytes 196612
  208.0 37.1 %copy-start.17 = (f32[8,16,512]{2,1,0:T(8,128)S(1)}, f32[8,16,512]{2,1,0:T(8,128)}, u32[]{:S(2)}) copy-start(f32[8,16,512]{2,1,0:T(8,128)} %refs_9_.1) | copy-start | bytes 786436
  208.0 37.1 %copy-start.18 = (f32[8,16,512]{2,1,0:T(8,128)S(1)}, f32[8,16,512]{2,1,0:T(8,128)}, u32[]{:S(2)}) copy-start(f32[8,16,512]{2,1,0:T(8,128)} %refs_10_.1) | copy-start | bytes 786436
  208.0 37.1 %copy-start.20 = (f32[8,16,512]{2,1,0:T(8,128)S(1)}, f32[8,16,512]{2,1,0:T(8,128)}, u32[]{:S(2)}) copy-start(f32[8,16,512]{2,1,0:T(8,128)} %copy-done.19) | copy-start | bytes 786436
  208.0 37.1 %copy-start.21 = (f32[8,16,128]{2,1,0:T(8,128)S(1)}, f32[8,16,128]{2,1,0:T(8,128)}, u32[]{:S(2)}) copy-start(f32[8,16,128]{2,1,0:T(8,128)} %refs_5_.1) | copy-start | bytes 196612
  208.0 37.1 %copy-start.22 = (f32[8,16,128]{2,1,0:T(8,128)S(1)}, f32[8,16,128]{2,1,0:T(8,128)}, u32[]{:S(2)}) copy-start(f32[8,16,128]{2,1,0:T(8,128)} %refs_6_.3) | copy-start | bytes 196612
  208.1 37.1 %copy-start.24 = (f32[8,16,128]{2,1,0:T(8,128)S(1)}, f32[8,16,128]{2,1,0:T(8,128)}, u32[]{:S(2)}) copy-start(f32[8,16,128]{2,1,0:T(8,128)} %copy-done.23) | copy-start | bytes 196612
  208.1 37.0 %collective-permute-start.17 = (f32[8,128]{1,0:T(8,128)S(1)}, f32[8,128]{1,0:T(8,128)S(1)}, u32[]{:S(2)}, u32[]{:S(2)}) collective-permute-start(f32[8,128]{1,0:T(8,128)S(1)} %add.11.refs_0_), channel_id=1, source_target_pairs={{0,12},{2,14},{4,8},{6,10},{8,4},{10,6},{12,0},{14,2},{1,13},{3,15... | collective-permute-start | bytes 12296 | tf_op jit(solution)/shard_map/ppermute | solution.py:550
  209.4 35.7 %collective-permute-start.16 = (f32[8,128]{1,0:T(8,128)S(1)}, f32[8,128]{1,0:T(8,128)S(1)}, u32[]{:S(2)}, u32[]{:S(2)}) collective-permute-start(f32[8,128]{1,0:T(8,128)S(1)} %add.11.refs_0_), channel_id=1, source_target_pairs={{0,4},{2,6},{4,0},{6,2},{8,12},{10,14},{12,8},{14,10},{1,5},{3,7},... | collective-permute-start | bytes 12296 | tf_op jit(solution)/shard_map/ppermute | solution.py:550
  212.0 33.1 %collective-permute-start.15 = (f32[8,128]{1,0:T(8,128)S(1)}, f32[8,128]{1,0:T(8,128)S(1)}, u32[]{:S(2)}, u32[]{:S(2)}) collective-permute-start(f32[8,128]{1,0:T(8,128)S(1)} %add.11.refs_0_), channel_id=1, source_target_pairs={{0,8},{2,10},{4,12},{6,14},{8,0},{10,2},{12,4},{14,6},{1,9},{3,11}... | collective-permute-start | bytes 12296 | tf_op jit(solution)/shard_map/ppermute | solution.py:550
  (5 other events, 3.6 us)

commit v8 on v7

--- a/solution.py
+++ b/solution.py
@@ -401,7 +401,7 @@
     summed = [paired[0]] + [
         lax.ppermute(paired[c], "chip", across(2 * c)) for c in range(1, chips // 2)
     ]
-    dm, _ = lax.optimization_barrier((dm, x_got))
+    dm, _ = lax.optimization_barrier((dm, x_sent))
     do = lax.ppermute(dm, "groups", other)
     b_got = lax.ppermute(dm[:, block:], "core", other)
 
@@ -464,11 +464,11 @@
 
     near = chips // 4
     stack = jnp.stack(
-        [held] + [lax.ppermute(held, "chip", across(m)) for m in (far, near, far + near)]
+        [held] + [lax.ppermute(held, "chip", across(m)) for m in (near, far, far + near)]
     )
     stack, _ = lax.optimization_barrier((stack, term_b))
     parts_b = lax.all_to_all(term_b, hid, split_axis=0, concat_axis=0, tiled=True)
-    pieces = [(stack, [0, far * cores, near * cores, (far + near) * cores])]
+    pieces = [(stack, [0, near * cores, far * cores, (far + near) * cores])]
     mask = near // 2
     while mask:
         arrived = [

time: 250 us -> 248 us (level)
  no operation moved by 1% of the time
where the time goes in v8:
time: 248 us; the launch traced here: 245 us
  waiting for transfers between devices  150 us (60%)
  starting transfers between devices  50.8 us (20%)
  Pallas kernels  28.2 us (11%)
  local copies, waits for them, and re-layouts  14.7 us (6%)
    all_to_all x1, waiting for transfers between devices, body(): wm = lax.all_to_all(w_send, hid, split_axis=0, concat_axis=0, tiled=True)  43.3 us
    all_to_all x1, waiting for transfers between devices, body(): xb = lax.all_to_all(x_send, hid, split_axis=0, concat_axis=0, tiled=True)  41 us
    all_to_all x1, waiting for transfers between devices, body(): lax.all_to_all(out_chunks, hid, split_axis=0, concat_axis=0, tiled=True)  31.6 us
    pallas_call x9, Pallas kernels, call(): pl.pallas_call(kernel, out_shape=out, grid_spec=pltpu.PrefetchScalarGridS...  16.6 us
    all_to_all x1, waiting for transfers between devices, body(): dm = lax.all_to_all(d_send, hid, split_axis=0, concat_axis=0, tiled=True)  15.9 us
    unnamed x59, local copies, waits for them, and re-layouts  14.7 us
    all_to_all x1, starting transfers between devices, body(): lax.all_to_all(term_b, hid, split_axis=0, concat_axis=0, tiled=True)  7.96 us
    ppermute x3, waiting for transfers between devices, body(): lax.ppermute(paired[c], 'chip', across(2 * c))  7.17 us
  transfers between devices with their start and end apart: 24, of which 15 were waited for; matrix products, arithmetic and copies ran while one was open for 0% of the time, Pallas kernels for 9%

profile of v8, /device:TPU:9, one launch (start us, length us, event | category | flops | bytes accessed | tf_op | source)
XLA Modules:
  0.0 244.5 jit_solution(16975363480737482649)
XLA Ops:
  0.6 3.2 %weight_rows.1 = bf16[16,528,128]{2,1,0:T(8,128)(2,1)} custom-call(bf16[8192,128]{1,0:T(8,128)(2,1)} %gate_ref.1, bf16[8192,128]{1,0:T(8,128)(2,1)} %up_ref.1, f32[8,16,128]{2,1,0:T(8,128)} %refs_4_.5), custom_call_target="tpu_custom_call" | custom-call | tf_op jit(solution)/shard_map/weight_rows/pallas_call | solution.py:351
  3.9 6.6 %all-to-all-start.1 = ((bf16[16,528,128]{2,1,0:T(8,128)(2,1)}), bf16[16,528,128]{2,1,0:T(8,128)(2,1)S(1)}, u32[]{:S(2)}, u32[]{:S(2)}) async-start(bf16[16,528,128]{2,1,0:T(8,128)(2,1)} %weight_rows.1), calls=%async_computation.1 | async-start | bytes 4325376 | tf_op jit(solution)/shard_map/all_to_all | solution.py:365
  10.5 1.6 copy-done.8
  12.1 1.0 token_columns.1
  13.1 1.3 copy-done
  14.5 43.3 %all-to-all-done.1.wm_ref.refs_5_.refs_6_ = bf16[16,528,128]{2,1,0:T(8,128)(2,1)S(1)} async-done(((bf16[16,528,128]{2,1,0:T(8,128)(2,1)}), bf16[16,528,128]{2,1,0:T(8,128)(2,1)S(1)}, u32[]{:S(2)}, u32[]{:S(2)}) %all-to-all-start.1) | async-done | bytes 2162720 | tf_op jit(solution)/shard_map/all_to_all | solution.py:365
  57.8 6.4 %all-to-all-start = ((bf16[16,128,512]{2,1,0:T(8,128)(2,1)}), bf16[16,128,512]{2,1,0:T(8,128)(2,1)}, u32[]{:S(2)}, u32[]{:S(2)}) async-start(bf16[16,128,512]{2,1,0:T(8,128)(2,1)} %copy-done), calls=%async_computation | async-start | bytes 4194304 | tf_op jit(solution)/shard_map/all_to_all | solution.py:378
  64.2 1.3 collective-permute-start
  65.5 1.6 copy-done.9
  67.0 1.2 down_columns.1
  68.3 1.0 copy-done.3
  69.3 41.0 %all-to-all-done.x_ref = bf16[16,128,512]{2,1,0:T(8,128)(2,1)} async-done(((bf16[16,128,512]{2,1,0:T(8,128)(2,1)}), bf16[16,128,512]{2,1,0:T(8,128)(2,1)}, u32[]{:S(2)}, u32[]{:S(2)}) %all-to-all-start) | async-done | bytes 2097184 | tf_op jit(solution)/shard_map/all_to_all | solution.py:378
  110.3 6.3 %all-to-all-start.2 = ((bf16[16,144,256]{2,1,0:T(8,128)(2,1)}), bf16[16,144,256]{2,1,0:T(8,128)(2,1)S(1)}, u32[]{:S(2)}, u32[]{:S(2)}) async-start(bf16[16,144,256]{2,1,0:T(8,128)(2,1)} %copy-done.3), calls=%async_computation.2 | async-start | bytes 2359296 | tf_op jit(solution)/shard_map/all_to_all | solution.py:391
  116.7 3.7 %gate_up_partial.3 = bf16[8,2,128,256]{3,2,1,0:T(8,128)(2,1)S(1)} custom-call(s32[3]{0:T(128)S(1)} %pad_add_fusion.ids, s32[16,2]{1,0:T(8,128)S(1)} %copy.26.active, bf16[16,128,512]{2,1,0:T(8,128)(2,1)} %all-to-all-done.x_ref, bf16[16,528,128]{2,1,0:T(8,128)(2,1)S(1)} %all-to-all-done.1.wm_ref.refs_5_.refs_6_, bf16[16,528,128]{2,1,0:T(8,128)(2,1)} %collective-permute-done.wo_ref), custom_call_target="tpu_custom_call" | custom-call | flops 536870912 | bytes 7471104 | tf_op jit(solution)/shard_map/gate_up_partial/pallas_call | solution.py:28
  120.9 3.7 %gate_up_partial.2.kept_ref = bf16[8,2,128,256]{3,2,1,0:T(8,128)(2,1)S(1)} custom-call(s32[3]{0:T(128)S(1)} %pad_add_fusion.ids, s32[16,2]{1,0:T(8,128)S(1)} %copy.26.active, bf16[16,128,512]{2,1,0:T(8,128)(2,1)} %all-to-all-done.x_ref, bf16[16,528,128]{2,1,0:T(8,128)(2,1)S(1)} %all-to-all-done.1.wm_ref.refs_5_.refs_6_, ...), custom_call_target="tpu_custom_call" | custom-call | flops 536870912 | bytes 7471104 | tf_op jit(solution)/shard_map/gate_up_partial/pallas_call | solution.py:28
  124.6 1.7 pair_sums.2
  127.1 1.2 collective-permute-start.2
  128.3 15.9 %all-to-all-done.2.refs_0_.refs_4_ = bf16[16,144,256]{2,1,0:T(8,128)(2,1)S(1)} async-done(((bf16[16,144,256]{2,1,0:T(8,128)(2,1)}), bf16[16,144,256]{2,1,0:T(8,128)(2,1)S(1)}, u32[]{:S(2)}, u32[]{:S(2)}) %all-to-all-start.2) | async-done | bytes 1179680 | tf_op jit(solution)/shard_map/all_to_all | solution.py:391
  144.2 1.3 collective-permute-start.18
  146.2 1.0 copy-done.15
  147.2 1.9 pair_sums.3
  149.2 3.6 %collective-permute-start.4 = (bf16[1,2,128,256]{3,2,1,0:T(8,128)(2,1)S(1)}, bf16[1,2,128,256]{3,2,1,0:T(8,128)(2,1)S(1)}, u32[]{:S(2)}, u32[]{:S(2)}) collective-permute-start(bf16[1,2,128,256]{3,2,1,0:T(8,128)(2,1)S(1)} %get-tuple-element.36), channel_id=1, source_target_pairs={{0,8},{2,10},{4,12},{6,14},{8,0},{10,2},{12,4},{14,6},{1,9},{3,11}... | collective-permute-start | bytes 393224 | tf_op jit(solution)/shard_map/ppermute | solution.py:402
  152.8 1.6 copy-done.1
  154.4 0.9 copy-done.4
  155.4 1.5 side_rows.1.refs_4_
  156.8 4.1 %collective-permute-done.4.refs_2_ = bf16[1,2,128,256]{3,2,1,0:T(8,128)(2,1)S(1)} collective-permute-done((bf16[1,2,128,256]{3,2,1,0:T(8,128)(2,1)S(1)}, bf16[1,2,128,256]{3,2,1,0:T(8,128)(2,1)S(1)}, u32[]{:S(2)}, u32[]{:S(2)}) %collective-permute-start.4) | collective-permute-done | bytes 131104 | tf_op jit(solution)/shard_map/ppermute | solution.py:402
  161.0 3.0 %collective-permute-done.5.refs_3_ = bf16[1,2,128,256]{3,2,1,0:T(8,128)(2,1)S(1)} collective-permute-done((bf16[1,2,128,256]{3,2,1,0:T(8,128)(2,1)S(1)}, bf16[1,2,128,256]{3,2,1,0:T(8,128)(2,1)S(1)}, u32[]{:S(2)}, u32[]{:S(2)}) %collective-permute-start.5) | collective-permute-done | bytes 131104 | tf_op jit(solution)/shard_map/ppermute | solution.py:402
  164.8 2.1 collective-permute-start.9
  166.9 1.2 collective-permute-start.7
  168.1 1.6 output_terms.1
  169.9 1.6 collective-permute-done.8
  171.5 1.0 collective-permute-done.7
  172.7 8.0 %all-to-all-start.3 = ((bf16[16,16,512]{2,1,0:T(8,128)(2,1)}), bf16[16,16,512]{2,1,0:T(8,128)(2,1)S(1)}, u32[]{:S(2)}, u32[]{:S(2)}) async-start(bf16[16,16,512]{2,1,0:T(8,128)(2,1)} %output_terms.1), calls=%async_computation.3 | async-start | bytes 524288 | tf_op jit(solution)/shard_map/all_to_all | solution.py:470
  181.0 1.0 collective-permute-start.12
  182.2 1.0 collective-permute-done.12.refs_3_
  183.2 3.4 %output_columns.1 = bf16[16,128,512]{2,1,0:T(8,128)(2,1)} custom-call(s32[3]{0:T(128)S(1)} %pad_add_fusion.ids, s32[16,2]{1,0:T(8,128)S(1)} %copy.26.active, bf16[4,288,128]{2,1,0:T(8,128)(2,1)S(1)} %pad_maximum_fusion.refs_0_, bf16[4,288,128]{2,1,0:T(8,128)(2,1)S(1)} %collective-permute-done.10.refs_1_, ...), custom_call_target="tpu_custom_call" | custom-call | tf_op jit(solution)/shard_map/output_columns/pallas_call | solution.py:486
  187.3 2.0 all-to-all-done.3.refs_5_
  190.0 5.0 %all-to-all-start.4 = ((bf16[16,128,512]{2,1,0:T(8,128)(2,1)}), bf16[16,128,512]{2,1,0:T(8,128)(2,1)S(1)}, u32[]{:S(2)}, u32[]{:S(2)}) async-start(bf16[16,128,512]{2,1,0:T(8,128)(2,1)} %output_columns.1), calls=%async_computation.4 | async-start | bytes 4194304 | tf_op jit(solution)/shard_map/all_to_all | solution.py:500
  195.0 1.0 copy-done.11
  196.0 0.9 copy-done.13
  197.0 1.3 gradients.1
  200.8 1.3 collective-permute-start.14
  202.1 3.4 %collective-permute-done.14 = f32[8,128]{1,0:T(8,128)S(1)} collective-permute-done((f32[8,128]{1,0:T(8,128)S(1)}, f32[8,128]{1,0:T(8,128)S(1)}, u32[]{:S(2)}, u32[]{:S(2)}) %collective-permute-start.14) | collective-permute-done | bytes 4128 | tf_op jit(solution)/shard_map/ppermute | solution.py:547
  205.6 1.3 collective-permute-start.17
  207.0 2.6 %collective-permute-start.16 = (f32[8,128]{1,0:T(8,128)S(1)}, f32[8,128]{1,0:T(8,128)S(1)}, u32[]{:S(2)}, u32[]{:S(2)}) collective-permute-start(f32[8,128]{1,0:T(8,128)S(1)} %add.11.refs_0_), channel_id=1, source_target_pairs={{0,4},{2,6},{4,0},{6,2},{8,12},{10,14},{12,8},{14,10},{1,5},{3,7},... | collective-permute-start | bytes 12296 | tf_op jit(solution)/shard_map/ppermute | solution.py:550
  209.6 31.6 %all-to-all-done.4.c_ref = bf16[16,128,512]{2,1,0:T(8,128)(2,1)S(1)} async-done(((bf16[16,128,512]{2,1,0:T(8,128)(2,1)}), bf16[16,128,512]{2,1,0:T(8,128)(2,1)S(1)}, u32[]{:S(2)}, u32[]{:S(2)}) %all-to-all-start.4) | async-done | bytes 2097184 | tf_op jit(solution)/shard_map/all_to_all | solution.py:500
  241.2 1.4 join_columns.1
  242.8 1.8 adamw.1
  (78 shorter events, 7.9 us)
Async XLA Ops:
  3.9 53.9 %all-to-all-start.1 = ((bf16[16,528,128]{2,1,0:T(8,128)(2,1)}), bf16[16,528,128]{2,1,0:T(8,128)(2,1)S(1)}, u32[]{:S(2)}, u32[]{:S(2)}) async-start(bf16[16,528,128]{2,1,0:T(8,128)(2,1)} %weight_rows.1), calls=%async_computation.1 | async-start | bytes 4325376 | tf_op jit(solution)/shard_map/all_to_all | solution.py:365
  10.5 1.6 copy-start.8
  13.1 1.3 copy-start
  14.5 51.0 %copy-start.6 = (f32[8,16,512]{2,1,0:T(8,128)S(1)}, f32[8,16,512]{2,1,0:T(8,128)}, u32[]{:S(2)}) copy-start(f32[8,16,512]{2,1,0:T(8,128)} %refs_8_.1) | copy-start | bytes 786436
  57.8 52.5 %all-to-all-start = ((bf16[16,128,512]{2,1,0:T(8,128)(2,1)}), bf16[16,128,512]{2,1,0:T(8,128)(2,1)}, u32[]{:S(2)}, u32[]{:S(2)}) async-start(bf16[16,128,512]{2,1,0:T(8,128)(2,1)} %copy-done), calls=%async_computation | async-start | bytes 4194304 | tf_op jit(solution)/shard_map/all_to_all | solution.py:378
  64.2 52.5 %collective-permute-start = (bf16[16,528,128]{2,1,0:T(8,128)(2,1)S(1)}, bf16[16,528,128]{2,1,0:T(8,128)(2,1)}, u32[]{:S(2)}, u32[]{:S(2)}) collective-permute-start(bf16[16,528,128]{2,1,0:T(8,128)(2,1)S(1)} %all-to-all-done.1.wm_ref.refs_5_.refs_6_), channel_id=1, source_target_pairs={{0,16},{16,0},{1,17},{17,1},{2,18},{18,2},{3,19},{19,3},{4,20},{20... | collective-permute-start | bytes 6488072 | tf_op jit(solution)/shard_map/ppermute | solution.py:366
  65.5 1.6 copy-start.9
  67.0 49.6 %copy-start.28 = (s32[16,2]{0,1:T(2,128)S(1)}, s32[16,2]{0,1:T(2,128)}, u32[]{:S(2)}) copy-start(s32[16,2]{0,1:T(2,128)} %param.27) | copy-start | bytes 388
  68.3 1.0 copy-start.3
  110.3 33.9 %all-to-all-start.2 = ((bf16[16,144,256]{2,1,0:T(8,128)(2,1)}), bf16[16,144,256]{2,1,0:T(8,128)(2,1)S(1)}, u32[]{:S(2)}, u32[]{:S(2)}) async-start(bf16[16,144,256]{2,1,0:T(8,128)(2,1)} %copy-done.3), calls=%async_computation.2 | async-start | bytes 2359296 | tf_op jit(solution)/shard_map/all_to_all | solution.py:391
  120.4 4.2 %collective-permute-start.1 = (bf16[8,2,128,256]{3,2,1,0:T(8,128)(2,1)S(1)}, bf16[8,2,128,256]{3,2,1,0:T(8,128)(2,1)S(1)}, u32[]{:S(2)}, u32[]{:S(2)}) collective-permute-start(bf16[8,2,128,256]{3,2,1,0:T(8,128)(2,1)S(1)} %gate_up_partial.3), channel_id=1, source_target_pairs={{0,1},{1,0},{2,3},{3,2},{4,5},{5,4},{6,7},{7,6},{8,9},{9,8},{10,11... | collective-permute-start | bytes 3145736 | tf_op jit(solution)/shard_map/ppermute | solution.py:396
  124.6 28.2 %copy-start.25 = (s32[16]{0:T(128)S(1)}, s32[16]{0:T(128)}, u32[]{:S(2)}) copy-start(s32[16]{0:T(128)} %counts.5) | copy-start | bytes 196
  124.6 28.2 %copy-start.26 = (s32[8]{0:T(128)S(1)}, s32[8]{0:T(128)}, u32[]{:S(2)}) copy-start(s32[8]{0:T(128)} %seeds.3) | copy-start | bytes 100
  127.1 19.1 %collective-permute-start.2 = (bf16[4,2,128,256]{3,2,1,0:T(8,128)(2,1)}, bf16[4,2,128,256]{3,2,1,0:T(8,128)(2,1)}, u32[]{:S(2)}, u32[]{:S(2)}) collective-permute-start(bf16[4,2,128,256]{3,2,1,0:T(8,128)(2,1)} %get-tuple-element.33), channel_id=1, source_target_pairs={{0,2},{2,0},{4,6},{6,4},{8,10},{10,8},{12,14},{14,12},{1,3},{3,1},... | collective-permute-start | bytes 1572872 | tf_op jit(solution)/shard_map/ppermute | solution.py:399
  144.2 38.0 %collective-permute-start.18 = (bf16[16,144,256]{2,1,0:T(8,128)(2,1)S(1)}, bf16[16,144,256]{2,1,0:T(8,128)(2,1)}, u32[]{:S(2)}, u32[]{:S(2)}) collective-permute-start(bf16[16,144,256]{2,1,0:T(8,128)(2,1)S(1)} %all-to-all-done.2.refs_0_.refs_4_), channel_id=1, source_target_pairs={{0,16},{16,0},{1,17},{17,1},{2,18},{18,2},{3,19},{19,3},{4,20},{20... | collective-permute-start | bytes 3538952 | tf_op jit(solution)/shard_map/ppermute | solution.py:405
  145.5 7.3 %collective-permute-start.6 = (bf16[16,16,256]{2,1,0:T(8,128)(2,1)S(1)}, bf16[16,16,256]{2,1,0:T(8,128)(2,1)S(1)}, u32[]{:S(2)}, u32[]{:S(2)}) collective-permute-start(bf16[16,16,256]{2,1,0:T(8,128)(2,1)S(1)} %slice.3), channel_id=1, source_target_pairs={{0,1},{1,0},{2,3},{3,2},{4,5},{5,4},{6,7},{7,6},{8,9},{9,8},{10,11... | collective-permute-start | bytes 393224 | tf_op jit(solution)/shard_map/ppermute | solution.py:406
  146.2 1.0 copy-start.15
  149.1 7.7 %collective-permute-start.3 = (bf16[1,2,128,256]{3,2,1,0:T(8,128)(2,1)S(1)}, bf16[1,2,128,256]{3,2,1,0:T(8,128)(2,1)S(1)}, u32[]{:S(2)}, u32[]{:S(2)}) collective-permute-start(bf16[1,2,128,256]{3,2,1,0:T(8,128)(2,1)S(1)} %get-tuple-element.35), channel_id=1, source_target_pairs={{0,4},{2,6},{4,0},{6,2},{8,12},{10,14},{12,8},{14,10},{1,5},{3,7},... | collective-permute-start | bytes 393224 | tf_op jit(solution)/shard_map/ppermute | solution.py:402
  149.2 11.8 %collective-permute-start.4 = (bf16[1,2,128,256]{3,2,1,0:T(8,128)(2,1)S(1)}, bf16[1,2,128,256]{3,2,1,0:T(8,128)(2,1)S(1)}, u32[]{:S(2)}, u32[]{:S(2)}) collective-permute-start(bf16[1,2,128,256]{3,2,1,0:T(8,128)(2,1)S(1)} %get-tuple-element.36), channel_id=1, source_target_pairs={{0,8},{2,10},{4,12},{6,14},{8,0},{10,2},{12,4},{14,6},{1,9},{3,11}... | collective-permute-start | bytes 393224 | tf_op jit(solution)/shard_map/ppermute | solution.py:402
  152.8 11.2 %collective-permute-start.5 = (bf16[1,2,128,256]{3,2,1,0:T(8,128)(2,1)S(1)}, bf16[1,2,128,256]{3,2,1,0:T(8,128)(2,1)S(1)}, u32[]{:S(2)}, u32[]{:S(2)}) collective-permute-start(bf16[1,2,128,256]{3,2,1,0:T(8,128)(2,1)S(1)} %get-tuple-element.37), channel_id=1, source_target_pairs={{0,12},{2,14},{4,8},{6,10},{8,4},{10,6},{12,0},{14,2},{1,13},{3,15... | collective-permute-start | bytes 393224 | tf_op jit(solution)/shard_map/ppermute | solution.py:402
  152.8 1.6 copy-start.1
  154.4 0.9 copy-start.4
  155.4 12.8 %copy-start.2 = (bf16[128,8192]{1,0:T(8,128)(2,1)S(1)}, bf16[128,8192]{1,0:T(8,128)(2,1)}, u32[]{:S(2)}) copy-start(bf16[128,8192]{1,0:T(8,128)(2,1)} %dy_ref.1) | copy-start | bytes 6291460
  164.0 19.2 %copy-start.7 = (f32[8,16,512]{2,1,0:T(8,128)S(1)}, f32[8,16,512]{2,1,0:T(8,128)}, u32[]{:S(2)}) copy-start(f32[8,16,512]{2,1,0:T(8,128)} %refs_8_.1) | copy-start | bytes 786436
  164.8 5.1 %collective-permute-start.9 = (bf16[288,128]{1,0:T(8,128)(2,1)S(1)}, bf16[288,128]{1,0:T(8,128)(2,1)S(1)}, u32[]{:S(2)}, u32[]{:S(2)}) collective-permute-start(bf16[288,128]{1,0:T(8,128)(2,1)S(1)} %hidden_values.1.z_ref), channel_id=1, source_target_pairs={{0,12},{2,14},{4,8},{6,10},{8,4},{10,6},{12,0},{14,2},{1,13},{3,15... | collective-permute-start | bytes 221192 | tf_op jit(solution)/shard_map/ppermute | solution.py:467
  166.9 4.6 %collective-permute-start.8 = (bf16[288,128]{1,0:T(8,128)(2,1)S(1)}, bf16[288,128]{1,0:T(8,128)(2,1)S(1)}, u32[]{:S(2)}, u32[]{:S(2)}) collective-permute-start(bf16[288,128]{1,0:T(8,128)(2,1)S(1)} %hidden_values.1.z_ref), channel_id=1, source_target_pairs={{0,8},{2,10},{4,12},{6,14},{8,0},{10,2},{12,4},{14,6},{1,9},{3,11}... | collective-permute-start | bytes 221192 | tf_op jit(solution)/shard_map/ppermute | solution.py:467
  166.9 5.6 %collective-permute-start.7 = (bf16[288,128]{1,0:T(8,128)(2,1)S(1)}, bf16[288,128]{1,0:T(8,128)(2,1)S(1)}, u32[]{:S(2)}, u32[]{:S(2)}) collective-permute-start(bf16[288,128]{1,0:T(8,128)(2,1)S(1)} %hidden_values.1.z_ref), channel_id=1, source_target_pairs={{0,4},{2,6},{4,0},{6,2},{8,12},{10,14},{12,8},{14,10},{1,5},{3,7},... | collective-permute-start | bytes 221192 | tf_op jit(solution)/shard_map/ppermute | solution.py:467
  172.5 8.5 %collective-permute-start.10 = (bf16[4,288,128]{2,1,0:T(8,128)(2,1)S(1)}, bf16[4,288,128]{2,1,0:T(8,128)(2,1)S(1)}, u32[]{:S(2)}, u32[]{:S(2)}) collective-permute-start(bf16[4,288,128]{2,1,0:T(8,128)(2,1)S(1)} %pad_maximum_fusion.refs_0_), channel_id=1, source_target_pairs={{0,2},{2,0},{4,6},{6,4},{8,10},{10,8},{12,14},{14,12},{1,3},{3,1},... | collective-permute-start | bytes 884744 | tf_op jit(solution)/shard_map/ppermute | solution.py:475
  172.7 16.6 %all-to-all-start.3 = ((bf16[16,16,512]{2,1,0:T(8,128)(2,1)}), bf16[16,16,512]{2,1,0:T(8,128)(2,1)S(1)}, u32[]{:S(2)}, u32[]{:S(2)}) async-start(bf16[16,16,512]{2,1,0:T(8,128)(2,1)} %output_terms.1), calls=%async_computation.3 | async-start | bytes 524288 | tf_op jit(solution)/shard_map/all_to_all | solution.py:470
  180.6 1.6 collective-permute-start.11
  181.0 2.2 collective-permute-start.12
  187.3 7.7 %copy-start.5 = (s32[4,128,128]{2,1,0:T(8,128)S(1)}, s32[4,128,128]{2,1,0:T(8,128)}, u32[]{:S(2)}) copy-start(s32[4,128,128]{2,1,0:T(8,128)} %refs_4_.4) | copy-start | bytes 786436
  187.3 7.7 %copy-start.27 = (s32[16]{0:T(128)S(1)}, s32[16]{0:T(128)}, u32[]{:S(2)}) copy-start(s32[16]{0:T(128)} %constant.16.clone.order) | copy-start | bytes 196
  190.0 51.2 %all-to-all-start.4 = ((bf16[16,128,512]{2,1,0:T(8,128)(2,1)}), bf16[16,128,512]{2,1,0:T(8,128)(2,1)S(1)}, u32[]{:S(2)}, u32[]{:S(2)}) async-start(bf16[16,128,512]{2,1,0:T(8,128)(2,1)} %output_columns.1), calls=%async_computation.4 | async-start | bytes 4194304 | tf_op jit(solution)/shard_map/all_to_all | solution.py:500
  195.0 1.0 copy-start.11
  196.0 0.9 copy-start.13
  199.6 1.2 collective-permute-start.13
  200.8 4.7 %collective-permute-start.14 = (f32[8,128]{1,0:T(8,128)S(1)}, f32[8,128]{1,0:T(8,128)S(1)}, u32[]{:S(2)}, u32[]{:S(2)}) collective-permute-start(f32[8,128]{1,0:T(8,128)S(1)} %add.10), channel_id=1, source_target_pairs={{0,2},{2,0},{4,6},{6,4},{8,10},{10,8},{12,14},{14,12},{1,3},{3,1},... | collective-permute-start | bytes 12296 | tf_op jit(solution)/shard_map/ppermute | solution.py:547
  205.6 37.1 %copy-start.16 = (f32[8,16,128]{2,1,0:T(8,128)S(1)}, f32[8,16,128]{2,1,0:T(8,128)}, u32[]{:S(2)}) copy-start(f32[8,16,128]{2,1,0:T(8,128)} %refs_4_.5) | copy-start | bytes 196612
  205.6 37.1 %copy-start.17 = (f32[8,16,512]{2,1,0:T(8,128)S(1)}, f32[8,16,512]{2,1,0:T(8,128)}, u32[]{:S(2)}) copy-start(f32[8,16,512]{2,1,0:T(8,128)} %refs_9_.1) | copy-start | bytes 786436
  205.6 37.1 %copy-start.18 = (f32[8,16,512]{2,1,0:T(8,128)S(1)}, f32[8,16,512]{2,1,0:T(8,128)}, u32[]{:S(2)}) copy-start(f32[8,16,512]{2,1,0:T(8,128)} %refs_10_.1) | copy-start | bytes 786436
  205.6 37.1 %copy-start.20 = (f32[8,16,512]{2,1,0:T(8,128)S(1)}, f32[8,16,512]{2,1,0:T(8,128)}, u32[]{:S(2)}) copy-start(f32[8,16,512]{2,1,0:T(8,128)} %copy-done.19) | copy-start | bytes 786436
  205.6 37.1 %copy-start.21 = (f32[8,16,128]{2,1,0:T(8,128)S(1)}, f32[8,16,128]{2,1,0:T(8,128)}, u32[]{:S(2)}) copy-start(f32[8,16,128]{2,1,0:T(8,128)} %refs_5_.1) | copy-start | bytes 196612
  205.6 37.1 %copy-start.22 = (f32[8,16,128]{2,1,0:T(8,128)S(1)}, f32[8,16,128]{2,1,0:T(8,128)}, u32[]{:S(2)}) copy-start(f32[8,16,128]{2,1,0:T(8,128)} %refs_6_.3) | copy-start | bytes 196612
  205.6 37.1 %copy-start.24 = (f32[8,16,128]{2,1,0:T(8,128)S(1)}, f32[8,16,128]{2,1,0:T(8,128)}, u32[]{:S(2)}) copy-start(f32[8,16,128]{2,1,0:T(8,128)} %copy-done.23) | copy-start | bytes 196612
  205.6 37.0 %collective-permute-start.17 = (f32[8,128]{1,0:T(8,128)S(1)}, f32[8,128]{1,0:T(8,128)S(1)}, u32[]{:S(2)}, u32[]{:S(2)}) collective-permute-start(f32[8,128]{1,0:T(8,128)S(1)} %add.11.refs_0_), channel_id=1, source_target_pairs={{0,12},{2,14},{4,8},{6,10},{8,4},{10,6},{12,0},{14,2},{1,13},{3,15... | collective-permute-start | bytes 12296 | tf_op jit(solution)/shard_map/ppermute | solution.py:550
  207.0 35.7 %collective-permute-start.16 = (f32[8,128]{1,0:T(8,128)S(1)}, f32[8,128]{1,0:T(8,128)S(1)}, u32[]{:S(2)}, u32[]{:S(2)}) collective-permute-start(f32[8,128]{1,0:T(8,128)S(1)} %add.11.refs_0_), channel_id=1, source_target_pairs={{0,4},{2,6},{4,0},{6,2},{8,12},{10,14},{12,8},{14,10},{1,5},{3,7},... | collective-permute-start | bytes 12296 | tf_op jit(solution)/shard_map/ppermute | solution.py:550
  209.6 33.1 %collective-permute-start.15 = (f32[8,128]{1,0:T(8,128)S(1)}, f32[8,128]{1,0:T(8,128)S(1)}, u32[]{:S(2)}, u32[]{:S(2)}) collective-permute-start(f32[8,128]{1,0:T(8,128)S(1)} %add.11.refs_0_), channel_id=1, source_target_pairs={{0,8},{2,10},{4,12},{6,14},{8,0},{10,2},{12,4},{14,6},{1,9},{3,11}... | collective-permute-start | bytes 12296 | tf_op jit(solution)/shard_map/ppermute | solution.py:550
  (5 other events, 3.6 us)
